TPU v7x, 256 devices: a whole 4x4x8 slice. The times are simulated.
256 devices in a mesh: blk: 64 (over y_hi, x, z), rows: 4 (over y_lo, core).
Axes of the slice: x: 4, y: 4 (y_hi: 2, y_lo: 2; y = y_hi * 2 + y_lo), z: 8, core: 2. Of those that a mesh axis runs over, the one named last changes fastest.
Arguments:
- factor_cols: float32 [16384, 8192], P('rows', 'blk'), may hold values from -1 to 1
- basis_cols: float32 [16384, 8192], P('rows', 'blk'), may hold values from -0.046875 to 0.046875
- samples: float32 [128, 16384], P(None, 'rows'), may hold values from -8 to 8
- pairing: int32 [3, 8, 128], replicated, may hold values from 0 to 127, each once within a row
Outputs:
- eigen_sums: float32 [8192], P('blk')
- corrected: float32 [8192], P('blk')
Inputs may be any that keep to these rules, and one draw needn't show every extreme that they name: Each pairing[r, s] lists every number 0 to 127 exactly once.
All inputs are finite; a program needn't handle non-finite values.
Results may differ from a plain program's by a relative error of at most 0.0003.
Values sent between devices are 32-bit elements; how exact they have to be, the bound alone decides.
No kernel may reach another device: no remote copies, remote signals or barrier semaphores. Data moves between devices by JAX's collectives and lax.ppermute only.
A program may use at most 128 MiB of HBM per device.

v0:
```python
import jax
import jax.numpy as jnp
from jax import lax
from jax.sharding import PartitionSpec as P

highest = lax.Precision.HIGHEST


def from_behind(value, axis, steps):
    count = lax.axis_size(axis)
    leading, last = (max(0, -steps), min(count, count - steps))
    return lax.ppermute(value, axis, [(source, source + steps) for source in range(leading, last)])


def small_solve(gram_pair, order_rows):
    breadth = gram_pair.shape[0]
    settled = gram_pair
    turned = jnp.eye(breadth, dtype=jnp.float32)
    for step_index in range(order_rows.shape[0]):
        order_row = order_rows[step_index]
        first_index = order_row[0::2]
        second_index = order_row[1::2]
        diag_first = settled[first_index, first_index]
        diag_second = settled[second_index, second_index]
        crossing = settled[first_index, second_index]
        angles = 0.5 * jnp.arctan2(2.0 * crossing, diag_first - diag_second)
        cosine = jnp.cos(angles)
        sines = jnp.sin(angles)
        col_first = settled[:, first_index]
        col_second = settled[:, second_index]
        settled = settled.at[:, first_index].set(
            cosine[None, :] * col_first + sines[None, :] * col_second
        )
        settled = settled.at[:, second_index].set(
            cosine[None, :] * col_second - sines[None, :] * col_first
        )
        row_first = settled[first_index, :]
        row_second = settled[second_index, :]
        settled = settled.at[first_index, :].set(
            cosine[:, None] * row_first + sines[:, None] * row_second
        )
        settled = settled.at[second_index, :].set(
            cosine[:, None] * row_second - sines[:, None] * row_first
        )
        turn_first = turned[:, first_index]
        turn_second = turned[:, second_index]
        turned = turned.at[:, first_index].set(
            cosine[None, :] * turn_first + sines[None, :] * turn_second
        )
        turned = turned.at[:, second_index].set(
            cosine[None, :] * turn_second - sines[None, :] * turn_first
        )
    return turned


def doubled(piece):
    zero_block = jnp.zeros_like(piece)
    return jnp.block([[piece, zero_block], [zero_block, piece]])


def cross_product(left, right):
    return lax.dot_general(
        left, right, (((0,), (0,)), ((), ())), precision=highest, preferred_element_type=jnp.float32
    )


def folded(whole, half_width):
    return whole[:half_width, :half_width] + whole[half_width:, half_width:]


def rotate_packed(source_pair, columns, half_width):
    upper_part = jnp.dot(
        source_pair[0],
        doubled(columns[:half_width]),
        precision=highest,
        preferred_element_type=jnp.float32,
    )
    lower_part = jnp.dot(
        source_pair[1],
        doubled(columns[half_width:]),
        precision=highest,
        preferred_element_type=jnp.float32,
    )
    return upper_part + lower_part


def unpack(packed_tops, packed_bottoms, half_width):
    row_count = packed_tops.shape[0] * 2
    return jnp.concatenate(
        [packed_tops.reshape(row_count, half_width), packed_bottoms.reshape(row_count, half_width)],
        1,
    )


def on_device(factor_cols, basis_cols, samples, pairing):
    pair_width = factor_cols.shape[1]
    half_width = pair_width // 2
    local_rows = factor_cols.shape[0]
    packed_factor = local_rows // 2
    position = lax.axis_index("blk")
    final_index = lax.axis_size("blk") - 1
    at_first = position == 0
    at_last = position == final_index
    carried = jnp.concatenate([factor_cols, basis_cols], 0)
    packed_rows = carried.shape[0] // 2
    tops = carried[:, :half_width].reshape(packed_rows, pair_width)
    bottoms = carried[:, half_width:].reshape(packed_rows, pair_width)
    for round_index in range(pairing.shape[0]):
        stacked = jnp.stack([tops, bottoms], 0)
        factor_tops = tops[:packed_factor]
        factor_bottoms = bottoms[:packed_factor]
        gram_tt = folded(cross_product(factor_tops, factor_tops), half_width)
        gram_tb = folded(cross_product(factor_tops, factor_bottoms), half_width)
        gram_bb = folded(cross_product(factor_bottoms, factor_bottoms), half_width)
        gram_local = jnp.block([[gram_tt, gram_tb], [gram_tb.T, gram_bb]])
        gram_total = lax.psum(gram_local, "rows")
        turned = small_solve(gram_total, pairing[round_index])
        new_top = rotate_packed(stacked, turned[:, :half_width], half_width)
        new_bottom = rotate_packed(stacked, turned[:, half_width:], half_width)
        rising = jnp.where(at_first, new_bottom, new_top)
        arrived_below = from_behind(rising, "blk", 1)
        arrived_above = from_behind(new_bottom, "blk", -1)
        tops = jnp.where(at_first, new_top, arrived_below)
        bottoms = jnp.where(at_last, new_top, arrived_above)
    factor_tops = tops[:packed_factor]
    factor_bottoms = bottoms[:packed_factor]
    top_squares = jnp.sum(factor_tops * factor_tops, axis=0)
    bottom_squares = jnp.sum(factor_bottoms * factor_bottoms, axis=0)
    column_norms = jnp.concatenate(
        [
            top_squares[:half_width] + top_squares[half_width:],
            bottom_squares[:half_width] + bottom_squares[half_width:],
        ],
        0,
    )
    extra_columns = unpack(tops[packed_factor:], bottoms[packed_factor:], half_width)
    partial_projection = jnp.dot(
        samples, extra_columns, precision=highest, preferred_element_type=jnp.float32
    )
    eigen_sums, projected = lax.psum((column_norms, partial_projection), "rows")
    corrected = jnp.mean(projected * projected, axis=0)
    return (eigen_sums, corrected)


def solution(mesh):
    in_specs = (P("rows", "blk"), P("rows", "blk"), P(None, "rows"), P())
    out_specs = (P("blk"), P("blk"))
    return jax.shard_map(
        on_device, mesh=mesh, in_specs=in_specs, out_specs=out_specs, check_vma=False
    )
```

profile of v0, /device:TPU:33, one launch (start us, length us, event | category | flops | bytes accessed | tf_op | source)
XLA Modules:
  0.0 694.1 jit_solution(2658975922899741447)
XLA Ops:
  7.2 5.0 fusion.946
  14.0 1.8 fusion.952
  15.8 2.6 slice.437
  18.4 3.4 fusion.950
  25.0 3.1 constant_dynamic-update-slice_fusion.1
  31.7 3.0 constant_dynamic-update-slice_fusion
  34.7 7.9 %fusion.943 = (f32[8192,64]{1,0:T(8,128)}, f32[8192,64]{1,0:T(8,128)}) fusion(f32[8192,128]{1,0:T(8,128)} %constant_dynamic-update-slice_fusion), kind=kLoop, calls=%fused_computation.1544 | loop fusion | bytes 8388608 | tf_op jit(solution)/shard_map/slice | solution.py:107
  42.6 4.6 squeeze_stack_reshape.2
  50.9 4.7 reshape.874
  55.8 12.7 %all-reduce.29.cloned.1.call-done = f32[128,128]{1,0:T(8,128)} async-done(((f32[128,128]{1,0:T(8,128)}), f32[128,128]{1,0:T(8,128)}) %all-reduce.29.cloned.1.call-update) | async-done | bytes 65552 | tf_op jit(solution)/shard_map/psum | solution.py:116
  156.4 3.6 fusion.61
  160.1 1.9 fusion.54
  162.1 2.1 convolution_add_fusion.5
  164.1 3.5 broadcast_select_fusion.8
  167.6 3.2 collective-permute-start
  170.8 3.6 collective-permute-start.1
  176.8 40.1 %collective-permute-done = f32[4096,128]{1,0:T(8,128)} collective-permute-done((f32[4096,128]{1,0:T(8,128)}, f32[4096,128]{1,0:T(8,128)}, u32[]{:S(2)}, u32[]{:S(2)}) %collective-permute-start) | collective-permute-done | bytes 2097184 | tf_op jit(solution)/shard_map/ppermute | solution.py:12
  216.9 2.9 collective-permute-done.1
  219.8 3.2 broadcast_select_fusion.7
  223.0 1.9 fusion.16
  224.9 1.9 fusion.18
  226.9 1.9 fusion.21
  229.9 44.0 %all-reduce.31.cloned.1.call-done = f32[128,128]{1,0:T(8,128)} async-done(((f32[128,128]{1,0:T(8,128)}), f32[128,128]{1,0:T(8,128)}) %all-reduce.31.cloned.1.call-update) | async-done | bytes 65552 | tf_op jit(solution)/shard_map/psum | solution.py:116
  361.8 3.6 fusion.44
  365.5 1.9 fusion.37
  367.4 2.0 convolution_add_fusion.3
  369.5 3.5 broadcast_select_fusion.6
  373.0 3.2 collective-permute-start.2
  376.2 3.6 collective-permute-start.3
  381.8 40.4 %collective-permute-done.2 = f32[4096,128]{1,0:T(8,128)} collective-permute-done((f32[4096,128]{1,0:T(8,128)}, f32[4096,128]{1,0:T(8,128)}, u32[]{:S(2)}, u32[]{:S(2)}) %collective-permute-start.2) | collective-permute-done | bytes 2097184 | tf_op jit(solution)/shard_map/ppermute | solution.py:12
  422.3 2.9 collective-permute-done.3
  425.1 3.2 broadcast_select_fusion.5
  428.4 1.9 fusion.9
  430.2 1.9 fusion.11
  432.3 1.9 fusion.14
  435.2 44.0 %all-reduce.33.cloned.1.call-done = f32[128,128]{1,0:T(8,128)} async-done(((f32[128,128]{1,0:T(8,128)}), f32[128,128]{1,0:T(8,128)}) %all-reduce.33.cloned.1.call-update) | async-done | bytes 65552 | tf_op jit(solution)/shard_map/psum | solution.py:116
  567.2 3.6 fusion.30
  570.9 1.9 fusion.23
  572.8 2.0 convolution_add_fusion.1
  574.8 2.0 broadcast_select_fusion.4
  576.9 3.2 collective-permute-start.4
  580.0 2.4 collective-permute-start.5
  582.5 43.4 %collective-permute-done.4 = f32[4096,128]{1,0:T(8,128)S(1)} collective-permute-done((f32[4096,128]{1,0:T(8,128)S(1)}, f32[4096,128]{1,0:T(8,128)S(1)}, u32[]{:S(2)}, u32[]{:S(2)}) %collective-permute-start.4) | collective-permute-done | bytes 2097184 | tf_op jit(solution)/shard_map/ppermute | solution.py:12
  625.8 2.9 collective-permute-done.5
  632.2 2.7 reshape.875
  634.9 6.9 fusion.4
  641.9 6.8 psum.38
  648.7 37.2 %all-reduce.35.cloned.1.call-done = f32[128,128]{0,1:T(8,128)} async-done(((f32[128,128]{0,1:T(8,128)}), f32[128,128]{0,1:T(8,128)}) %all-reduce.35.cloned.1.call-update) | async-done | bytes 65552 | tf_op jit(solution)/shard_map/psum | solution.py:140
  (602 shorter events, 286.2 us)
Async XLA Ops:
  7.2 627.7 %copy-start = (f32[128,4096]{1,0:T(8,128)S(1)}, f32[128,4096]{1,0:T(8,128)}, u32[]{:S(2)}) copy-start(f32[128,4096]{1,0:T(8,128)} %param.6) | copy-start | bytes 6291460
  7.2 61.3 %all-reduce.29.cloned.1.call-start = ((), (), s32[]{:S(2)}) async-start(), calls=%async_computation | async-start | bytes 131072 | tf_op jit(solution)/shard_map/psum | solution.py:116
  18.4 3.4 copy-start.16
  24.8 3.4 copy-start.17
  24.8 249.0 %all-reduce.31.cloned.1.call-start = ((), (), s32[]{:S(2)}) async-start(), calls=%async_computation.1 | async-start | bytes 131072 | tf_op jit(solution)/shard_map/psum | solution.py:116
  68.5 3.9 copy-start.1
  156.4 3.7 copy-start.12
  160.1 2.0 copy-start.13
  164.1 3.5 copy-start.14
  167.6 49.3 %collective-permute-start = (f32[4096,128]{1,0:T(8,128)}, f32[4096,128]{1,0:T(8,128)}, u32[]{:S(2)}, u32[]{:S(2)}) collective-permute-start(f32[4096,128]{1,0:T(8,128)} %get-tuple-element.220), channel_id=1, source_target_pairs={{0,4},{4,8},{8,12},{12,16},{16,20},{20,24},{24,28},{28,32},{32,36}... | collective-permute-start | bytes 6291464 | tf_op jit(solution)/shard_map/ppermute | solution.py:12
  170.8 49.0 %collective-permute-start.1 = (f32[4096,128]{1,0:T(8,128)}, f32[4096,128]{1,0:T(8,128)}, u32[]{:S(2)}, u32[]{:S(2)}) collective-permute-start(f32[4096,128]{1,0:T(8,128)} %get-tuple-element.221), channel_id=1, source_target_pairs={{4,0},{8,4},{12,8},{16,12},{20,16},{24,20},{28,24},{32,28},{36,32}... | collective-permute-start | bytes 6291464 | tf_op jit(solution)/shard_map/ppermute | solution.py:12
  223.0 5.8 copy-start.4
  223.0 5.8 copy-start.8
  229.8 249.4 %all-reduce.33.cloned.1.call-start = ((), (), s32[]{:S(2)}) async-start(), calls=%async_computation.2 | async-start | bytes 131072 | tf_op jit(solution)/shard_map/psum | solution.py:116
  273.8 3.9 copy-start.2
  361.8 3.7 copy-start.9
  365.5 2.0 copy-start.5
  369.5 3.5 copy-start.15
  373.0 49.3 %collective-permute-start.2 = (f32[4096,128]{1,0:T(8,128)}, f32[4096,128]{1,0:T(8,128)}, u32[]{:S(2)}, u32[]{:S(2)}) collective-permute-start(f32[4096,128]{1,0:T(8,128)} %get-tuple-element.222), channel_id=1, source_target_pairs={{0,4},{4,8},{8,12},{12,16},{16,20},{20,24},{24,28},{28,32},{32,36}... | collective-permute-start | bytes 6291464 | tf_op jit(solution)/shard_map/ppermute | solution.py:12
  376.2 49.0 %collective-permute-start.3 = (f32[4096,128]{1,0:T(8,128)}, f32[4096,128]{1,0:T(8,128)}, u32[]{:S(2)}, u32[]{:S(2)}) collective-permute-start(f32[4096,128]{1,0:T(8,128)} %get-tuple-element.223), channel_id=1, source_target_pairs={{4,0},{8,4},{12,8},{16,12},{20,16},{24,20},{28,24},{32,28},{36,32}... | collective-permute-start | bytes 6291464 | tf_op jit(solution)/shard_map/ppermute | solution.py:12
  428.3 5.8 copy-start.6
  428.3 5.8 copy-start.10
  435.2 250.7 %all-reduce.35.cloned.1.call-start = ((), (), s32[]{:S(2)}) async-start(), calls=%async_computation.3 | async-start | bytes 131072 | tf_op jit(solution)/shard_map/psum | solution.py:140
  479.2 3.9 copy-start.3
  567.2 3.7 copy-start.11
  570.9 2.0 copy-start.7
  576.9 49.0 %collective-permute-start.4 = (f32[4096,128]{1,0:T(8,128)S(1)}, f32[4096,128]{1,0:T(8,128)S(1)}, u32[]{:S(2)}, u32[]{:S(2)}) collective-permute-start(f32[4096,128]{1,0:T(8,128)S(1)} %get-tuple-element.224), channel_id=1, source_target_pairs={{0,4},{4,8},{8,12},{12,16},{16,20},{20,24},{24,28},{28,32},{32,36}... | collective-permute-start | bytes 6291464 | tf_op jit(solution)/shard_map/ppermute | solution.py:12
  580.0 48.6 %collective-permute-start.5 = (f32[4096,128]{1,0:T(8,128)S(1)}, f32[4096,128]{1,0:T(8,128)S(1)}, u32[]{:S(2)}, u32[]{:S(2)}) collective-permute-start(f32[4096,128]{1,0:T(8,128)S(1)} %get-tuple-element.225), channel_id=1, source_target_pairs={{4,0},{8,4},{12,8},{16,12},{20,16},{24,20},{28,24},{32,28},{36,32}... | collective-permute-start | bytes 6291464 | tf_op jit(solution)/shard_map/ppermute | solution.py:12
Sparse Core Ops, SparseCore 0:
  24.9 43.5 all-reduce.28
  229.9 43.8 all-reduce.30
  435.3 43.8 all-reduce.32
  642.0 43.8 all-reduce.34
where the time goes:
time: 702 us; the launch traced here: 694 us
  waiting for transfers between devices  270 us (38%)
  local copies, waits for them, and re-layouts  191 us (27%)
  other arithmetic  133 us (19%)
  matrix products  57.1 us (8%)
  starting transfers between devices  19.4 us (3%)
  between operations  16.5 us (2%)
    ppermute x6, waiting for transfers between devices, from_behind(): lax.ppermute(value, axis, [(source, source + steps) for source in range(l...  132 us
    psum x3, waiting for transfers between devices, on_device(): gram_total = lax.psum(gram_local, 'rows')  101 us
    psum x1, waiting for transfers between devices, on_device(): eigen_sums, projected = lax.psum((column_norms, partial_projection), 'rows')  37.2 us
    gather x24, local copies, waits for them, and re-layouts, small_solve(): diag_first = settled[first_index, first_index]  21.7 us
    scatter x24, other arithmetic, small_solve(): turned.at[:, first_index]  21.5 us
    scatter x24, other arithmetic, small_solve(): turned.at[:, second_index]  21.3 us
    scatter x21, other arithmetic, small_solve(): settled.at[second_index, :]  19.7 us
    ppermute x6, starting transfers between devices, from_behind(): lax.ppermute(value, axis, [(source, source + steps) for source in range(l...  19 us
  transfers between devices with their start and end apart: 10, of which 10 were waited for; matrix products, arithmetic and copies ran while one was open for 5% of the time, Pallas kernels for 0%

commit v1 on v0

v1 whole, which is shorter than its diff:
```python
import jax
import jax.numpy as jnp
from jax import lax
from jax.experimental import pallas as pl
from jax.experimental.pallas import tpu as pltpu
from jax.sharding import PartitionSpec as P

f32 = jnp.float32
bf16 = jnp.bfloat16
VMEM = pl.BlockSpec(memory_space=pltpu.VMEM)
SMEM = pl.BlockSpec(memory_space=pltpu.SMEM)
params = pltpu.CompilerParams(vmem_limit_bytes=40 * 1024 * 1024)


def split(value):
    high = value.astype(bf16)
    low = (value - high.astype(f32)).astype(bf16)
    return high, low


def dot(left, right):
    return jnp.dot(left, right, preferred_element_type=f32)


def dot_rows(left, right):
    return lax.dot_general(left, right, (((0,), (0,)), ((), ())), preferred_element_type=f32)


def dot_fine(left, right):
    return jnp.dot(left, right, precision=lax.Precision.HIGHEST, preferred_element_type=f32)


def rotated(left, right_high, right_low):
    high, low = split(left)
    return dot(high, right_high) + dot(low, right_high) + dot(high, right_low)


def chunks_of(rows, most):
    size = min(rows, most)
    return rows // size, size


def call(body, out_shape, in_specs, scratch=(), cost=None):
    outs = jax.tree.map(lambda _: VMEM, out_shape)
    return pl.pallas_call(
        body,
        out_shape=out_shape,
        in_specs=in_specs,
        out_specs=outs,
        scratch_shapes=list(scratch),
        compiler_params=params,
        cost_estimate=cost,
    )


def shape(*dims):
    return jax.ShapeDtypeStruct(dims, f32)


def first_gram_body(factor_ref, out_ref):
    count, size = chunks_of(factor_ref.shape[0], 1024)
    width = factor_ref.shape[1]

    def step(i, total):
        high, low = split(factor_ref[pl.ds(pl.multiple_of(i * size, size), size), :])
        return total + dot_rows(high, jnp.concatenate([high, low], 1))

    total = lax.fori_loop(0, count, step, jnp.zeros((width, 2 * width), f32))
    cross = total[:, width:]
    out_ref[...] = total[:, :width] + (cross + cross.T)


def project_body(samples_ref, basis_ref, out_ref):
    count, size = chunks_of(basis_ref.shape[0], 1024)

    def step(i, total):
        rows = pl.ds(pl.multiple_of(i * size, size), size)
        left_high, left_low = split(samples_ref[:, rows])
        right_high, right_low = split(basis_ref[rows, :])
        both = dot(left_high, jnp.concatenate([right_high, right_low], 1))
        width = right_high.shape[1]
        return total + both[:, :width] + both[:, width:] + dot(left_low, right_high)

    out_ref[...] = lax.fori_loop(0, count, step, jnp.zeros(out_ref.shape, f32))


def diagonal_of(value, eye):
    return jnp.sum(jnp.where(eye, value, 0.0), axis=0, keepdims=True)


def lanes(value, index):
    return jnp.take_along_axis(value, index, axis=1, mode="promise_in_bounds")


def solve(settled, carried, partner_ref, sign_ref):
    width = settled.shape[0]
    row_id = lax.broadcasted_iota(jnp.int32, (width, width), 0)
    col_id = lax.broadcasted_iota(jnp.int32, (width, width), 1)
    eye = row_id == col_id
    for step in range(partner_ref.shape[0]):
        sign = sign_ref[step : step + 1, :]
        index = jnp.broadcast_to(partner_ref[step : step + 1, :], (width, width))
        swapped = lanes(settled, index)
        own = diagonal_of(settled, eye)
        crossing = diagonal_of(swapped, eye)
        both = lanes(
            jnp.concatenate([jnp.broadcast_to(own, (8, width)), jnp.broadcast_to(crossing, (8, width))], 0),
            index[:16],
        )
        across = sign * (own - both[0:1])
        up = crossing + both[8:9]
        scale = jnp.maximum(jnp.abs(across), jnp.abs(up))
        safe = jnp.where(scale > 0.0, scale, 1.0)
        across = jnp.where(scale > 0.0, across / safe, 1.0)
        up = up / safe
        hypot = jnp.sqrt(across * across + up * up)
        major = jnp.sqrt(0.5 + 0.5 * jnp.abs(across) / hypot)
        minor = 0.5 * jnp.abs(up) / (hypot * major)
        ahead = across >= 0.0
        cosine = jnp.where(ahead, major, minor)
        sine = jnp.where(ahead, minor, major)
        sine = jnp.where(up < 0.0, -sine, sine) * sign
        turned = settled * cosine + swapped * sine
        turned = turned.T
        settled = turned * cosine + lanes(turned, index) * sine
        carried = carried * cosine + lanes(carried, index) * sine
    return settled, carried, eye


def first_solve_body(own_ref, other_ref, partner_ref, sign_ref, turn_ref):
    gram = own_ref[...] + other_ref[...]
    width = gram.shape[0]
    row_id = lax.broadcasted_iota(jnp.int32, (width, width), 0)
    col_id = lax.broadcasted_iota(jnp.int32, (width, width), 1)
    identity = jnp.where(row_id == col_id, 1.0, 0.0).astype(f32)
    settled, turn, _ = solve(gram, identity, partner_ref, sign_ref)
    turn_ref[...] = turn


def rotate_body(place_ref, factor_ref, projected_ref, turn_ref, rise_ref, fall_ref):
    width = factor_ref.shape[1]
    half = width // 2
    packed = factor_ref.shape[0] // 2
    count, size = chunks_of(packed, 512)
    turn = turn_ref[...]
    swapped = jnp.concatenate([turn[:, half:], turn[:, :half]], 1)
    turn = jnp.where(place_ref[0] == 0, swapped, turn)
    rising, falling = turn[:, :half], turn[:, half:]
    empty = jnp.zeros_like(rising)
    weights = jnp.concatenate(
        [
            jnp.concatenate([rising, empty, falling, empty], 1),
            jnp.concatenate([empty, rising, empty, falling], 1),
        ],
        0,
    )
    weights_high, weights_low = split(weights)

    def step(i, _):
        start = pl.multiple_of(i * size, size)
        rows = pl.ds(start, size)
        left = jnp.concatenate(
            [factor_ref[rows, :], factor_ref[pl.ds(pl.multiple_of(packed + start, size), size), :]], 1
        )
        result = rotated(left, weights_high, weights_low)
        rise_ref[rows, :] = result[:, :width]
        fall_ref[rows, :] = result[:, width:]
        return 0

    lax.fori_loop(0, count, step, 0)
    extra = projected_ref.shape[0] // 2
    left = jnp.concatenate([projected_ref[:extra, :], projected_ref[extra:, :]], 1)
    result = rotated(left, weights_high, weights_low)
    rise_ref[packed : packed + extra, :] = result[:, :width]
    fall_ref[packed : packed + extra, :] = result[:, width:]


def folded(whole):
    half = whole.shape[0] // 4

    def block(i, j):
        return whole[i * half : (i + 1) * half, j * half : (j + 1) * half]

    return jnp.concatenate(
        [
            jnp.concatenate([block(0, 0) + block(1, 1), block(0, 2) + block(1, 3)], 1),
            jnp.concatenate([block(2, 0) + block(3, 1), block(2, 2) + block(3, 3)], 1),
        ],
        0,
    )


def second_gram_body(rows, top_ref, bottom_ref, out_ref):
    count, size = chunks_of(rows, 512)
    width = 2 * top_ref.shape[1]

    def step(i, total):
        part = pl.ds(pl.multiple_of(i * size, size), size)
        high, low = split(jnp.concatenate([top_ref[part, :], bottom_ref[part, :]], 1))
        return total + dot_rows(high, jnp.concatenate([high, low], 1))

    total = lax.fori_loop(0, count, step, jnp.zeros((width, 2 * width), f32))
    cross = folded(total[:, width:])
    out_ref[...] = folded(total[:, :width]) + (cross + cross.T)


def second_solve_body(place_ref, own_ref, other_ref, partner_ref, sign_ref, up_ref, down_ref):
    gram = own_ref[...] + other_ref[...]
    width = gram.shape[0]
    half = width // 2
    row_id = lax.broadcasted_iota(jnp.int32, (width, width), 0)
    col_id = lax.broadcasted_iota(jnp.int32, (width, width), 1)
    identity = jnp.where(row_id == col_id, 1.0, 0.0).astype(f32)
    settled, turn, _ = solve(gram, identity, partner_ref, sign_ref)
    empty = jnp.zeros((half, half), f32)
    top = jnp.concatenate(
        [turn[:, :half], jnp.concatenate([settled[:half, :half], empty], 0)], 1
    )
    bottom = jnp.concatenate(
        [turn[:, half:], jnp.concatenate([settled[half:, half:], empty], 0)], 1
    )
    at_first = place_ref[0] == 0
    up_ref[...] = jnp.where(at_first, bottom, top)
    down_ref[...] = jnp.where(at_first, top, bottom)


def cross_body(
    rows, final, place_ref, rise_ref, fall_ref, low1_ref, high1_ref, low2_ref, high2_ref,
    left_ref, right_ref, out_ref,
):
    width = rise_ref.shape[1]
    half = width // 2
    count, size = chunks_of(rows, 512)
    at_first = place_ref[0] == 0
    at_last = place_ref[0] == final

    def sides(part):
        rise = rise_ref[part, :]
        fall = fall_ref[part, :]
        left = jnp.concatenate(
            [
                jnp.where(at_first, fall, low2_ref[part, :]),
                jnp.where(at_first, high1_ref[part, :], fall),
            ],
            1,
        )
        right = jnp.concatenate(
            [
                jnp.where(at_last, low1_ref[part, :], rise),
                jnp.where(at_last, rise, high2_ref[part, :]),
            ],
            1,
        )
        return left, right

    def step(i, total):
        left, right = sides(pl.ds(pl.multiple_of(i * size, size), size))
        left_high, left_low = split(left)
        right_high, right_low = split(right)
        return total + (
            dot_rows(left_high, right_high)
            + dot_rows(left_high, right_low)
            + dot_rows(left_low, right_high)
        )

    total = lax.fori_loop(0, count, step, jnp.zeros((2 * width, 2 * width), f32))
    cross = folded(total)
    left_turn = left_ref[:, :half]
    right_turn = right_ref[:, :half]
    cross = dot_fine(dot_fine(left_turn.T, cross), right_turn)
    extra = rise_ref.shape[0] - rows
    left, right = sides(slice(rows, rows + extra))

    def unpacked(value):
        return jnp.concatenate(
            [
                jnp.concatenate([value[:, :half], value[:, width : width + half]], 1),
                jnp.concatenate([value[:, half:width], value[:, width + half :]], 1),
            ],
            0,
        )

    out_ref[: 2 * extra, :half] = dot_fine(unpacked(left), left_turn)
    out_ref[: 2 * extra, half:] = dot_fine(unpacked(right), right_turn)
    out_ref[2 * extra :, :half] = cross
    out_ref[2 * extra :, half:] = jnp.zeros_like(cross)


def last_solve_body(own_ref, other_ref, left_ref, right_ref, partner_ref, sign_ref, out_ref):
    whole = own_ref[...] + other_ref[...]
    width = whole.shape[1]
    half = width // 2
    rows = whole.shape[0] - half
    cross = whole[rows:, :half]
    gram = jnp.concatenate(
        [
            jnp.concatenate([left_ref[:half, half:], cross], 1),
            jnp.concatenate([cross.T, right_ref[:half, half:]], 1),
        ],
        0,
    )
    settled, projected, eye = solve(gram, whole[:rows], partner_ref, sign_ref)
    squares = jnp.sum(projected * projected, axis=0, keepdims=True) * (1.0 / rows)
    sums = diagonal_of(settled, eye)
    out_ref[...] = jnp.concatenate([sums, squares, jnp.zeros((6, width), f32)], 0)


def shifted(value, steps):
    count = lax.axis_size("blk")
    leading, last = (max(0, -steps), min(count, count - steps))
    return lax.ppermute(value, "blk", [(i, i + steps) for i in range(leading, last)])


def flipped(value, bit):
    return lax.ppermute(value, "rows", [(i, i ^ bit) for i in range(lax.axis_size("rows"))])


def partial_sums(value):
    paired = value + flipped(value, 1)
    return paired, flipped(paired, 2)


def partners_of(pairing):
    width = pairing.shape[-1]
    hits = pairing[..., :, None] == jnp.arange(width, dtype=jnp.int32)
    swapped = pairing.reshape(*pairing.shape[:-1], width // 2, 2)[..., ::-1].reshape(pairing.shape)
    partner = jnp.sum(jnp.where(hits, swapped[..., :, None], 0), axis=-2)
    signs = jnp.where(jnp.arange(width) % 2 == 0, 1.0, -1.0).astype(f32)
    sign = jnp.sum(jnp.where(hits, signs[:, None], 0.0), axis=-2)
    return partner, sign


def on_device(factor_cols, basis_cols, samples, pairing):
    width = factor_cols.shape[1]
    half = width // 2
    packed = factor_cols.shape[0] // 2
    sample_count = samples.shape[0]
    long = packed + sample_count // 2
    position = lax.axis_index("blk")
    final = lax.axis_size("blk") - 1
    at_first = position == 0
    at_last = position == final
    place = position.astype(jnp.int32).reshape(1)
    partner, sign = partners_of(pairing)

    gram = call(first_gram_body, shape(width, width), [VMEM])(factor_cols)
    own, other = partial_sums(gram)
    projected = call(project_body, shape(sample_count, width), [VMEM, VMEM])(samples, basis_cols)
    turn = call(first_solve_body, shape(width, width), [VMEM] * 4)(own, other, partner[0], sign[0])
    rise, fall = call(rotate_body, (shape(long, width), shape(long, width)), [SMEM] + [VMEM] * 3)(
        place, factor_cols, projected, turn
    )
    low1 = shifted(rise, 1)
    high1 = shifted(fall, -1)
    top = jnp.where(at_first, fall, low1)
    bottom = jnp.where(at_last, rise, high1)
    low2 = shifted(top, 1)
    high2 = shifted(bottom, -1)
    gram = call(lambda *refs: second_gram_body(packed, *refs), shape(width, width), [VMEM] * 2)(top, bottom)
    own, other = partial_sums(gram)
    up, down = call(second_solve_body, (shape(width, width), shape(width, width)), [SMEM] + [VMEM] * 4)(
        place, own, other, partner[1], sign[1]
    )
    from_low = shifted(up, 1)
    from_high = shifted(down, -1)
    left = jnp.where(at_first, down, from_low)
    right = jnp.where(at_last, up, from_high)
    whole = call(
        lambda *refs: cross_body(packed, final, *refs),
        shape(sample_count + half, width),
        [SMEM] + [VMEM] * 8,
    )(place, rise, fall, low1, high1, low2, high2, left, right)
    own, other = partial_sums(whole)
    result = call(last_solve_body, shape(8, width), [VMEM] * 6)(
        own, other, left, right, partner[2], sign[2]
    )
    from_low = shifted(result, 1)
    from_high = shifted(result, -1)
    lower = jnp.where(
        at_first, result[:2, :half], jnp.where(position == 1, from_low[:2, half:], from_low[:2, :half])
    )
    upper = jnp.where(at_last, result[:2, :half], from_high[:2, half:])
    both = jnp.concatenate([lower, upper], 1)
    return (both[0], both[1])


def solution(mesh):
    in_specs = (P("rows", "blk"), P("rows", "blk"), P(None, "rows"), P())
    out_specs = (P("blk"), P("blk"))
    return jax.shard_map(
        on_device, mesh=mesh, in_specs=in_specs, out_specs=out_specs, check_vma=False
    )
```

time: 702 us -> 123 us (0.18)
  the two profiles are of different devices: /device:TPU:33 before, /device:TPU:24 now
where the time goes in v1:
time: 123 us; the launch traced here: 122 us
  starting transfers between devices  49.6 us (40%)
  waiting for transfers between devices  44.3 us (36%)
  Pallas kernels  19 us (15%)
  local copies, waits for them, and re-layouts  4.84 us (4%)
  other arithmetic  3.48 us (3%)
    ppermute x8, starting transfers between devices, shifted(): lax.ppermute(value, 'blk', [(i, i + steps) for i in range(leading, last)])  47.7 us
    ppermute x8, waiting for transfers between devices, shifted(): lax.ppermute(value, 'blk', [(i, i + steps) for i in range(leading, last)])  32.4 us
    ppermute x6, waiting for transfers between devices, flipped(): lax.ppermute(value, 'rows', [(i, i ^ bit) for i in range(lax.axis_size('r...  12 us
    pallas_call x1, Pallas kernels, on_device(): call(lambda *refs: cross_body(packed, final, *refs), shape(sample_count +...  3.99 us
    unnamed x11, local copies, waits for them, and re-layouts  3.31 us
    pallas_call x1, Pallas kernels, on_device(): call(last_solve_body, shape(8, width), [VMEM] * 6)  3.13 us
    pallas_call x1, Pallas kernels, on_device(): call(second_solve_body, (shape(width, width), shape(width, width)), [SMEM...  3.01 us
    pallas_call x1, Pallas kernels, on_device(): call(first_solve_body, shape(width, width), [VMEM] * 4)  2.85 us
  transfers between devices with their start and end apart: 14, of which 8 were waited for; matrix products, arithmetic and copies ran while one was open for 4% of the time, Pallas kernels for 5%

profile of v1, /device:TPU:24, one launch (start us, length us, event | category | flops | bytes accessed | tf_op | source)
XLA Modules:
  0.0 122.2 jit_solution(16456156837723970724)
XLA Ops:
  0.6 0.0 copy-start
  0.6 1.6 %copy-done = f32[4096,128]{1,0:T(8,128)S(1)} copy-done((f32[4096,128]{1,0:T(8,128)S(1)}, f32[4096,128]{1,0:T(8,128)}, u32[]{:S(2)}) %copy-start) | copy-done | bytes 2097176
  2.2 1.2 shard_map.60
  3.4 0.1 collective-permute-start
  3.5 0.1 copy.8
  3.7 0.9 rev.3
  4.6 0.1 copy.9
  4.7 1.2 select_reduce_fusion.1
  5.9 0.6 select_reduce_fusion
  6.5 0.0 collective-permute-done
  6.5 0.8 collective-permute-start.1
  7.4 1.6 %copy-done.3 = f32[4096,128]{1,0:T(8,128)S(1)} copy-done((f32[4096,128]{1,0:T(8,128)S(1)}, f32[4096,128]{1,0:T(8,128)}, u32[]{:S(2)}) %copy-start.3) | copy-done | bytes 2097176
  9.0 1.2 %shard_map.59.projected_ref = f32[128,128]{1,0:T(8,128)S(1)} custom-call(f32[128,4096]{1,0:T(8,128)S(1)} %copy-done.2, f32[4096,128]{1,0:T(8,128)S(1)} %copy-done.3), custom_call_target="tpu_custom_call" | custom-call | tf_op jit(solution)/shard_map/pallas_call | solution.py:348
  10.2 0.9 collective-permute-done.1.other_ref
  11.1 2.8 %shard_map.61.turn_ref = f32[128,128]{1,0:T(8,128)S(1)} custom-call(f32[128,128]{1,0:T(8,128)S(1)} %add.15.own_ref, f32[128,128]{1,0:T(8,128)S(1)} %collective-permute-done.1.other_ref, s32[8,128]{1,0:T(8,128)S(1)} %get-tuple-element.15.partner_ref, f32[8,128]{1,0:T(8,128)S(1)} %get-tuple-element.12.sign_ref), custom_call_target="tpu_custom_call" | custom-call | tf_op jit(solution)/shard_map/pallas_call | solution.py:349
  14.0 1.9 %shard_map.62 = (f32[2112,128]{1,0:T(8,128)S(1)}, f32[2112,128]{1,0:T(8,128)S(1)}) custom-call(s32[1]{0:T(128)} %bitcast.place_ref.refs_0_, f32[4096,128]{1,0:T(8,128)S(1)} %copy-done.1, f32[128,128]{1,0:T(8,128)S(1)} %shard_map.59.projected_ref, f32[128,128]{1,0:T(8,128)S(1)} %shard_map.61.turn_ref), custom_call_target="tpu_custom_call" | custom-call | tf_op jit(solution)/shard_map/pallas_call | solution.py:350
  15.8 10.6 %collective-permute-start.3 = (f32[2112,128]{1,0:T(8,128)S(1)}, f32[2112,128]{1,0:T(8,128)S(1)}, u32[]{:S(2)}, u32[]{:S(2)}) collective-permute-start(f32[2112,128]{1,0:T(8,128)S(1)} %get-tuple-element.7.refs_2_), channel_id=1, source_target_pairs={{4,0},{8,4},{12,8},{16,12},{20,16},{24,20},{28,24},{32,28},{36,32}... | collective-permute-start | bytes 3244040 | tf_op jit(solution)/shard_map/ppermute | solution.py:311
  26.5 1.9 %collective-permute-start.2 = (f32[2112,128]{1,0:T(8,128)S(1)}, f32[2112,128]{1,0:T(8,128)}, u32[]{:S(2)}, u32[]{:S(2)}) collective-permute-start(f32[2112,128]{1,0:T(8,128)S(1)} %get-tuple-element.6.refs_1_), channel_id=1, source_target_pairs={{0,4},{4,8},{8,12},{12,16},{16,20},{20,24},{24,28},{28,32},{32,36}... | collective-permute-start | bytes 3244040 | tf_op jit(solution)/shard_map/ppermute | solution.py:311
  28.4 21.0 %collective-permute-done.3.refs_4_ = f32[2112,128]{1,0:T(8,128)S(1)} collective-permute-done((f32[2112,128]{1,0:T(8,128)S(1)}, f32[2112,128]{1,0:T(8,128)S(1)}, u32[]{:S(2)}, u32[]{:S(2)}) %collective-permute-start.3) | collective-permute-done | bytes 1081376 | tf_op jit(solution)/shard_map/ppermute | solution.py:311
  49.4 0.1 broadcast_select_fusion.refs_1_
  49.5 10.1 %collective-permute-start.5 = (f32[2112,128]{1,0:T(8,128)S(1)}, f32[2112,128]{1,0:T(8,128)S(1)}, u32[]{:S(2)}, u32[]{:S(2)}) collective-permute-start(f32[2112,128]{1,0:T(8,128)S(1)} %broadcast_select_fusion.refs_1_), channel_id=1, source_target_pairs={{4,0},{8,4},{12,8},{16,12},{20,16},{24,20},{28,24},{32,28},{36,32}... | collective-permute-start | bytes 3244040 | tf_op jit(solution)/shard_map/ppermute | solution.py:311
  59.7 0.0 collective-permute-done.2.refs_3_
  59.7 1.4 %broadcast_select_fusion.1.refs_0_ = f32[2112,128]{1,0:T(8,128)S(1)} fusion(f32[2112,128]{1,0:T(8,128)S(1)} %get-tuple-element.7.refs_2_, f32[2112,128]{1,0:T(8,128)} %collective-permute-done.2.refs_3_, pred[]{:T(512)S(6)} %eq.28), kind=kLoop, calls=%fused_computation.4 | loop fusion | flops 270336 | bytes 3244033 | tf_op jit(solution)/shard_map/jit(_where)/select_n | solution.py:355
  61.0 1.9 %collective-permute-start.4 = (f32[2112,128]{1,0:T(8,128)S(1)}, f32[2112,128]{1,0:T(8,128)S(1)}, u32[]{:S(2)}, u32[]{:S(2)}) collective-permute-start(f32[2112,128]{1,0:T(8,128)S(1)} %broadcast_select_fusion.1.refs_0_), channel_id=1, source_target_pairs={{0,4},{4,8},{8,12},{12,16},{16,20},{20,24},{24,28},{28,32},{32,36}... | collective-permute-start | bytes 3244040 | tf_op jit(solution)/shard_map/ppermute | solution.py:311
  63.0 1.7 %shard_map.63 = f32[128,128]{1,0:T(8,128)S(1)} custom-call(f32[2112,128]{1,0:T(8,128)S(1)} %broadcast_select_fusion.1.refs_0_, f32[2112,128]{1,0:T(8,128)S(1)} %broadcast_select_fusion.refs_1_), custom_call_target="tpu_custom_call" | custom-call | tf_op jit(solution)/shard_map/pallas_call | solution.py:359
  64.7 0.1 collective-permute-start.6
  64.8 1.2 %collective-permute-done.6 = f32[128,128]{1,0:T(8,128)S(1)} collective-permute-done((f32[128,128]{1,0:T(8,128)S(1)}, f32[128,128]{1,0:T(8,128)S(1)}, u32[]{:S(2)}, u32[]{:S(2)}) %collective-permute-start.6) | collective-permute-done | bytes 65568 | tf_op jit(solution)/shard_map/ppermute | solution.py:315
  66.1 0.4 collective-permute-start.7
  66.5 4.0 %collective-permute-done.7.other_ref = f32[128,128]{1,0:T(8,128)S(1)} collective-permute-done((f32[128,128]{1,0:T(8,128)S(1)}, f32[128,128]{1,0:T(8,128)S(1)}, u32[]{:S(2)}, u32[]{:S(2)}) %collective-permute-start.7) | collective-permute-done | bytes 65568 | tf_op jit(solution)/shard_map/ppermute | solution.py:315
  70.4 3.0 %shard_map.64 = (f32[128,128]{1,0:T(8,128)S(1)}, f32[128,128]{1,0:T(8,128)S(1)}) custom-call(s32[1]{0:T(128)} %bitcast.place_ref.refs_0_, f32[128,128]{1,0:T(8,128)S(1)} %add.17.own_ref, f32[128,128]{1,0:T(8,128)S(1)} %collective-permute-done.7.other_ref, s32[8,128]{1,0:T(8,128)S(1)} %get-tuple-element.14.partner_ref, f32[8,128]{1,0:T(8,128)S(1)} %get-tuple-element.11.sign_ref), custom_call_target="tpu_custom_call" | custom-call | tf_op jit(solution)/shard_map/pallas_call | solution.py:361
  73.4 9.6 %collective-permute-start.9 = (f32[128,128]{1,0:T(8,128)S(1)}, f32[128,128]{1,0:T(8,128)S(1)}, u32[]{:S(2)}, u32[]{:S(2)}) collective-permute-start(f32[128,128]{1,0:T(8,128)S(1)} %get-tuple-element.8), channel_id=1, source_target_pairs={{4,0},{8,4},{12,8},{16,12},{20,16},{24,20},{28,24},{32,28},{36,32}... | collective-permute-start | bytes 196616 | tf_op jit(solution)/shard_map/ppermute | solution.py:311
  83.1 1.9 %collective-permute-start.8 = (f32[128,128]{1,0:T(8,128)S(1)}, f32[128,128]{1,0:T(8,128)S(1)}, u32[]{:S(2)}, u32[]{:S(2)}) collective-permute-start(f32[128,128]{1,0:T(8,128)S(1)} %get-tuple-element.9), channel_id=1, source_target_pairs={{0,4},{4,8},{8,12},{12,16},{16,20},{20,24},{24,28},{28,32},{32,36}... | collective-permute-start | bytes 196616 | tf_op jit(solution)/shard_map/ppermute | solution.py:311
  85.0 0.0 collective-permute-done.9
  85.1 10.0 %collective-permute-done.8 = f32[128,128]{1,0:T(8,128)S(1)} collective-permute-done((f32[128,128]{1,0:T(8,128)S(1)}, f32[128,128]{1,0:T(8,128)S(1)}, u32[]{:S(2)}, u32[]{:S(2)}) %collective-permute-start.8) | collective-permute-done | bytes 65568 | tf_op jit(solution)/shard_map/ppermute | solution.py:311
  95.1 0.0 collective-permute-done.4.refs_5_
  95.1 4.0 %shard_map.65 = f32[192,128]{1,0:T(8,128)S(1)} custom-call(s32[1]{0:T(128)} %bitcast.place_ref.refs_0_, f32[2112,128]{1,0:T(8,128)S(1)} %get-tuple-element.6.refs_1_, f32[2112,128]{1,0:T(8,128)S(1)} %get-tuple-element.7.refs_2_, f32[2112,128]{1,0:T(8,128)} %collective-permute-done.2.refs_3_, f32[2112,128]{1,0:T(8,128)S(1)} %collective-permute-done.3.refs_4_, ...), custom_call_target="tpu_custom_call" | custom-call | tf_op jit(solution)/shard_map/pallas_call | solution.py:368
  99.1 0.1 collective-permute-start.10
  99.2 1.3 %collective-permute-done.10 = f32[192,128]{1,0:T(8,128)S(1)} collective-permute-done((f32[192,128]{1,0:T(8,128)S(1)}, f32[192,128]{1,0:T(8,128)S(1)}, u32[]{:S(2)}, u32[]{:S(2)}) %collective-permute-start.10) | collective-permute-done | bytes 98336 | tf_op jit(solution)/shard_map/ppermute | solution.py:315
  100.5 0.4 collective-permute-start.11
  100.9 4.6 %collective-permute-done.11.other_ref = f32[192,128]{1,0:T(8,128)S(1)} collective-permute-done((f32[192,128]{1,0:T(8,128)S(1)}, f32[192,128]{1,0:T(8,128)S(1)}, u32[]{:S(2)}, u32[]{:S(2)}) %collective-permute-start.11) | collective-permute-done | bytes 98336 | tf_op jit(solution)/shard_map/ppermute | solution.py:315
  105.5 3.1 %shard_map.66 = f32[8,128]{1,0:T(8,128)S(1)} custom-call(f32[192,128]{1,0:T(8,128)S(1)} %add.18.own_ref, f32[192,128]{1,0:T(8,128)S(1)} %collective-permute-done.11.other_ref, f32[128,128]{1,0:T(8,128)S(1)} %broadcast_select_fusion.3.refs_7_.left_ref, f32[128,128]{1,0:T(8,128)S(1)} %broadcast_select_fusion.2.refs_8_.right_ref, ...), custom_call_target="tpu_custom_call" | custom-call | tf_op jit(solution)/shard_map/pallas_call | solution.py:374
  108.6 1.9 %collective-permute-start.12 = (f32[8,128]{1,0:T(8,128)S(1)}, f32[8,128]{1,0:T(8,128)S(1)}, u32[]{:S(2)}, u32[]{:S(2)}) collective-permute-start(f32[8,128]{1,0:T(8,128)S(1)} %shard_map.66), channel_id=1, source_target_pairs={{0,4},{4,8},{8,12},{12,16},{16,20},{20,24},{24,28},{28,32},{32,36}... | collective-permute-start | bytes 12296 | tf_op jit(solution)/shard_map/ppermute | solution.py:311
  110.5 9.6 %collective-permute-start.13 = (f32[8,128]{1,0:T(8,128)S(1)}, f32[8,128]{1,0:T(8,128)S(1)}, u32[]{:S(2)}, u32[]{:S(2)}) collective-permute-start(f32[8,128]{1,0:T(8,128)S(1)} %shard_map.66), channel_id=1, source_target_pairs={{4,0},{8,4},{12,8},{16,12},{20,16},{24,20},{28,24},{32,28},{36,32}... | collective-permute-start | bytes 12296 | tf_op jit(solution)/shard_map/ppermute | solution.py:311
  120.2 0.0 collective-permute-done.12
  120.2 1.3 %collective-permute-done.13 = f32[8,128]{1,0:T(8,128)S(1)} collective-permute-done((f32[8,128]{1,0:T(8,128)S(1)}, f32[8,128]{1,0:T(8,128)S(1)}, u32[]{:S(2)}, u32[]{:S(2)}) %collective-permute-start.13) | collective-permute-done | bytes 4128 | tf_op jit(solution)/shard_map/ppermute | solution.py:311
  121.5 0.1 select_select_fusion
  121.6 0.1 pad_maximum_fusion
  121.6 0.5 slice_bitcast_fusion.6
  (16 shorter events, 0.1 us)
Async XLA Ops:
  0.6 1.6 %copy-start = (f32[4096,128]{1,0:T(8,128)S(1)}, f32[4096,128]{1,0:T(8,128)}, u32[]{:S(2)}) copy-start(f32[4096,128]{1,0:T(8,128)} %factor_ref.3) | copy-start | bytes 6291460
  2.2 1.3 %copy-start.4 = (s32[3,8,128]{2,1,0:T(8,128)S(1)}, s32[3,8,128]{2,1,0:T(8,128)}, u32[]{:S(2)}) copy-start(s32[3,8,128]{2,1,0:T(8,128)} %param.7) | copy-start | bytes 36868
  2.2 5.1 %copy-start.2 = (f32[128,4096]{1,0:T(8,128)S(1)}, f32[128,4096]{1,0:T(8,128)}, u32[]{:S(2)}) copy-start(f32[128,4096]{1,0:T(8,128)} %samples_ref.1) | copy-start | bytes 6291460
  3.4 3.1 %collective-permute-start = (f32[128,128]{1,0:T(8,128)S(1)}, f32[128,128]{1,0:T(8,128)S(1)}, u32[]{:S(2)}, u32[]{:S(2)}) collective-permute-start(f32[128,128]{1,0:T(8,128)S(1)} %shard_map.60), channel_id=1, source_target_pairs={{0,1},{1,0},{2,3},{3,2},{4,5},{5,4},{6,7},{7,6},{8,9},{9,8},{10,11... | collective-permute-start | bytes 196616 | tf_op jit(solution)/shard_map/ppermute | solution.py:315
  6.5 4.6 %collective-permute-start.1 = (f32[128,128]{1,0:T(8,128)S(1)}, f32[128,128]{1,0:T(8,128)S(1)}, u32[]{:S(2)}, u32[]{:S(2)}) collective-permute-start(f32[128,128]{1,0:T(8,128)S(1)} %add.15.own_ref), channel_id=1, source_target_pairs={{0,2},{1,3},{2,0},{3,1},{4,6},{5,7},{6,4},{7,5},{8,10},{9,11},{10,... | collective-permute-start | bytes 196616 | tf_op jit(solution)/shard_map/ppermute | solution.py:315
  7.4 1.6 %copy-start.3 = (f32[4096,128]{1,0:T(8,128)S(1)}, f32[4096,128]{1,0:T(8,128)}, u32[]{:S(2)}) copy-start(f32[4096,128]{1,0:T(8,128)} %basis_ref.1) | copy-start | bytes 6291460
  9.0 5.0 %copy-start.1 = (f32[4096,128]{1,0:T(8,128)S(1)}, f32[4096,128]{1,0:T(8,128)}, u32[]{:S(2)}) copy-start(f32[4096,128]{1,0:T(8,128)} %factor_ref.3) | copy-start | bytes 6291460
  15.8 33.6 %collective-permute-start.3 = (f32[2112,128]{1,0:T(8,128)S(1)}, f32[2112,128]{1,0:T(8,128)S(1)}, u32[]{:S(2)}, u32[]{:S(2)}) collective-permute-start(f32[2112,128]{1,0:T(8,128)S(1)} %get-tuple-element.7.refs_2_), channel_id=1, source_target_pairs={{4,0},{8,4},{12,8},{16,12},{20,16},{24,20},{28,24},{32,28},{36,32}... | collective-permute-start | bytes 3244040 | tf_op jit(solution)/shard_map/ppermute | solution.py:311
  26.5 33.2 %collective-permute-start.2 = (f32[2112,128]{1,0:T(8,128)S(1)}, f32[2112,128]{1,0:T(8,128)}, u32[]{:S(2)}, u32[]{:S(2)}) collective-permute-start(f32[2112,128]{1,0:T(8,128)S(1)} %get-tuple-element.6.refs_1_), channel_id=1, source_target_pairs={{0,4},{4,8},{8,12},{12,16},{16,20},{20,24},{24,28},{28,32},{32,36}... | collective-permute-start | bytes 3244040 | tf_op jit(solution)/shard_map/ppermute | solution.py:311
  49.5 45.6 %collective-permute-start.5 = (f32[2112,128]{1,0:T(8,128)S(1)}, f32[2112,128]{1,0:T(8,128)S(1)}, u32[]{:S(2)}, u32[]{:S(2)}) collective-permute-start(f32[2112,128]{1,0:T(8,128)S(1)} %broadcast_select_fusion.refs_1_), channel_id=1, source_target_pairs={{4,0},{8,4},{12,8},{16,12},{20,16},{24,20},{28,24},{32,28},{36,32}... | collective-permute-start | bytes 3244040 | tf_op jit(solution)/shard_map/ppermute | solution.py:311
  61.0 34.1 %collective-permute-start.4 = (f32[2112,128]{1,0:T(8,128)S(1)}, f32[2112,128]{1,0:T(8,128)S(1)}, u32[]{:S(2)}, u32[]{:S(2)}) collective-permute-start(f32[2112,128]{1,0:T(8,128)S(1)} %broadcast_select_fusion.1.refs_0_), channel_id=1, source_target_pairs={{0,4},{4,8},{8,12},{12,16},{16,20},{20,24},{24,28},{28,32},{32,36}... | collective-permute-start | bytes 3244040 | tf_op jit(solution)/shard_map/ppermute | solution.py:311
  64.7 1.3 %collective-permute-start.6 = (f32[128,128]{1,0:T(8,128)S(1)}, f32[128,128]{1,0:T(8,128)S(1)}, u32[]{:S(2)}, u32[]{:S(2)}) collective-permute-start(f32[128,128]{1,0:T(8,128)S(1)} %shard_map.63), channel_id=1, source_target_pairs={{0,1},{1,0},{2,3},{3,2},{4,5},{5,4},{6,7},{7,6},{8,9},{9,8},{10,11... | collective-permute-start | bytes 196616 | tf_op jit(solution)/shard_map/ppermute | solution.py:315
  66.1 4.4 %collective-permute-start.7 = (f32[128,128]{1,0:T(8,128)S(1)}, f32[128,128]{1,0:T(8,128)S(1)}, u32[]{:S(2)}, u32[]{:S(2)}) collective-permute-start(f32[128,128]{1,0:T(8,128)S(1)} %add.17.own_ref), channel_id=1, source_target_pairs={{0,2},{1,3},{2,0},{3,1},{4,6},{5,7},{6,4},{7,5},{8,10},{9,11},{10,... | collective-permute-start | bytes 196616 | tf_op jit(solution)/shard_map/ppermute | solution.py:315
  73.4 11.6 %collective-permute-start.9 = (f32[128,128]{1,0:T(8,128)S(1)}, f32[128,128]{1,0:T(8,128)S(1)}, u32[]{:S(2)}, u32[]{:S(2)}) collective-permute-start(f32[128,128]{1,0:T(8,128)S(1)} %get-tuple-element.8), channel_id=1, source_target_pairs={{4,0},{8,4},{12,8},{16,12},{20,16},{24,20},{28,24},{32,28},{36,32}... | collective-permute-start | bytes 196616 | tf_op jit(solution)/shard_map/ppermute | solution.py:311
  83.1 12.0 %collective-permute-start.8 = (f32[128,128]{1,0:T(8,128)S(1)}, f32[128,128]{1,0:T(8,128)S(1)}, u32[]{:S(2)}, u32[]{:S(2)}) collective-permute-start(f32[128,128]{1,0:T(8,128)S(1)} %get-tuple-element.9), channel_id=1, source_target_pairs={{0,4},{4,8},{8,12},{12,16},{16,20},{20,24},{24,28},{28,32},{32,36}... | collective-permute-start | bytes 196616 | tf_op jit(solution)/shard_map/ppermute | solution.py:311
  99.1 1.4 %collective-permute-start.10 = (f32[192,128]{1,0:T(8,128)S(1)}, f32[192,128]{1,0:T(8,128)S(1)}, u32[]{:S(2)}, u32[]{:S(2)}) collective-permute-start(f32[192,128]{1,0:T(8,128)S(1)} %shard_map.65), channel_id=1, source_target_pairs={{0,1},{1,0},{2,3},{3,2},{4,5},{5,4},{6,7},{7,6},{8,9},{9,8},{10,11... | collective-permute-start | bytes 294920 | tf_op jit(solution)/shard_map/ppermute | solution.py:315
  100.5 4.9 %collective-permute-start.11 = (f32[192,128]{1,0:T(8,128)S(1)}, f32[192,128]{1,0:T(8,128)S(1)}, u32[]{:S(2)}, u32[]{:S(2)}) collective-permute-start(f32[192,128]{1,0:T(8,128)S(1)} %add.18.own_ref), channel_id=1, source_target_pairs={{0,2},{1,3},{2,0},{3,1},{4,6},{5,7},{6,4},{7,5},{8,10},{9,11},{10,... | collective-permute-start | bytes 294920 | tf_op jit(solution)/shard_map/ppermute | solution.py:315
  108.6 11.6 %collective-permute-start.12 = (f32[8,128]{1,0:T(8,128)S(1)}, f32[8,128]{1,0:T(8,128)S(1)}, u32[]{:S(2)}, u32[]{:S(2)}) collective-permute-start(f32[8,128]{1,0:T(8,128)S(1)} %shard_map.66), channel_id=1, source_target_pairs={{0,4},{4,8},{8,12},{12,16},{16,20},{20,24},{24,28},{28,32},{32,36}... | collective-permute-start | bytes 12296 | tf_op jit(solution)/shard_map/ppermute | solution.py:311
  110.5 11.0 %collective-permute-start.13 = (f32[8,128]{1,0:T(8,128)S(1)}, f32[8,128]{1,0:T(8,128)S(1)}, u32[]{:S(2)}, u32[]{:S(2)}) collective-permute-start(f32[8,128]{1,0:T(8,128)S(1)} %shard_map.66), channel_id=1, source_target_pairs={{4,0},{8,4},{12,8},{16,12},{20,16},{24,20},{28,24},{32,28},{36,32}... | collective-permute-start | bytes 12296 | tf_op jit(solution)/shard_map/ppermute | solution.py:311

commit v2 on v0

v2 whole, which is shorter than its diff:
```python
import jax
import jax.numpy as jnp
from jax import lax
from jax.experimental import pallas as pl
from jax.experimental.pallas import tpu as pltpu
from jax.sharding import PartitionSpec as P

f32 = jnp.float32
bf16 = jnp.bfloat16
i32 = jnp.int32
VMEM = pl.BlockSpec(memory_space=pltpu.VMEM)
params = pltpu.CompilerParams(vmem_limit_bytes=24 * 1024 * 1024)
PIECES = 1


def split(value):
    high = value.astype(bf16)
    low = (value - high.astype(f32)).astype(bf16)
    return high, low


def dot(left, right):
    return jnp.dot(left, right, preferred_element_type=f32)


def dot_rows(left, right):
    return lax.dot_general(left, right, (((0,), (0,)), ((), ())), preferred_element_type=f32)


def dot_fine(left, right):
    return jnp.dot(left, right, precision=lax.Precision.HIGHEST, preferred_element_type=f32)


def rotated(left, right):
    high, low = split(left)
    return dot(jnp.concatenate([high, low, high], 1), right)


def stacked(right):
    high, low = split(right)
    return jnp.concatenate([high, high, low], 0)


def chunks_of(rows, most):
    size = min(rows, most)
    return rows // size, size


def rows_at(index, size):
    return pl.ds(pl.multiple_of(index * size, size), size)


def call(body, out_shape, in_specs):
    return pl.pallas_call(
        body,
        out_shape=out_shape,
        in_specs=in_specs,
        out_specs=jax.tree.map(lambda _: VMEM, out_shape),
        compiler_params=params,
    )


def shape(*dims, dtype=f32):
    return jax.ShapeDtypeStruct(dims, dtype)


def swapped_rows(value):
    half = value.shape[0] // 2
    return jnp.concatenate([value[half:], value[:half]], 0)


def swapped_cols(value):
    half = value.shape[1] // 2
    return jnp.concatenate([value[:, half:], value[:, :half]], 1)


def first_gram_body(factor_ref, out_ref, total_ref):
    width = factor_ref.shape[1]
    step = pl.program_id(0)
    high, low = split(factor_ref[...])
    part = dot_rows(high, jnp.concatenate([high, low], 1))

    @pl.when(step == 0)
    def _():
        total_ref[...] = part

    @pl.when(step > 0)
    def _():
        total_ref[...] += part

    @pl.when(step == pl.num_programs(0) - 1)
    def _():
        total = total_ref[...]
        cross = total[:, width:]
        out_ref[...] = total[:, :width] + (cross + cross.T)


def first_gram(factor_cols):
    rows, width = factor_cols.shape
    count, size = chunks_of(rows, 1024)
    return pl.pallas_call(
        first_gram_body,
        out_shape=shape(width, width),
        grid=(count,),
        in_specs=[pl.BlockSpec((size, width), lambda i: (i, 0))],
        out_specs=pl.BlockSpec((width, width), lambda i: (0, 0)),
        scratch_shapes=[pltpu.VMEM((width, 2 * width), f32)],
        compiler_params=params,
    )(factor_cols)


def project_body(samples_ref, basis_ref, order_ref, out_ref, partner_ref, sign_ref):
    width = basis_ref.shape[1]
    count, size = chunks_of(basis_ref.shape[0], 1024)

    def step(i, total):
        rows = rows_at(i, size)
        left_high, left_low = split(samples_ref[:, rows])
        right_high, right_low = split(basis_ref[rows, :])
        both = dot(left_high, jnp.concatenate([right_high, right_low], 1))
        return total + both[:, :width] + both[:, width:] + dot(left_low, right_high)

    out_ref[...] = lax.fori_loop(0, count, step, jnp.zeros(out_ref.shape, f32))

    lines = order_ref.shape[0]
    order = order_ref[...]
    lane = lax.broadcasted_iota(i32, (lines, width), 1)
    ahead = jnp.concatenate([order[:, 1:], order[:, :1]], 1)
    behind = jnp.concatenate([order[:, -1:], order[:, :-1]], 1)
    even = lane % 2 == 0
    other = jnp.where(even, ahead, behind + width)
    filler = jnp.zeros((width - lines, width), i32)
    order = jnp.concatenate([order, filler], 0).T
    other = jnp.concatenate([other, filler], 0).T
    column = lax.broadcasted_iota(i32, (width, width), 1)
    found = []
    for line in range(lines):
        hits = jnp.where(order[:, line : line + 1] == column, other[:, line : line + 1], 0)
        found.append(jnp.sum(hits, axis=0, keepdims=True))
    found = jnp.concatenate(found, 0)
    first = found < width
    partner_ref[...] = jnp.where(first, found, found - width)
    sign_ref[...] = jnp.where(first, 1.0, -1.0).astype(f32)


def diagonal_of(value, eye):
    return jnp.sum(jnp.where(eye, value, 0.0), axis=0, keepdims=True)


def lanes(value, index):
    return jnp.take_along_axis(value, index, axis=1, mode="promise_in_bounds")


def eye_of(width):
    row_id = lax.broadcasted_iota(i32, (width, width), 0)
    col_id = lax.broadcasted_iota(i32, (width, width), 1)
    return row_id == col_id


def turn_step(settled, carried, eye, index, sign):
    width = settled.shape[0]
    swapped = lanes(settled, index)
    own = diagonal_of(settled, eye)
    crossing = diagonal_of(swapped, eye)
    both = lanes(
        jnp.concatenate([jnp.broadcast_to(own, (8, width)), jnp.broadcast_to(crossing, (8, width))], 0),
        index[:16],
    )
    across = sign * (own - both[0:1])
    up = crossing + both[8:9]
    scale = jnp.maximum(jnp.abs(across), jnp.abs(up))
    safe = jnp.where(scale > 0.0, scale, 1.0)
    across = jnp.where(scale > 0.0, across / safe, 1.0)
    up = up / safe
    hypot = jnp.sqrt(across * across + up * up)
    major = jnp.sqrt(0.5 + 0.5 * jnp.abs(across) / hypot)
    minor = 0.5 * jnp.abs(up) / (hypot * major)
    ahead = across >= 0.0
    cosine = jnp.where(ahead, major, minor)
    sine = jnp.where(ahead, minor, major)
    sine = jnp.where(up < 0.0, -sine, sine) * sign
    turned = (settled * cosine + swapped * sine).T
    settled = turned * cosine + lanes(turned, index) * sine
    carried = carried * cosine + lanes(carried, index) * sine
    return settled, carried


def solve(problems, partners, signs):
    width = problems[0][0].shape[0]
    eye = eye_of(width)
    for step in range(partners.shape[0]):
        sign = signs[step : step + 1, :]
        index = jnp.broadcast_to(partners[step : step + 1, :], (width, width))
        problems = [turn_step(*problem, eye, index, sign) for problem in problems]
    return problems


def round_of(ref, index, rounds):
    steps = ref.shape[0] // rounds
    return ref[index * steps : (index + 1) * steps, :]


def blk_index():
    return lax.axis_index("blk").astype(i32)


def top_goes_odd():
    position = blk_index()
    return jnp.logical_or(position % 2 == 1, position == 0)


def odd_takes_top(final):
    position = blk_index()
    return jnp.logical_or(position % 2 == 0, position == final)


def even_takes_top():
    position = blk_index()
    return jnp.logical_and(position % 2 == 1, position != 1)


def identity_of(width):
    return jnp.where(eye_of(width), 1.0, 0.0).astype(f32)


def first_solve_body(rounds, own_ref, other_ref, partner_ref, sign_ref, turn_ref):
    gram = own_ref[...] + other_ref[...]
    ((_, turn_ref[...]),) = solve(
        [(gram, identity_of(gram.shape[0]))],
        round_of(partner_ref, 0, rounds),
        round_of(sign_ref, 0, rounds),
    )


def rotate_body(factor_ref, projected_ref, turn_ref, *out_refs):
    odd_refs, even_refs = out_refs[: len(out_refs) // 2], out_refs[len(out_refs) // 2 :]
    width = factor_ref.shape[1]
    half = width // 2
    packed = factor_ref.shape[0] // 2
    turn = turn_ref[...]
    turn = jnp.where(top_goes_odd(), turn, swapped_cols(turn))
    for_odd, for_even = turn[:, :half], turn[:, half:]
    empty = jnp.zeros_like(for_odd)
    weights = jnp.concatenate(
        [
            jnp.concatenate([for_odd, empty, for_even, empty], 1),
            jnp.concatenate([empty, for_odd, empty, for_even], 1),
        ],
        0,
    )
    weights = stacked(weights)
    piece = packed // len(odd_refs)
    count, size = chunks_of(piece, 512)
    for number, (odd_ref, even_ref) in enumerate(zip(odd_refs, even_refs)):

        def step(i, _):
            start = pl.multiple_of(i * size, size)
            lower = pl.ds(pl.multiple_of(number * piece + start, size), size)
            upper = pl.ds(pl.multiple_of(packed + number * piece + start, size), size)
            left = jnp.concatenate([factor_ref[lower, :], factor_ref[upper, :]], 1)
            result = rotated(left, weights)
            odd_ref[pl.ds(start, size), :] = result[:, :width]
            even_ref[pl.ds(start, size), :] = result[:, width:]
            return 0

        lax.fori_loop(0, count, step, 0)
    extra = projected_ref.shape[0] // 2
    left = jnp.concatenate([projected_ref[:extra, :], projected_ref[extra:, :]], 1)
    result = rotated(left, weights)
    odd_refs[-1][piece : piece + extra, :] = result[:, :width]
    even_refs[-1][piece : piece + extra, :] = result[:, width:]


def folded(whole):
    half = whole.shape[0] // 4

    def block(i, j):
        return whole[i * half : (i + 1) * half, j * half : (j + 1) * half]

    return jnp.concatenate(
        [
            jnp.concatenate([block(0, 0) + block(1, 1), block(0, 2) + block(1, 3)], 1),
            jnp.concatenate([block(2, 0) + block(3, 1), block(2, 2) + block(3, 3)], 1),
        ],
        0,
    )


def second_gram_body(piece, *refs):
    refs, out_ref = refs[:-1], refs[-1]
    odd_refs, even_refs = refs[: len(refs) // 2], refs[len(refs) // 2 :]
    count, size = chunks_of(piece, 512)
    width = 2 * odd_refs[0].shape[1]
    total = jnp.zeros((width, 2 * width), f32)
    for odd_ref, even_ref in zip(odd_refs, even_refs):

        def step(i, total):
            part = rows_at(i, size)
            high, low = split(jnp.concatenate([odd_ref[part, :], even_ref[part, :]], 1))
            return total + dot_rows(high, jnp.concatenate([high, low], 1))

        total = lax.fori_loop(0, count, step, total)
    cross = folded(total[:, width:])
    gram = folded(total[:, :width]) + (cross + cross.T)
    out_ref[...] = jnp.where(blk_index() % 2 == 1, swapped_rows(swapped_cols(gram)), gram)


def second_solve_body(rounds, own_ref, other_ref, partner_ref, sign_ref, out_ref):
    gram = own_ref[...] + other_ref[...]
    width = gram.shape[0]
    half = width // 2
    ((settled, turn),) = solve(
        [(gram, identity_of(width))], round_of(partner_ref, 1, rounds), round_of(sign_ref, 1, rounds)
    )
    take_top = jnp.logical_xor(top_goes_odd(), lax.axis_index("rows") % 2 == 1)
    out_ref[:, :half] = jnp.where(take_top, turn[:, :half], turn[:, half:])
    out_ref[:half, half:] = jnp.where(take_top, settled[:half, :half], settled[half:, half:])
    out_ref[half:, half:] = jnp.zeros((half, half), f32)


def cross_body(piece, final, *refs):
    refs, out_ref = refs[:-1], refs[-1]
    number = len(refs) // 5
    odd_far, odd_own, even_own, even_far, even_once = (
        refs[i * number : (i + 1) * number] for i in range(5)
    )
    position = blk_index()
    at_edge = jnp.logical_or(position == 0, position == final)
    width = odd_own[0].shape[1]
    half = width // 2
    count, size = chunks_of(piece, 512)

    def sides(index, part):
        return (
            jnp.concatenate(
                [
                    jnp.where(at_edge, even_once[index][part, :], odd_far[index][part, :]),
                    odd_own[index][part, :],
                ],
                1,
            ),
            jnp.concatenate([even_own[index][part, :], even_far[index][part, :]], 1),
        )

    total = jnp.zeros((2 * width, 2 * width), f32)
    for index in range(number):

        def step(i, total):
            left, right = sides(index, rows_at(i, size))
            left_high, left_low = split(left)
            right_high, right_low = split(right)
            return total + dot_rows(
                jnp.concatenate([left_high, left_high, left_low], 0),
                jnp.concatenate([right_high, right_low, right_high], 0),
            )

        total = lax.fori_loop(0, count, step, total)
    out_ref[:width, :] = folded(total)
    extra = odd_own[-1].shape[0] - piece
    for side, value in enumerate(sides(-1, slice(piece, piece + extra))):
        start = width + side * 2 * extra
        out_ref[start : start + extra, :half] = value[:, :half]
        out_ref[start : start + extra, half:] = value[:, width : width + half]
        out_ref[start + extra : start + 2 * extra, :half] = value[:, half:width]
        out_ref[start + extra : start + 2 * extra, half:] = value[:, width + half :]


def combine_body(final, cross_ref, own_ref, other_ref, out_ref):
    width = cross_ref.shape[1]
    half = width // 2
    count = (cross_ref.shape[0] - width) // 2
    position = blk_index()
    odd = position % 2 == 1
    at_edge = jnp.logical_or(position == 0, position == final)
    first_core = lax.axis_index("rows") % 2 == 0
    from_odd = jnp.where(first_core, own_ref[...], other_ref[...])
    from_even = jnp.where(first_core, other_ref[...], own_ref[...])
    odd_turn, even_turn = from_odd[:, :half], from_even[:, :half]
    odd_turn = jnp.where(jnp.logical_xor(odd, at_edge), swapped_rows(odd_turn), odd_turn)
    even_turn = jnp.where(odd, swapped_rows(even_turn), even_turn)
    cross = dot_fine(dot_fine(odd_turn.T, cross_ref[:width, :]), even_turn)
    cross_turned = cross.T
    share = 0.25
    odd_gram = from_odd[:half, half:] * share
    even_gram = from_even[:half, half:] * share
    odd_samples = dot_fine(cross_ref[width : width + count, :], odd_turn)
    even_samples = dot_fine(cross_ref[width + count :, :], even_turn)
    straight = jnp.concatenate(
        [
            jnp.concatenate([odd_gram, cross], 1),
            jnp.concatenate([cross_turned, even_gram], 1),
            jnp.concatenate([odd_samples, even_samples], 1),
        ],
        0,
    )
    turned = jnp.concatenate(
        [
            jnp.concatenate([even_gram, cross_turned], 1),
            jnp.concatenate([cross, odd_gram], 1),
            jnp.concatenate([even_samples, odd_samples], 1),
        ],
        0,
    )
    out_ref[...] = jnp.where(odd, turned, straight)


def last_solve_body(
    rounds, final, odd_ref, odd_other_ref, even_ref, even_other_ref, partner_ref, sign_ref, sums_ref, squares_ref
):
    wholes = [odd_ref[...] + odd_other_ref[...], even_ref[...] + even_other_ref[...]]
    width = wholes[0].shape[1]
    half = width // 2
    samples = wholes[0].shape[0] - width
    solved = solve(
        [(whole[:width], whole[width:]) for whole in wholes],
        round_of(partner_ref, 2, rounds),
        round_of(sign_ref, 2, rounds),
    )
    takes = [odd_takes_top(final), even_takes_top()]
    halves = []
    for (settled, projected), take_top in zip(solved, takes):
        sums = diagonal_of(settled, eye_of(width))
        squares = jnp.sum(projected * projected, axis=0, keepdims=True) * (1.0 / samples)
        both = jnp.concatenate([sums, squares], 0)
        halves.append(jnp.where(take_top, both[:, :half], both[:, half:]))
    odd = blk_index() % 2 == 1
    first = jnp.where(odd, halves[1], halves[0])
    second = jnp.where(odd, halves[0], halves[1])
    result = jnp.concatenate([first, second], 1)
    sums_ref[...] = result[0:1]
    squares_ref[...] = result[1:2]


def odd_partner(position, count):
    partner = position - 1 if position % 2 == 0 else position + 1
    return partner if 0 <= partner < count else position


def even_partner(position):
    return position + 1 if position % 2 == 0 else position - 1


def via_odd(value, closed):
    count = lax.axis_size("blk")
    pairs = [(i, odd_partner(i, count)) for i in range(count)]
    return lax.ppermute(value, "blk", [pair for pair in pairs if closed or pair[0] != pair[1]])


def via_even(value):
    count = lax.axis_size("blk")
    return lax.ppermute(value, "blk", [(i, even_partner(i)) for i in range(count)])


def both_chips(value, partner_of):
    count, rows = lax.axis_size("blk"), lax.axis_size("rows")
    pairs = []
    for i in range(count):
        for row in range(rows):
            chip, core = row // 2, row % 2
            pairs.append((i * rows + row, partner_of(i) * rows + core * 2 + chip))
    mine = lax.ppermute(value, ("blk", "rows"), pairs)
    return mine, flipped(mine, 1)


def both_partners(value):
    count = lax.axis_size("blk")
    even = both_chips(value, even_partner)
    odd = both_chips(value, lambda i: odd_partner(i, count))
    return odd + even


def by_core(value):
    count, rows = lax.axis_size("blk"), lax.axis_size("rows")
    pairs = []
    for i in range(count):
        for row in range(rows):
            target = even_partner(i) if row % 2 else odd_partner(i, count)
            pairs.append((i * rows + row, target * rows + row))
    return lax.ppermute(value, ("blk", "rows"), pairs)


def flipped(value, bit):
    return lax.ppermute(value, "rows", [(i, i ^ bit) for i in range(lax.axis_size("rows"))])


def on_device(factor_cols, basis_cols, samples, pairing):
    width = factor_cols.shape[1]
    packed = factor_cols.shape[0] // 2
    sample_count = samples.shape[0]
    extra = sample_count // 2
    rounds, steps = pairing.shape[0], pairing.shape[1]
    piece = packed // PIECES
    final = lax.axis_size("blk") - 1

    gram = first_gram(factor_cols)
    paired = gram + flipped(gram, 1)
    pairing, paired = lax.optimization_barrier((pairing, paired))
    projected, partner, sign = call(
        project_body,
        (
            shape(sample_count, width),
            shape(rounds * steps, width, dtype=i32),
            shape(rounds * steps, width),
        ),
        [VMEM] * 3,
    )(samples, basis_cols, pairing.reshape(rounds * steps, width))
    turn = call(lambda *refs: first_solve_body(rounds, *refs), shape(width, width), [VMEM] * 4)(
        paired, flipped(paired, 2), partner, sign
    )
    pieces = [shape(piece + (extra if i == PIECES - 1 else 0), width) for i in range(PIECES)]
    sent = call(rotate_body, tuple(pieces + pieces), [VMEM] * 3)(factor_cols, projected, turn)
    to_odd, to_even = sent[:PIECES], sent[PIECES:]
    odd_once, even_once, odd_twice, even_twice = [], [], [], []
    for i in range(PIECES):
        even_once.append(via_even(to_even[i]))
        odd_once.append(via_odd(to_odd[i], True))
    for i in range(PIECES):
        odd_twice.append(via_odd(even_once[i], False))
        even_twice.append(via_even(odd_once[i]))
    gram = call(lambda *refs: second_gram_body(piece, *refs), shape(width, width), [VMEM] * (2 * PIECES))(
        *odd_once, *even_once
    )
    paired = gram + flipped(gram, 1)
    message = call(lambda *refs: second_solve_body(rounds, *refs), shape(width, width), [VMEM] * 4)(
        paired, flipped(paired, 2), partner, sign
    )
    message = by_core(message)
    message_other = flipped(message, 1)
    cross = call(
        lambda *refs: cross_body(piece, final, *refs),
        shape(width + 2 * sample_count, width),
        [VMEM] * (5 * PIECES),
    )(*odd_twice, *to_odd, *to_even, *even_twice, *even_once)
    whole = call(
        lambda *refs: combine_body(final, *refs), shape(width + sample_count, width), [VMEM] * 3
    )(cross, message, message_other)
    paired = whole + flipped(whole, 1)
    sums, squares = call(
        lambda *refs: last_solve_body(rounds, final, *refs),
        (shape(1, width), shape(1, width)),
        [VMEM] * 6,
    )(*both_partners(paired), partner, sign)
    return (sums.reshape(width), squares.reshape(width))


def solution(mesh):
    in_specs = (P("rows", "blk"), P("rows", "blk"), P(None, "rows"), P())
    out_specs = (P("blk"), P("blk"))
    return jax.shard_map(
        on_device, mesh=mesh, in_specs=in_specs, out_specs=out_specs, check_vma=False
    )
```

time: 702 us -> 103 us (0.15); the launches traced: 694 us -> 103 us
  waiting for transfers between devices: 270 us -> 33.4 us
  local copies, waits for them, and re-layouts: 191 us -> 3.19 us
  other arithmetic: 133 us -> 0.03 us
  matrix products: 57.1 us -> 0 us
  starting transfers between devices: 19.4 us -> 44.9 us
  Pallas kernels: 0 us -> 20.2 us
  between operations: 16.5 us -> 0.78 us
    gather x204 -> x0, local copies, waits for them, and re-layouts: 139 us -> none  [the longest x24 21.7 us: small_solve(): diag_first = settled[first_index, first_index]]
    psum x4 -> x0, waiting for transfers between devices: 138 us -> none  [the longest x3 101 us: on_device(): gram_total = lax.psum(gram_local, 'rows')]
    scatter x132 -> x0, other arithmetic: 118 us -> none  [the longest x24 21.5 us: small_solve(): turned.at[:, first_index]]
    ppermute x6 -> x15, waiting for transfers between devices: 132 us -> 33.4 us  [the longest x2 19.6 us: via_even(): lax.ppermute(value, 'blk', [(i, even_partner(i)) for i in range(count)])]
    dot_general x22 -> x0, matrix products: 57.1 us -> none  [the longest x9 18.4 us: cross_product(): lax.dot_general(left, right, (((0,), (0,)), ((), ())), precision=highest,...]
    ppermute x6 -> x15, starting transfers between devices: 19 us -> 44.9 us  [the longest x1 25.8 us: by_core(): return lax.ppermute(value, ('blk', 'rows'), pairs)]
    slice x55 -> x0, local copies, waits for them, and re-layouts: 25 us -> none  [the longest x1 7.87 us: on_device(): bottoms = carried[:, half_width:].reshape(packed_rows, pair_width)]
    pallas_call x0 -> x9, Pallas kernels: none -> 20.2 us  [the longest x1 4.17 us: on_device(): call(lambda *refs: last_solve_body(rounds, final, *refs), (shape(1, width...]
  transfers between devices with their start and end apart: 10 -> 15, of which waited for: 10 -> 9; matrix products, arithmetic and copies ran while one was open for 5% -> 0% of each run, Pallas kernels for 0% -> 9%
where the time goes in v2:
time: 103 us
  starting transfers between devices  44.9 us (44%)
  waiting for transfers between devices  33.4 us (32%)
  Pallas kernels  20.2 us (20%)
  local copies, waits for them, and re-layouts  3.19 us (3%)
    ppermute x1, starting transfers between devices, by_core(): return lax.ppermute(value, ('blk', 'rows'), pairs)  25.8 us
    ppermute x2, waiting for transfers between devices, via_even(): lax.ppermute(value, 'blk', [(i, even_partner(i)) for i in range(count)])  19.6 us
    ppermute x2, starting transfers between devices, via_odd(): lax.ppermute(value, 'blk', [pair for pair in pairs if closed or pair[0] !...  8.77 us
    ppermute x8, waiting for transfers between devices, flipped(): lax.ppermute(value, 'rows', [(i, i ^ bit) for i in range(lax.axis_size('r...  7.02 us
    ppermute x8, starting transfers between devices, flipped(): lax.ppermute(value, 'rows', [(i, i ^ bit) for i in range(lax.axis_size('r...  5.16 us
    ppermute x2, waiting for transfers between devices, both_chips(): mine = lax.ppermute(value, ('blk', 'rows'), pairs)  5.13 us
    ppermute x2, starting transfers between devices, both_chips(): mine = lax.ppermute(value, ('blk', 'rows'), pairs)  4.72 us
    pallas_call x1, Pallas kernels, on_device(): call(lambda *refs: last_solve_body(rounds, final, *refs), (shape(1, width...  4.17 us
  transfers between devices with their start and end apart: 15, of which 9 were waited for; matrix products, arithmetic and copies ran while one was open for 0% of the time, Pallas kernels for 9%

profile of v2, /device:TPU:33, one launch (start us, length us, event | category | flops | bytes accessed | tf_op | source)
XLA Modules:
  0.0 102.6 jit_solution(3510646315800328444)
XLA Ops:
  0.6 0.0 copy-start
  0.6 1.6 %copy-done = f32[4096,128]{1,0:T(8,128)S(1)} copy-done((f32[4096,128]{1,0:T(8,128)S(1)}, f32[4096,128]{1,0:T(8,128)}, u32[]{:S(2)}) %copy-start) | copy-done | bytes 2097176
  2.2 0.0 copy-start.2
  2.2 0.0 copy-start.4
  2.2 1.3 %shard_map.59 = f32[128,128]{1,0:T(8,128)S(1)} custom-call(f32[4096,128]{1,0:T(8,128)S(1)} %copy-done), custom_call_target="tpu_custom_call" | custom-call | tf_op jit(solution)/shard_map/pallas_call | solution.py:101
  3.5 0.8 collective-permute-start
  4.3 0.9 collective-permute-done
  5.2 1.4 %collective-permute-start.1 = (f32[128,128]{1,0:T(8,128)S(1)}, f32[128,128]{1,0:T(8,128)S(1)}, u32[]{:S(2)}, u32[]{:S(2)}) collective-permute-start(f32[128,128]{1,0:T(8,128)S(1)} %add.9.refs_0_), channel_id=1, source_target_pairs={{0,2},{1,3},{2,0},{3,1},{4,6},{5,7},{6,4},{7,5},{8,10},{9,11},{10,... | collective-permute-start | bytes 196616 | tf_op jit(solution)/shard_map/ppermute | solution.py:483
  6.6 0.0 copy-done.2
  6.6 0.0 copy-done.4
  6.6 0.0 copy-start.3
  6.6 1.6 %copy-done.3 = f32[4096,128]{1,0:T(8,128)S(1)} copy-done((f32[4096,128]{1,0:T(8,128)S(1)}, f32[4096,128]{1,0:T(8,128)}, u32[]{:S(2)}) %copy-start.3) | copy-done | bytes 2097176
  8.2 2.3 %shard_map.60 = (f32[128,128]{1,0:T(8,128)S(1)}, s32[24,128]{1,0:T(8,128)S(1)}, f32[24,128]{1,0:T(8,128)S(1)}) custom-call(f32[128,4096]{1,0:T(8,128)S(1)} %copy-done.2, f32[4096,128]{1,0:T(8,128)S(1)} %copy-done.3, s32[24,128]{1,0:T(8,128)S(1)} %bitcast.3), custom_call_target="tpu_custom_call" | custom-call | tf_op jit(solution)/shard_map/pallas_call | solution.py:498
  10.5 0.0 collective-permute-done.1.refs_1_
  10.5 2.8 %shard_map.61.turn_ref = f32[128,128]{1,0:T(8,128)S(1)} custom-call(f32[128,128]{1,0:T(8,128)S(1)} %add.9.refs_0_, f32[128,128]{1,0:T(8,128)S(1)} %collective-permute-done.1.refs_1_, s32[24,128]{1,0:T(8,128)S(1)} %get-tuple-element.14.refs_2_.refs_4_, f32[24,128]{1,0:T(8,128)S(1)} %get-tuple-element.15.refs_3_.refs_5_), custom_call_target="tpu_custom_call" | custom-call | tf_op jit(solution)/shard_map/pallas_call | solution.py:507
  13.4 0.0 copy-done.1
  13.4 1.8 %shard_map.62 = (f32[2112,128]{1,0:T(8,128)S(1)}, f32[2112,128]{1,0:T(8,128)S(1)}) custom-call(f32[4096,128]{1,0:T(8,128)S(1)} %copy-done.1, f32[128,128]{1,0:T(8,128)S(1)} %get-tuple-element.12.projected_ref, f32[128,128]{1,0:T(8,128)S(1)} %shard_map.61.turn_ref), custom_call_target="tpu_custom_call" | custom-call | tf_op jit(solution)/shard_map/pallas_call | solution.py:511
  15.2 0.4 collective-permute-start.2
  15.6 4.9 %collective-permute-start.4 = (f32[2112,128]{1,0:T(8,128)S(1)}, f32[2112,128]{1,0:T(8,128)S(1)}, u32[]{:S(2)}, u32[]{:S(2)}) collective-permute-start(f32[2112,128]{1,0:T(8,128)S(1)} %get-tuple-element.17.refs_1_), channel_id=1, source_target_pairs={{0,0},{4,8},{8,4},{12,16},{16,12},{20,24},{24,20},{28,32},{32,28},... | collective-permute-start | bytes 3244040 | tf_op jit(solution)/shard_map/ppermute | solution.py:446
  20.5 19.6 %collective-permute-done.2.refs_4_.refs_1_ = f32[2112,128]{1,0:T(8,128)S(1)} collective-permute-done((f32[2112,128]{1,0:T(8,128)S(1)}, f32[2112,128]{1,0:T(8,128)S(1)}, u32[]{:S(2)}, u32[]{:S(2)}) %collective-permute-start.2) | collective-permute-done | bytes 1081376 | tf_op jit(solution)/shard_map/ppermute | solution.py:451
  40.1 3.9 %collective-permute-start.3 = (f32[2112,128]{1,0:T(8,128)S(1)}, f32[2112,128]{1,0:T(8,128)S(1)}, u32[]{:S(2)}, u32[]{:S(2)}) collective-permute-start(f32[2112,128]{1,0:T(8,128)S(1)} %collective-permute-done.2.refs_4_.refs_1_), channel_id=1, source_target_pairs={{4,8},{8,4},{12,16},{16,12},{20,24},{24,20},{28,32},{32,28},{36,40... | collective-permute-start | bytes 3244040 | tf_op jit(solution)/shard_map/ppermute | solution.py:446
  44.0 0.0 collective-permute-done.4.refs_0_
  44.0 0.1 collective-permute-start.5
  44.1 1.8 %shard_map.64 = f32[128,128]{1,0:T(8,128)S(1)} custom-call(f32[2112,128]{1,0:T(8,128)S(1)} %collective-permute-done.4.refs_0_, f32[2112,128]{1,0:T(8,128)S(1)} %collective-permute-done.2.refs_4_.refs_1_), custom_call_target="tpu_custom_call" | custom-call | tf_op jit(solution)/shard_map/pallas_call | solution.py:520
  45.9 1.7 %collective-permute-start.6 = (f32[128,128]{1,0:T(8,128)S(1)}, f32[128,128]{1,0:T(8,128)S(1)}, u32[]{:S(2)}, u32[]{:S(2)}) collective-permute-start(f32[128,128]{1,0:T(8,128)S(1)} %shard_map.64), channel_id=1, source_target_pairs={{0,1},{1,0},{2,3},{3,2},{4,5},{5,4},{6,7},{7,6},{8,9},{9,8},{10,11... | collective-permute-start | bytes 196616 | tf_op jit(solution)/shard_map/ppermute | solution.py:483
  47.6 0.9 collective-permute-done.6
  48.5 0.3 collective-permute-start.7
  48.7 3.2 %collective-permute-done.7.refs_1_ = f32[128,128]{1,0:T(8,128)S(1)} collective-permute-done((f32[128,128]{1,0:T(8,128)S(1)}, f32[128,128]{1,0:T(8,128)S(1)}, u32[]{:S(2)}, u32[]{:S(2)}) %collective-permute-start.7) | collective-permute-done | bytes 65568 | tf_op jit(solution)/shard_map/ppermute | solution.py:483
  52.0 3.2 %shard_map.65 = f32[128,128]{1,0:T(8,128)S(1)} custom-call(f32[128,128]{1,0:T(8,128)S(1)} %add.10.refs_0_, f32[128,128]{1,0:T(8,128)S(1)} %collective-permute-done.7.refs_1_, s32[24,128]{1,0:T(8,128)S(1)} %get-tuple-element.14.refs_2_.refs_4_, f32[24,128]{1,0:T(8,128)S(1)} %get-tuple-element.15.refs_3_.refs_5_), custom_call_target="tpu_custom_call" | custom-call | tf_op jit(solution)/shard_map/pallas_call | solution.py:524
  55.2 25.8 %collective-permute-start.8 = (f32[128,128]{1,0:T(8,128)S(1)}, f32[128,128]{1,0:T(8,128)S(1)}, u32[]{:S(2)}, u32[]{:S(2)}) collective-permute-start(f32[128,128]{1,0:T(8,128)S(1)} %shard_map.65), channel_id=1, source_target_pairs={{0,0},{1,5},{2,2},{3,7},{4,8},{5,1},{6,10},{7,3},{8,4},{9,13},{10,... | collective-permute-start | bytes 196616 | tf_op jit(solution)/shard_map/ppermute | solution.py:479
  81.0 1.6 %collective-permute-done.8.refs_1_ = f32[128,128]{1,0:T(8,128)S(1)} collective-permute-done((f32[128,128]{1,0:T(8,128)S(1)}, f32[128,128]{1,0:T(8,128)S(1)}, u32[]{:S(2)}, u32[]{:S(2)}) %collective-permute-start.8) | collective-permute-done | bytes 65568 | tf_op jit(solution)/shard_map/ppermute | solution.py:479
  82.6 0.0 collective-permute-start.9
  82.6 0.0 collective-permute-done.3.refs_0_
  82.6 0.0 collective-permute-done.5.refs_3_
  82.7 2.1 %shard_map.63.refs_0_ = f32[384,128]{1,0:T(8,128)S(1)} custom-call(f32[2112,128]{1,0:T(8,128)S(1)} %collective-permute-done.3.refs_0_, f32[2112,128]{1,0:T(8,128)S(1)} %get-tuple-element.17.refs_1_, f32[2112,128]{1,0:T(8,128)S(1)} %get-tuple-element.16.refs_2_, f32[2112,128]{1,0:T(8,128)S(1)} %collective-permute-done.5.refs_3_, ...), custom_call_target="tpu_custom_call" | custom-call | tf_op jit(solution)/shard_map/pallas_call | solution.py:529
  84.7 0.0 collective-permute-done.9.refs_2_
  84.7 0.7 shard_map.66
  85.5 0.6 collective-permute-start.10
  86.0 1.0 collective-permute-done.10
  87.0 2.8 %collective-permute-start.13 = (f32[256,128]{1,0:T(8,128)S(1)}, f32[256,128]{1,0:T(8,128)S(1)}, u32[]{:S(2)}, u32[]{:S(2)}) collective-permute-start(f32[256,128]{1,0:T(8,128)S(1)} %add.11), channel_id=1, source_target_pairs={{0,4},{1,6},{2,5},{3,7},{4,0},{5,2},{6,1},{7,3},{8,12},{9,14},{10,... | collective-permute-start | bytes 393224 | tf_op jit(solution)/shard_map/ppermute | solution.py:461
  89.9 1.9 %collective-permute-start.11 = (f32[256,128]{1,0:T(8,128)S(1)}, f32[256,128]{1,0:T(8,128)S(1)}, u32[]{:S(2)}, u32[]{:S(2)}) collective-permute-start(f32[256,128]{1,0:T(8,128)S(1)} %add.11), channel_id=1, source_target_pairs={{0,0},{1,2},{2,1},{3,3},{4,8},{5,10},{6,9},{7,11},{8,4},{9,6},{10,... | collective-permute-start | bytes 393224 | tf_op jit(solution)/shard_map/ppermute | solution.py:461
  91.8 1.6 %collective-permute-done.13.refs_2_ = f32[256,128]{1,0:T(8,128)S(1)} collective-permute-done((f32[256,128]{1,0:T(8,128)S(1)}, f32[256,128]{1,0:T(8,128)S(1)}, u32[]{:S(2)}, u32[]{:S(2)}) %collective-permute-start.13) | collective-permute-done | bytes 131104 | tf_op jit(solution)/shard_map/ppermute | solution.py:461
  93.4 0.1 collective-permute-start.14
  93.5 3.5 %collective-permute-done.11.refs_0_ = f32[256,128]{1,0:T(8,128)S(1)} collective-permute-done((f32[256,128]{1,0:T(8,128)S(1)}, f32[256,128]{1,0:T(8,128)S(1)}, u32[]{:S(2)}, u32[]{:S(2)}) %collective-permute-start.11) | collective-permute-done | bytes 131104 | tf_op jit(solution)/shard_map/ppermute | solution.py:461
  97.0 0.4 collective-permute-start.12
  97.4 0.0 collective-permute-done.14.refs_3_
  97.4 1.0 collective-permute-done.12.refs_1_
  98.4 4.2 %shard_map.67 = (f32[1,128]{1,0:T(1,128)}, f32[1,128]{1,0:T(1,128)}) custom-call(f32[256,128]{1,0:T(8,128)S(1)} %collective-permute-done.11.refs_0_, f32[256,128]{1,0:T(8,128)S(1)} %collective-permute-done.12.refs_1_, f32[256,128]{1,0:T(8,128)S(1)} %collective-permute-done.13.refs_2_, f32[256,128]{1,0:T(8,128)S(1)} %collective-permute-done.14.refs_3_, ...), custom_call_target="tpu_custom_call" | custom-call | tf_op jit(solution)/shard_map/pallas_call | solution.py:538
  (4 shorter events, 0.0 us)
Async XLA Ops:
  0.6 1.6 %copy-start = (f32[4096,128]{1,0:T(8,128)S(1)}, f32[4096,128]{1,0:T(8,128)}, u32[]{:S(2)}) copy-start(f32[4096,128]{1,0:T(8,128)} %factor_ref.3) | copy-start | bytes 6291460
  2.2 4.4 %copy-start.2 = (f32[128,4096]{1,0:T(8,128)S(1)}, f32[128,4096]{1,0:T(8,128)}, u32[]{:S(2)}) copy-start(f32[128,4096]{1,0:T(8,128)} %samples_ref.1) | copy-start | bytes 6291460
  2.2 4.4 %copy-start.4 = (s32[3,8,128]{2,1,0:T(8,128)S(1)}, s32[3,8,128]{2,1,0:T(8,128)}, u32[]{:S(2)}) copy-start(s32[3,8,128]{2,1,0:T(8,128)} %param.7) | copy-start | bytes 36868
  3.5 1.7 %collective-permute-start = (f32[128,128]{1,0:T(8,128)S(1)}, f32[128,128]{1,0:T(8,128)S(1)}, u32[]{:S(2)}, u32[]{:S(2)}) collective-permute-start(f32[128,128]{1,0:T(8,128)S(1)} %shard_map.59), channel_id=1, source_target_pairs={{0,1},{1,0},{2,3},{3,2},{4,5},{5,4},{6,7},{7,6},{8,9},{9,8},{10,11... | collective-permute-start | bytes 196616 | tf_op jit(solution)/shard_map/ppermute | solution.py:483
  5.2 5.3 %collective-permute-start.1 = (f32[128,128]{1,0:T(8,128)S(1)}, f32[128,128]{1,0:T(8,128)S(1)}, u32[]{:S(2)}, u32[]{:S(2)}) collective-permute-start(f32[128,128]{1,0:T(8,128)S(1)} %add.9.refs_0_), channel_id=1, source_target_pairs={{0,2},{1,3},{2,0},{3,1},{4,6},{5,7},{6,4},{7,5},{8,10},{9,11},{10,... | collective-permute-start | bytes 196616 | tf_op jit(solution)/shard_map/ppermute | solution.py:483
  6.6 1.6 %copy-start.3 = (f32[4096,128]{1,0:T(8,128)S(1)}, f32[4096,128]{1,0:T(8,128)}, u32[]{:S(2)}) copy-start(f32[4096,128]{1,0:T(8,128)} %basis_ref.1) | copy-start | bytes 6291460
  8.2 5.2 %copy-start.1 = (f32[4096,128]{1,0:T(8,128)S(1)}, f32[4096,128]{1,0:T(8,128)}, u32[]{:S(2)}) copy-start(f32[4096,128]{1,0:T(8,128)} %factor_ref.3) | copy-start | bytes 6291460
  15.2 24.9 %collective-permute-start.2 = (f32[2112,128]{1,0:T(8,128)S(1)}, f32[2112,128]{1,0:T(8,128)S(1)}, u32[]{:S(2)}, u32[]{:S(2)}) collective-permute-start(f32[2112,128]{1,0:T(8,128)S(1)} %get-tuple-element.16.refs_2_), channel_id=1, source_target_pairs={{0,4},{4,0},{8,12},{12,8},{16,20},{20,16},{24,28},{28,24},{32,36},... | collective-permute-start | bytes 3244040 | tf_op jit(solution)/shard_map/ppermute | solution.py:451
  15.6 28.4 %collective-permute-start.4 = (f32[2112,128]{1,0:T(8,128)S(1)}, f32[2112,128]{1,0:T(8,128)S(1)}, u32[]{:S(2)}, u32[]{:S(2)}) collective-permute-start(f32[2112,128]{1,0:T(8,128)S(1)} %get-tuple-element.17.refs_1_), channel_id=1, source_target_pairs={{0,0},{4,8},{8,4},{12,16},{16,12},{20,24},{24,20},{28,32},{32,28},... | collective-permute-start | bytes 3244040 | tf_op jit(solution)/shard_map/ppermute | solution.py:446
  40.1 42.6 %collective-permute-start.3 = (f32[2112,128]{1,0:T(8,128)S(1)}, f32[2112,128]{1,0:T(8,128)S(1)}, u32[]{:S(2)}, u32[]{:S(2)}) collective-permute-start(f32[2112,128]{1,0:T(8,128)S(1)} %collective-permute-done.2.refs_4_.refs_1_), channel_id=1, source_target_pairs={{4,8},{8,4},{12,16},{16,12},{20,24},{24,20},{28,32},{32,28},{36,40... | collective-permute-start | bytes 3244040 | tf_op jit(solution)/shard_map/ppermute | solution.py:446
  44.0 38.7 %collective-permute-start.5 = (f32[2112,128]{1,0:T(8,128)S(1)}, f32[2112,128]{1,0:T(8,128)S(1)}, u32[]{:S(2)}, u32[]{:S(2)}) collective-permute-start(f32[2112,128]{1,0:T(8,128)S(1)} %collective-permute-done.4.refs_0_), channel_id=1, source_target_pairs={{0,4},{4,0},{8,12},{12,8},{16,20},{20,16},{24,28},{28,24},{32,36},... | collective-permute-start | bytes 3244040 | tf_op jit(solution)/shard_map/ppermute | solution.py:451
  45.9 2.6 %collective-permute-start.6 = (f32[128,128]{1,0:T(8,128)S(1)}, f32[128,128]{1,0:T(8,128)S(1)}, u32[]{:S(2)}, u32[]{:S(2)}) collective-permute-start(f32[128,128]{1,0:T(8,128)S(1)} %shard_map.64), channel_id=1, source_target_pairs={{0,1},{1,0},{2,3},{3,2},{4,5},{5,4},{6,7},{7,6},{8,9},{9,8},{10,11... | collective-permute-start | bytes 196616 | tf_op jit(solution)/shard_map/ppermute | solution.py:483
  48.5 3.5 %collective-permute-start.7 = (f32[128,128]{1,0:T(8,128)S(1)}, f32[128,128]{1,0:T(8,128)S(1)}, u32[]{:S(2)}, u32[]{:S(2)}) collective-permute-start(f32[128,128]{1,0:T(8,128)S(1)} %add.10.refs_0_), channel_id=1, source_target_pairs={{0,2},{1,3},{2,0},{3,1},{4,6},{5,7},{6,4},{7,5},{8,10},{9,11},{10,... | collective-permute-start | bytes 196616 | tf_op jit(solution)/shard_map/ppermute | solution.py:483
  55.2 27.4 %collective-permute-start.8 = (f32[128,128]{1,0:T(8,128)S(1)}, f32[128,128]{1,0:T(8,128)S(1)}, u32[]{:S(2)}, u32[]{:S(2)}) collective-permute-start(f32[128,128]{1,0:T(8,128)S(1)} %shard_map.65), channel_id=1, source_target_pairs={{0,0},{1,5},{2,2},{3,7},{4,8},{5,1},{6,10},{7,3},{8,4},{9,13},{10,... | collective-permute-start | bytes 196616 | tf_op jit(solution)/shard_map/ppermute | solution.py:479
  82.6 2.1 %collective-permute-start.9 = (f32[128,128]{1,0:T(8,128)S(1)}, f32[128,128]{1,0:T(8,128)S(1)}, u32[]{:S(2)}, u32[]{:S(2)}) collective-permute-start(f32[128,128]{1,0:T(8,128)S(1)} %collective-permute-done.8.refs_1_), channel_id=1, source_target_pairs={{0,1},{1,0},{2,3},{3,2},{4,5},{5,4},{6,7},{7,6},{8,9},{9,8},{10,11... | collective-permute-start | bytes 196616 | tf_op jit(solution)/shard_map/ppermute | solution.py:483
  85.5 1.6 %collective-permute-start.10 = (f32[256,128]{1,0:T(8,128)S(1)}, f32[256,128]{1,0:T(8,128)S(1)}, u32[]{:S(2)}, u32[]{:S(2)}) collective-permute-start(f32[256,128]{1,0:T(8,128)S(1)} %shard_map.66), channel_id=1, source_target_pairs={{0,1},{1,0},{2,3},{3,2},{4,5},{5,4},{6,7},{7,6},{8,9},{9,8},{10,11... | collective-permute-start | bytes 393224 | tf_op jit(solution)/shard_map/ppermute | solution.py:483
  87.0 6.3 %collective-permute-start.13 = (f32[256,128]{1,0:T(8,128)S(1)}, f32[256,128]{1,0:T(8,128)S(1)}, u32[]{:S(2)}, u32[]{:S(2)}) collective-permute-start(f32[256,128]{1,0:T(8,128)S(1)} %add.11), channel_id=1, source_target_pairs={{0,4},{1,6},{2,5},{3,7},{4,0},{5,2},{6,1},{7,3},{8,12},{9,14},{10,... | collective-permute-start | bytes 393224 | tf_op jit(solution)/shard_map/ppermute | solution.py:461
  89.9 7.2 %collective-permute-start.11 = (f32[256,128]{1,0:T(8,128)S(1)}, f32[256,128]{1,0:T(8,128)S(1)}, u32[]{:S(2)}, u32[]{:S(2)}) collective-permute-start(f32[256,128]{1,0:T(8,128)S(1)} %add.11), channel_id=1, source_target_pairs={{0,0},{1,2},{2,1},{3,3},{4,8},{5,10},{6,9},{7,11},{8,4},{9,6},{10,... | collective-permute-start | bytes 393224 | tf_op jit(solution)/shard_map/ppermute | solution.py:461
  93.4 4.0 %collective-permute-start.14 = (f32[256,128]{1,0:T(8,128)S(1)}, f32[256,128]{1,0:T(8,128)S(1)}, u32[]{:S(2)}, u32[]{:S(2)}) collective-permute-start(f32[256,128]{1,0:T(8,128)S(1)} %collective-permute-done.13.refs_2_), channel_id=1, source_target_pairs={{0,1},{1,0},{2,3},{3,2},{4,5},{5,4},{6,7},{7,6},{8,9},{9,8},{10,11... | collective-permute-start | bytes 393224 | tf_op jit(solution)/shard_map/ppermute | solution.py:483
  97.0 1.4 %collective-permute-start.12 = (f32[256,128]{1,0:T(8,128)S(1)}, f32[256,128]{1,0:T(8,128)S(1)}, u32[]{:S(2)}, u32[]{:S(2)}) collective-permute-start(f32[256,128]{1,0:T(8,128)S(1)} %collective-permute-done.11.refs_0_), channel_id=1, source_target_pairs={{0,1},{1,0},{2,3},{3,2},{4,5},{5,4},{6,7},{7,6},{8,9},{9,8},{10,11... | collective-permute-start | bytes 393224 | tf_op jit(solution)/shard_map/ppermute | solution.py:483

commit v3 on v2

--- a/solution.py
+++ b/solution.py
@@ -10,6 +10,7 @@
 i32 = jnp.int32
 VMEM = pl.BlockSpec(memory_space=pltpu.VMEM)
 params = pltpu.CompilerParams(vmem_limit_bytes=24 * 1024 * 1024)
+large_params = pltpu.CompilerParams(vmem_limit_bytes=52 * 1024 * 1024)
 PIECES = 1
 
 
@@ -74,53 +75,74 @@
     return jnp.concatenate([value[:, half:], value[:, :half]], 1)
 
 
-def first_gram_body(factor_ref, out_ref, total_ref):
+def fetches(source, target, sems, first, cut):
+    count, size = chunks_of(target.shape[cut], 1024)
+    copies = []
+    for i in range(count):
+        part = (slice(None),) * cut + (pl.ds(i * size, size),)
+        copies.append(pltpu.make_async_copy(source.at[part], target.at[part], sems.at[first + i]))
+    return copies, size
+
+
+def tall(value):
+    quarter = value.shape[0] // 2
+    return jnp.concatenate([value[:quarter], value[quarter:]], 1)
+
+
+def square(value):
+    half = value.shape[1] // 2
+    return jnp.concatenate([value[:, :half], value[:, half:]], 0)
+
+
+def packed_gram(gram):
+    half = gram.shape[0] // 2
+    return jnp.concatenate([gram[:half], tall(gram[half:, half:])], 0)
+
+
+def unpacked_gram(value):
+    half = value.shape[1] // 2
+    across = value[:half, half:]
+    return jnp.concatenate(
+        [value[:half], jnp.concatenate([across.T, square(value[half:])], 1)], 0
+    )
+
+
+def first_gram_body(factor_hbm, out_ref, factor_ref, sems):
     width = factor_ref.shape[1]
-    step = pl.program_id(0)
-    high, low = split(factor_ref[...])
-    part = dot_rows(high, jnp.concatenate([high, low], 1))
-
-    @pl.when(step == 0)
-    def _():
-        total_ref[...] = part
-
-    @pl.when(step > 0)
-    def _():
-        total_ref[...] += part
-
-    @pl.when(step == pl.num_programs(0) - 1)
-    def _():
-        total = total_ref[...]
-        cross = total[:, width:]
-        out_ref[...] = total[:, :width] + (cross + cross.T)
+    copies, size = fetches(factor_hbm, factor_ref, sems, 0, 0)
+    for copy in copies:
+        copy.start()
+    total = jnp.zeros((width, 2 * width), f32)
+    for i, copy in enumerate(copies):
+        copy.wait()
+        high, low = split(factor_ref[i * size : (i + 1) * size, :])
+        total += dot_rows(high, jnp.concatenate([high, low], 1))
+    cross = total[:, width:]
+    out_ref[...] = packed_gram(total[:, :width] + (cross + cross.T))
 
 
 def first_gram(factor_cols):
     rows, width = factor_cols.shape
-    count, size = chunks_of(rows, 1024)
     return pl.pallas_call(
         first_gram_body,
-        out_shape=shape(width, width),
-        grid=(count,),
-        in_specs=[pl.BlockSpec((size, width), lambda i: (i, 0))],
-        out_specs=pl.BlockSpec((width, width), lambda i: (0, 0)),
-        scratch_shapes=[pltpu.VMEM((width, 2 * width), f32)],
-        compiler_params=params,
+        out_shape=shape(width * 3 // 4, width),
+        in_specs=[pl.BlockSpec(memory_space=pl.ANY)],
+        out_specs=VMEM,
+        scratch_shapes=[
+            pltpu.VMEM((rows, width), f32),
+            pltpu.SemaphoreType.DMA((chunks_of(rows, 1024)[0],)),
+        ],
+        compiler_params=large_params,
     )(factor_cols)
 
 
-def project_body(samples_ref, basis_ref, order_ref, out_ref, partner_ref, sign_ref):
+def project_body(samples_hbm, basis_hbm, order_ref, out_ref, partner_ref, sign_ref, samples_ref, basis_ref, sems):
     width = basis_ref.shape[1]
-    count, size = chunks_of(basis_ref.shape[0], 1024)
-
-    def step(i, total):
-        rows = rows_at(i, size)
-        left_high, left_low = split(samples_ref[:, rows])
-        right_high, right_low = split(basis_ref[rows, :])
-        both = dot(left_high, jnp.concatenate([right_high, right_low], 1))
-        return total + both[:, :width] + both[:, width:] + dot(left_low, right_high)
-
-    out_ref[...] = lax.fori_loop(0, count, step, jnp.zeros(out_ref.shape, f32))
+    lefts, size = fetches(samples_hbm, samples_ref, sems, 0, 1)
+    rights, size = fetches(basis_hbm, basis_ref, sems, len(lefts), 0)
+    for left, right in zip(lefts, rights):
+        left.start()
+        right.start()
 
     lines = order_ref.shape[0]
     order = order_ref[...]
@@ -142,6 +164,37 @@
     partner_ref[...] = jnp.where(first, found, found - width)
     sign_ref[...] = jnp.where(first, 1.0, -1.0).astype(f32)
 
+    total = jnp.zeros(out_ref.shape, f32)
+    for i, (left, right) in enumerate(zip(lefts, rights)):
+        left.wait()
+        right.wait()
+        left_high, left_low = split(samples_ref[:, i * size : (i + 1) * size])
+        right_high, right_low = split(basis_ref[i * size : (i + 1) * size, :])
+        both = dot(left_high, jnp.concatenate([right_high, right_low], 1))
+        total += both[:, :width] + both[:, width:] + dot(left_low, right_high)
+    out_ref[...] = total
+
+
+def project(samples, basis_cols, order):
+    rows, width = basis_cols.shape
+    lines = order.shape[0]
+    return pl.pallas_call(
+        project_body,
+        out_shape=(
+            shape(samples.shape[0], width),
+            shape(lines, width, dtype=i32),
+            shape(lines, width),
+        ),
+        in_specs=[pl.BlockSpec(memory_space=pl.ANY)] * 2 + [VMEM],
+        out_specs=(VMEM, VMEM, VMEM),
+        scratch_shapes=[
+            pltpu.VMEM(samples.shape, f32),
+            pltpu.VMEM((rows, width), f32),
+            pltpu.SemaphoreType.DMA((2 * chunks_of(rows, 1024)[0],)),
+        ],
+        compiler_params=large_params,
+    )(samples, basis_cols, order)
+
 
 def diagonal_of(value, eye):
     return jnp.sum(jnp.where(eye, value, 0.0), axis=0, keepdims=True)
@@ -157,7 +210,7 @@
     return row_id == col_id
 
 
-def turn_step(settled, carried, eye, index, sign):
+def turn_step(settled, carried, eye, index, sign, last):
     width = settled.shape[0]
     swapped = lanes(settled, index)
     own = diagonal_of(settled, eye)
@@ -169,29 +222,36 @@
     across = sign * (own - both[0:1])
     up = crossing + both[8:9]
     scale = jnp.maximum(jnp.abs(across), jnp.abs(up))
-    safe = jnp.where(scale > 0.0, scale, 1.0)
-    across = jnp.where(scale > 0.0, across / safe, 1.0)
-    up = up / safe
-    hypot = jnp.sqrt(across * across + up * up)
-    major = jnp.sqrt(0.5 + 0.5 * jnp.abs(across) / hypot)
-    minor = 0.5 * jnp.abs(up) / (hypot * major)
-    ahead = across >= 0.0
+    found = scale > 0.0
+    shrink = 1.0 / jnp.where(found, scale, 1.0)
+    level = jnp.where(found, across * shrink, 1.0)
+    slope = up * shrink
+    inverse = lax.rsqrt(level * level + slope * slope)
+    square = 0.5 + 0.5 * jnp.abs(level) * inverse
+    against = lax.rsqrt(square)
+    major = square * against
+    minor = 0.5 * jnp.abs(slope) * inverse * against
+    ahead = level >= 0.0
     cosine = jnp.where(ahead, major, minor)
     sine = jnp.where(ahead, minor, major)
-    sine = jnp.where(up < 0.0, -sine, sine) * sign
+    sine = jnp.where(slope < 0.0, -sine, sine) * sign
+    carried = carried * cosine + lanes(carried, index) * sine
+    if last == "turn":
+        return None, carried
+    if last == "sums":
+        return own * (cosine * cosine) + both[0:1] * (sine * sine) + up * (cosine * sine), carried
     turned = (settled * cosine + swapped * sine).T
-    settled = turned * cosine + lanes(turned, index) * sine
-    carried = carried * cosine + lanes(carried, index) * sine
-    return settled, carried
-
-
-def solve(problems, partners, signs):
+    return turned * cosine + lanes(turned, index) * sine, carried
+
+
+def solve(problems, partners, signs, last=None):
     width = problems[0][0].shape[0]
     eye = eye_of(width)
     for step in range(partners.shape[0]):
         sign = signs[step : step + 1, :]
         index = jnp.broadcast_to(partners[step : step + 1, :], (width, width))
-        problems = [turn_step(*problem, eye, index, sign) for problem in problems]
+        ending = last if step == partners.shape[0] - 1 else None
+        problems = [turn_step(*problem, eye, index, sign, ending) for problem in problems]
     return problems
 
 
@@ -224,11 +284,12 @@
 
 
 def first_solve_body(rounds, own_ref, other_ref, partner_ref, sign_ref, turn_ref):
-    gram = own_ref[...] + other_ref[...]
+    gram = unpacked_gram(own_ref[...] + other_ref[...])
     ((_, turn_ref[...]),) = solve(
         [(gram, identity_of(gram.shape[0]))],
         round_of(partner_ref, 0, rounds),
         round_of(sign_ref, 0, rounds),
+        "turn",
     )
 
 
@@ -302,20 +363,21 @@
         total = lax.fori_loop(0, count, step, total)
     cross = folded(total[:, width:])
     gram = folded(total[:, :width]) + (cross + cross.T)
-    out_ref[...] = jnp.where(blk_index() % 2 == 1, swapped_rows(swapped_cols(gram)), gram)
-
-
-def second_solve_body(rounds, own_ref, other_ref, partner_ref, sign_ref, out_ref):
-    gram = own_ref[...] + other_ref[...]
+    out_ref[...] = packed_gram(jnp.where(blk_index() % 2 == 1, swapped_rows(swapped_cols(gram)), gram))
+
+
+def second_solve_body(rounds, own_ref, other_ref, partner_ref, sign_ref, odd_ref, even_ref):
+    gram = unpacked_gram(own_ref[...] + other_ref[...])
     width = gram.shape[0]
     half = width // 2
     ((settled, turn),) = solve(
         [(gram, identity_of(width))], round_of(partner_ref, 1, rounds), round_of(sign_ref, 1, rounds)
     )
-    take_top = jnp.logical_xor(top_goes_odd(), lax.axis_index("rows") % 2 == 1)
-    out_ref[:, :half] = jnp.where(take_top, turn[:, :half], turn[:, half:])
-    out_ref[:half, half:] = jnp.where(take_top, settled[:half, :half], settled[half:, half:])
-    out_ref[half:, half:] = jnp.zeros((half, half), f32)
+    top = jnp.concatenate([tall(turn[:, :half]), tall(settled[:half, :half])], 0)
+    bottom = jnp.concatenate([tall(turn[:, half:]), tall(settled[half:, half:])], 0)
+    take_top = top_goes_odd()
+    odd_ref[...] = jnp.where(take_top, top, bottom)
+    even_ref[...] = jnp.where(take_top, bottom, top)
 
 
 def cross_body(piece, final, *refs):
@@ -365,43 +427,30 @@
         out_ref[start + extra : start + 2 * extra, half:] = value[:, width + half :]
 
 
-def combine_body(final, cross_ref, own_ref, other_ref, out_ref):
+def combine_body(final, cross_ref, odd_ref, even_ref, out_ref):
     width = cross_ref.shape[1]
     half = width // 2
     count = (cross_ref.shape[0] - width) // 2
     position = blk_index()
     odd = position % 2 == 1
     at_edge = jnp.logical_or(position == 0, position == final)
-    first_core = lax.axis_index("rows") % 2 == 0
-    from_odd = jnp.where(first_core, own_ref[...], other_ref[...])
-    from_even = jnp.where(first_core, other_ref[...], own_ref[...])
-    odd_turn, even_turn = from_odd[:, :half], from_even[:, :half]
+    odd_turn, even_turn = square(odd_ref[:half, :]), square(even_ref[:half, :])
     odd_turn = jnp.where(jnp.logical_xor(odd, at_edge), swapped_rows(odd_turn), odd_turn)
     even_turn = jnp.where(odd, swapped_rows(even_turn), even_turn)
     cross = dot_fine(dot_fine(odd_turn.T, cross_ref[:width, :]), even_turn)
-    cross_turned = cross.T
     share = 0.25
-    odd_gram = from_odd[:half, half:] * share
-    even_gram = from_even[:half, half:] * share
+    odd_gram = square(odd_ref[half:, :]) * share
+    even_gram = square(even_ref[half:, :]) * share
     odd_samples = dot_fine(cross_ref[width : width + count, :], odd_turn)
     even_samples = dot_fine(cross_ref[width + count :, :], even_turn)
-    straight = jnp.concatenate(
-        [
-            jnp.concatenate([odd_gram, cross], 1),
-            jnp.concatenate([cross_turned, even_gram], 1),
-            jnp.concatenate([odd_samples, even_samples], 1),
-        ],
-        0,
-    )
-    turned = jnp.concatenate(
-        [
-            jnp.concatenate([even_gram, cross_turned], 1),
-            jnp.concatenate([cross, odd_gram], 1),
-            jnp.concatenate([even_samples, odd_samples], 1),
-        ],
-        0,
-    )
-    out_ref[...] = jnp.where(odd, turned, straight)
+    first = jnp.where(odd, even_gram, odd_gram)
+    second = jnp.where(odd, odd_gram, even_gram)
+    cross = jnp.where(odd, cross.T, cross)
+    out_ref[:count, :half] = jnp.where(odd, even_samples, odd_samples)
+    out_ref[:count, half:] = jnp.where(odd, odd_samples, even_samples)
+    out_ref[count : count + half, :half] = first
+    out_ref[count : count + half, half:] = cross
+    out_ref[count + half :, :] = tall(second)
 
 
 def last_solve_body(
@@ -410,16 +459,16 @@
     wholes = [odd_ref[...] + odd_other_ref[...], even_ref[...] + even_other_ref[...]]
     width = wholes[0].shape[1]
     half = width // 2
-    samples = wholes[0].shape[0] - width
+    samples = wholes[0].shape[0] - width * 3 // 4
     solved = solve(
-        [(whole[:width], whole[width:]) for whole in wholes],
+        [(unpacked_gram(whole[samples:]), whole[:samples]) for whole in wholes],
         round_of(partner_ref, 2, rounds),
         round_of(sign_ref, 2, rounds),
+        "sums",
     )
     takes = [odd_takes_top(final), even_takes_top()]
     halves = []
-    for (settled, projected), take_top in zip(solved, takes):
-        sums = diagonal_of(settled, eye_of(width))
+    for (sums, projected), take_top in zip(solved, takes):
         squares = jnp.sum(projected * projected, axis=0, keepdims=True) * (1.0 / samples)
         both = jnp.concatenate([sums, squares], 0)
         halves.append(jnp.where(take_top, both[:, :half], both[:, half:]))
@@ -469,16 +518,6 @@
     return odd + even
 
 
-def by_core(value):
-    count, rows = lax.axis_size("blk"), lax.axis_size("rows")
-    pairs = []
-    for i in range(count):
-        for row in range(rows):
-            target = even_partner(i) if row % 2 else odd_partner(i, count)
-            pairs.append((i * rows + row, target * rows + row))
-    return lax.ppermute(value, ("blk", "rows"), pairs)
-
-
 def flipped(value, bit):
     return lax.ppermute(value, "rows", [(i, i ^ bit) for i in range(lax.axis_size("rows"))])
 
@@ -495,15 +534,7 @@
     gram = first_gram(factor_cols)
     paired = gram + flipped(gram, 1)
     pairing, paired = lax.optimization_barrier((pairing, paired))
-    projected, partner, sign = call(
-        project_body,
-        (
-            shape(sample_count, width),
-            shape(rounds * steps, width, dtype=i32),
-            shape(rounds * steps, width),
-        ),
-        [VMEM] * 3,
-    )(samples, basis_cols, pairing.reshape(rounds * steps, width))
+    projected, partner, sign = project(samples, basis_cols, pairing.reshape(rounds * steps, width))
     turn = call(lambda *refs: first_solve_body(rounds, *refs), shape(width, width), [VMEM] * 4)(
         paired, flipped(paired, 2), partner, sign
     )
@@ -517,23 +548,25 @@
     for i in range(PIECES):
         odd_twice.append(via_odd(even_once[i], False))
         even_twice.append(via_even(odd_once[i]))
-    gram = call(lambda *refs: second_gram_body(piece, *refs), shape(width, width), [VMEM] * (2 * PIECES))(
+    gram = call(lambda *refs: second_gram_body(piece, *refs), shape(width * 3 // 4, width), [VMEM] * (2 * PIECES))(
         *odd_once, *even_once
     )
     paired = gram + flipped(gram, 1)
-    message = call(lambda *refs: second_solve_body(rounds, *refs), shape(width, width), [VMEM] * 4)(
-        paired, flipped(paired, 2), partner, sign
-    )
-    message = by_core(message)
-    message_other = flipped(message, 1)
+    for_odd, for_even = call(
+        lambda *refs: second_solve_body(rounds, *refs),
+        (shape(width * 3 // 4, width), shape(width * 3 // 4, width)),
+        [VMEM] * 4,
+    )(paired, flipped(paired, 2), partner, sign)
+    from_even = via_even(for_even)
+    from_odd = via_odd(for_odd, True)
     cross = call(
         lambda *refs: cross_body(piece, final, *refs),
         shape(width + 2 * sample_count, width),
         [VMEM] * (5 * PIECES),
     )(*odd_twice, *to_odd, *to_even, *even_twice, *even_once)
     whole = call(
-        lambda *refs: combine_body(final, *refs), shape(width + sample_count, width), [VMEM] * 3
-    )(cross, message, message_other)
+        lambda *refs: combine_body(final, *refs), shape(width * 3 // 4 + sample_count, width), [VMEM] * 3
+    )(cross, from_odd, from_even)
     paired = whole + flipped(whole, 1)
     sums, squares = call(
         lambda *refs: last_solve_body(rounds, final, *refs),

time: 103 us -> 98 us (0.951)
  local copies, waits for them, and re-layouts: 3.19 us -> 0.01 us
  waiting for transfers between devices: 33.4 us -> 31.4 us
    ppermute x1 -> x0, starting transfers between devices: 25.8 us -> none  [by_core(): return lax.ppermute(value, ('blk', 'rows'), pairs)]
    ppermute x2 -> x3, starting transfers between devices: 0.47 us -> 18.3 us  [via_even(): lax.ppermute(value, 'blk', [(i, even_partner(i)) for i in range(count)])]
    ppermute x2 -> x3, starting transfers between devices: 8.77 us -> 15.1 us  [via_odd(): lax.ppermute(value, 'blk', [pair for pair in pairs if closed or pair[0] !...]
    unnamed x10 -> x4, local copies, waits for them, and re-layouts: 3.19 us -> 0.01 us
    ppermute x1 -> x0, waiting for transfers between devices: 1.64 us -> none  [by_core(): return lax.ppermute(value, ('blk', 'rows'), pairs)]
    pallas_call x5, Pallas kernels: 9.34 us -> 10.7 us  [the longest x1 3.1 us: on_device(): call(lambda *refs: second_solve_body(rounds, *refs), (shape(width * 3 //...]
    ppermute x2, starting transfers between devices: 4.72 us -> 5.91 us  [both_chips(): mine = lax.ppermute(value, ('blk', 'rows'), pairs)]
    ppermute x8 -> x7, waiting for transfers between devices: 7.02 us -> 6.85 us  [flipped(): lax.ppermute(value, 'rows', [(i, i ^ bit) for i in range(lax.axis_size('r...]
  transfers between devices with their start and end apart: 15 -> 15, of which waited for: 9 -> 8; matrix products, arithmetic and copies ran while one was open for 0% -> 0% of each run, Pallas kernels for 9% -> 10%
where the time goes in v3:
time: 98 us; the launch traced here: 97.7 us
  starting transfers between devices  44.3 us (45%)
  waiting for transfers between devices  31.4 us (32%)
  Pallas kernels  21.2 us (22%)
    ppermute x3, waiting for transfers between devices, via_even(): lax.ppermute(value, 'blk', [(i, even_partner(i)) for i in range(count)])  19.5 us
    ppermute x3, starting transfers between devices, via_even(): lax.ppermute(value, 'blk', [(i, even_partner(i)) for i in range(count)])  18.3 us
    ppermute x3, starting transfers between devices, via_odd(): lax.ppermute(value, 'blk', [pair for pair in pairs if closed or pair[0] !...  15.1 us
    ppermute x7, waiting for transfers between devices, flipped(): lax.ppermute(value, 'rows', [(i, i ^ bit) for i in range(lax.axis_size('r...  6.85 us
    ppermute x2, starting transfers between devices, both_chips(): mine = lax.ppermute(value, ('blk', 'rows'), pairs)  5.91 us
    ppermute x2, waiting for transfers between devices, both_chips(): mine = lax.ppermute(value, ('blk', 'rows'), pairs)  5.08 us
    ppermute x7, starting transfers between devices, flipped(): lax.ppermute(value, 'rows', [(i, i ^ bit) for i in range(lax.axis_size('r...  5.07 us
    pallas_call x1, Pallas kernels, on_device(): call(lambda *refs: last_solve_body(rounds, final, *refs), (shape(1, width...  3.75 us
  transfers between devices with their start and end apart: 15, of which 8 were waited for; matrix products, arithmetic and copies ran while one was open for 0% of the time, Pallas kernels for 10%

profile of v3, /device:TPU:33, one launch (start us, length us, event | category | flops | bytes accessed | tf_op | source)
XLA Modules:
  0.0 97.7 jit_solution(16894621799244165409)
XLA Ops:
  0.6 0.0 copy-start.1
  0.6 2.3 %shard_map.59 = f32[96,128]{1,0:T(8,128)S(1)} custom-call(f32[4096,128]{1,0:T(8,128)} %factor_ref.1), custom_call_target="tpu_custom_call" | custom-call | tf_op jit(solution)/shard_map/pallas_call | solution.py:126
  3.0 0.8 collective-permute-start
  3.7 0.9 collective-permute-done
  4.6 1.3 %collective-permute-start.1 = (f32[96,128]{1,0:T(8,128)S(1)}, f32[96,128]{1,0:T(8,128)S(1)}, u32[]{:S(2)}, u32[]{:S(2)}) collective-permute-start(f32[96,128]{1,0:T(8,128)S(1)} %add.9.refs_0_), channel_id=1, source_target_pairs={{0,2},{1,3},{2,0},{3,1},{4,6},{5,7},{6,4},{7,5},{8,10},{9,11},{10,... | collective-permute-start | bytes 147464 | tf_op jit(solution)/shard_map/ppermute | solution.py:522
  5.9 0.0 copy-done.1
  5.9 0.0 copy-start
  5.9 2.7 %shard_map.60 = (f32[128,128]{1,0:T(8,128)S(1)}, s32[24,128]{1,0:T(8,128)S(1)}, f32[24,128]{1,0:T(8,128)S(1)}) custom-call(f32[128,4096]{1,0:T(8,128)} %samples_hbm.1, f32[4096,128]{1,0:T(8,128)} %basis_hbm.1, s32[24,128]{1,0:T(8,128)S(1)} %bitcast.3), custom_call_target="tpu_custom_call" | custom-call | tf_op jit(solution)/shard_map/pallas_call | solution.py:181
  8.6 0.0 collective-permute-done.1.refs_1_
  8.6 2.9 %shard_map.61.turn_ref = f32[128,128]{1,0:T(8,128)S(1)} custom-call(f32[96,128]{1,0:T(8,128)S(1)} %add.9.refs_0_, f32[96,128]{1,0:T(8,128)S(1)} %collective-permute-done.1.refs_1_, s32[24,128]{1,0:T(8,128)S(1)} %get-tuple-element.16.refs_2_.refs_4_, f32[24,128]{1,0:T(8,128)S(1)} %get-tuple-element.17.refs_3_.refs_5_), custom_call_target="tpu_custom_call" | custom-call | tf_op jit(solution)/shard_map/pallas_call | solution.py:538
  11.5 0.0 copy-done
  11.5 1.8 %shard_map.62 = (f32[2112,128]{1,0:T(8,128)S(1)}, f32[2112,128]{1,0:T(8,128)S(1)}) custom-call(f32[4096,128]{1,0:T(8,128)S(1)} %copy-done, f32[128,128]{1,0:T(8,128)S(1)} %get-tuple-element.14.projected_ref, f32[128,128]{1,0:T(8,128)S(1)} %shard_map.61.turn_ref), custom_call_target="tpu_custom_call" | custom-call | tf_op jit(solution)/shard_map/pallas_call | solution.py:542
  13.3 0.6 collective-permute-start.2
  13.9 4.7 %collective-permute-start.4 = (f32[2112,128]{1,0:T(8,128)S(1)}, f32[2112,128]{1,0:T(8,128)S(1)}, u32[]{:S(2)}, u32[]{:S(2)}) collective-permute-start(f32[2112,128]{1,0:T(8,128)S(1)} %get-tuple-element.19.refs_1_), channel_id=1, source_target_pairs={{0,0},{4,8},{8,4},{12,16},{16,12},{20,24},{24,20},{28,32},{32,28},... | collective-permute-start | bytes 3244040 | tf_op jit(solution)/shard_map/ppermute | solution.py:495
  18.6 19.5 %collective-permute-done.2.refs_4_.refs_1_ = f32[2112,128]{1,0:T(8,128)S(1)} collective-permute-done((f32[2112,128]{1,0:T(8,128)S(1)}, f32[2112,128]{1,0:T(8,128)S(1)}, u32[]{:S(2)}, u32[]{:S(2)}) %collective-permute-start.2) | collective-permute-done | bytes 1081376 | tf_op jit(solution)/shard_map/ppermute | solution.py:500
  38.1 3.9 %collective-permute-start.3 = (f32[2112,128]{1,0:T(8,128)S(1)}, f32[2112,128]{1,0:T(8,128)S(1)}, u32[]{:S(2)}, u32[]{:S(2)}) collective-permute-start(f32[2112,128]{1,0:T(8,128)S(1)} %collective-permute-done.2.refs_4_.refs_1_), channel_id=1, source_target_pairs={{4,8},{8,4},{12,16},{16,12},{20,24},{24,20},{28,32},{32,28},{36,40... | collective-permute-start | bytes 3244040 | tf_op jit(solution)/shard_map/ppermute | solution.py:495
  42.0 0.0 collective-permute-done.4.refs_0_
  42.0 0.1 collective-permute-start.5
  42.1 1.9 %shard_map.64 = f32[96,128]{1,0:T(8,128)S(1)} custom-call(f32[2112,128]{1,0:T(8,128)S(1)} %collective-permute-done.4.refs_0_, f32[2112,128]{1,0:T(8,128)S(1)} %collective-permute-done.2.refs_4_.refs_1_), custom_call_target="tpu_custom_call" | custom-call | tf_op jit(solution)/shard_map/pallas_call | solution.py:551
  44.0 1.7 %collective-permute-start.6 = (f32[96,128]{1,0:T(8,128)S(1)}, f32[96,128]{1,0:T(8,128)S(1)}, u32[]{:S(2)}, u32[]{:S(2)}) collective-permute-start(f32[96,128]{1,0:T(8,128)S(1)} %shard_map.64), channel_id=1, source_target_pairs={{0,1},{1,0},{2,3},{3,2},{4,5},{5,4},{6,7},{7,6},{8,9},{9,8},{10,11... | collective-permute-start | bytes 147464 | tf_op jit(solution)/shard_map/ppermute | solution.py:522
  45.7 0.9 collective-permute-done.6
  46.6 0.4 collective-permute-start.7
  47.0 2.8 %collective-permute-done.7.refs_1_ = f32[96,128]{1,0:T(8,128)S(1)} collective-permute-done((f32[96,128]{1,0:T(8,128)S(1)}, f32[96,128]{1,0:T(8,128)S(1)}, u32[]{:S(2)}, u32[]{:S(2)}) %collective-permute-start.7) | collective-permute-done | bytes 49184 | tf_op jit(solution)/shard_map/ppermute | solution.py:522
  49.8 3.1 %shard_map.65 = (f32[96,128]{1,0:T(8,128)S(1)}, f32[96,128]{1,0:T(8,128)S(1)}) custom-call(f32[96,128]{1,0:T(8,128)S(1)} %add.10.refs_0_, f32[96,128]{1,0:T(8,128)S(1)} %collective-permute-done.7.refs_1_, s32[24,128]{1,0:T(8,128)S(1)} %get-tuple-element.16.refs_2_.refs_4_, f32[24,128]{1,0:T(8,128)S(1)} %get-tuple-element.17.refs_3_.refs_5_), custom_call_target="tpu_custom_call" | custom-call | tf_op jit(solution)/shard_map/pallas_call | solution.py:555
  52.9 6.5 %collective-permute-start.8 = (f32[96,128]{1,0:T(8,128)S(1)}, f32[96,128]{1,0:T(8,128)S(1)}, u32[]{:S(2)}, u32[]{:S(2)}) collective-permute-start(f32[96,128]{1,0:T(8,128)S(1)} %get-tuple-element.20), channel_id=1, source_target_pairs={{0,0},{4,8},{8,4},{12,16},{16,12},{20,24},{24,20},{28,32},{32,28},... | collective-permute-start | bytes 147464 | tf_op jit(solution)/shard_map/ppermute | solution.py:495
  59.4 17.6 %collective-permute-start.9 = (f32[96,128]{1,0:T(8,128)S(1)}, f32[96,128]{1,0:T(8,128)S(1)}, u32[]{:S(2)}, u32[]{:S(2)}) collective-permute-start(f32[96,128]{1,0:T(8,128)S(1)} %get-tuple-element.21), channel_id=1, source_target_pairs={{0,4},{4,0},{8,12},{12,8},{16,20},{20,16},{24,28},{28,24},{32,36},... | collective-permute-start | bytes 147464 | tf_op jit(solution)/shard_map/ppermute | solution.py:500
  77.0 0.0 collective-permute-done.3.refs_0_
  77.0 0.0 collective-permute-done.5.refs_3_
  77.0 2.0 %shard_map.63.refs_0_ = f32[384,128]{1,0:T(8,128)S(1)} custom-call(f32[2112,128]{1,0:T(8,128)S(1)} %collective-permute-done.3.refs_0_, f32[2112,128]{1,0:T(8,128)S(1)} %get-tuple-element.19.refs_1_, f32[2112,128]{1,0:T(8,128)S(1)} %get-tuple-element.18.refs_2_, f32[2112,128]{1,0:T(8,128)S(1)} %collective-permute-done.5.refs_3_, ...), custom_call_target="tpu_custom_call" | custom-call | tf_op jit(solution)/shard_map/pallas_call | solution.py:562
  79.1 0.0 collective-permute-done.8.refs_1_
  79.1 0.0 collective-permute-done.9.refs_2_
  79.1 0.7 shard_map.66
  79.8 0.8 collective-permute-start.10
  80.7 1.0 collective-permute-done.10
  81.7 4.0 %collective-permute-start.13 = (f32[224,128]{1,0:T(8,128)S(1)}, f32[224,128]{1,0:T(8,128)S(1)}, u32[]{:S(2)}, u32[]{:S(2)}) collective-permute-start(f32[224,128]{1,0:T(8,128)S(1)} %add.11), channel_id=1, source_target_pairs={{0,4},{1,6},{2,5},{3,7},{4,0},{5,2},{6,1},{7,3},{8,12},{9,14},{10,... | collective-permute-start | bytes 344072 | tf_op jit(solution)/shard_map/ppermute | solution.py:510
  85.7 1.9 %collective-permute-start.11 = (f32[224,128]{1,0:T(8,128)S(1)}, f32[224,128]{1,0:T(8,128)S(1)}, u32[]{:S(2)}, u32[]{:S(2)}) collective-permute-start(f32[224,128]{1,0:T(8,128)S(1)} %add.11), channel_id=1, source_target_pairs={{0,0},{1,2},{2,1},{3,3},{4,8},{5,10},{6,9},{7,11},{8,4},{9,6},{10,... | collective-permute-start | bytes 344072 | tf_op jit(solution)/shard_map/ppermute | solution.py:510
  87.6 1.2 %collective-permute-done.13.refs_2_ = f32[224,128]{1,0:T(8,128)S(1)} collective-permute-done((f32[224,128]{1,0:T(8,128)S(1)}, f32[224,128]{1,0:T(8,128)S(1)}, u32[]{:S(2)}, u32[]{:S(2)}) %collective-permute-start.13) | collective-permute-done | bytes 114720 | tf_op jit(solution)/shard_map/ppermute | solution.py:510
  88.8 0.0 collective-permute-start.14
  88.8 3.8 %collective-permute-done.11.refs_0_ = f32[224,128]{1,0:T(8,128)S(1)} collective-permute-done((f32[224,128]{1,0:T(8,128)S(1)}, f32[224,128]{1,0:T(8,128)S(1)}, u32[]{:S(2)}, u32[]{:S(2)}) %collective-permute-start.11) | collective-permute-done | bytes 114720 | tf_op jit(solution)/shard_map/ppermute | solution.py:510
  92.7 0.0 collective-permute-start.12
  92.7 0.0 collective-permute-done.14.refs_3_
  92.7 1.3 %collective-permute-done.12.refs_1_ = f32[224,128]{1,0:T(8,128)S(1)} collective-permute-done((f32[224,128]{1,0:T(8,128)S(1)}, f32[224,128]{1,0:T(8,128)S(1)}, u32[]{:S(2)}, u32[]{:S(2)}) %collective-permute-start.12) | collective-permute-done | bytes 114720 | tf_op jit(solution)/shard_map/ppermute | solution.py:522
  94.0 3.7 %shard_map.67 = (f32[1,128]{1,0:T(1,128)}, f32[1,128]{1,0:T(1,128)}) custom-call(f32[224,128]{1,0:T(8,128)S(1)} %collective-permute-done.11.refs_0_, f32[224,128]{1,0:T(8,128)S(1)} %collective-permute-done.12.refs_1_, f32[224,128]{1,0:T(8,128)S(1)} %collective-permute-done.13.refs_2_, f32[224,128]{1,0:T(8,128)S(1)} %collective-permute-done.14.refs_3_, ...), custom_call_target="tpu_custom_call" | custom-call | tf_op jit(solution)/shard_map/pallas_call | solution.py:571
  (3 shorter events, 0.0 us)
Async XLA Ops:
  0.6 5.3 %copy-start.1 = (s32[3,8,128]{2,1,0:T(8,128)S(1)}, s32[3,8,128]{2,1,0:T(8,128)}, u32[]{:S(2)}) copy-start(s32[3,8,128]{2,1,0:T(8,128)} %param.7) | copy-start | bytes 36868
  3.0 1.6 %collective-permute-start = (f32[96,128]{1,0:T(8,128)S(1)}, f32[96,128]{1,0:T(8,128)S(1)}, u32[]{:S(2)}, u32[]{:S(2)}) collective-permute-start(f32[96,128]{1,0:T(8,128)S(1)} %shard_map.59), channel_id=1, source_target_pairs={{0,1},{1,0},{2,3},{3,2},{4,5},{5,4},{6,7},{7,6},{8,9},{9,8},{10,11... | collective-permute-start | bytes 147464 | tf_op jit(solution)/shard_map/ppermute | solution.py:522
  4.6 4.0 %collective-permute-start.1 = (f32[96,128]{1,0:T(8,128)S(1)}, f32[96,128]{1,0:T(8,128)S(1)}, u32[]{:S(2)}, u32[]{:S(2)}) collective-permute-start(f32[96,128]{1,0:T(8,128)S(1)} %add.9.refs_0_), channel_id=1, source_target_pairs={{0,2},{1,3},{2,0},{3,1},{4,6},{5,7},{6,4},{7,5},{8,10},{9,11},{10,... | collective-permute-start | bytes 147464 | tf_op jit(solution)/shard_map/ppermute | solution.py:522
  5.9 5.6 %copy-start = (f32[4096,128]{1,0:T(8,128)S(1)}, f32[4096,128]{1,0:T(8,128)}, u32[]{:S(2)}) copy-start(f32[4096,128]{1,0:T(8,128)} %factor_ref.1) | copy-start | bytes 6291460
  13.3 24.8 %collective-permute-start.2 = (f32[2112,128]{1,0:T(8,128)S(1)}, f32[2112,128]{1,0:T(8,128)S(1)}, u32[]{:S(2)}, u32[]{:S(2)}) collective-permute-start(f32[2112,128]{1,0:T(8,128)S(1)} %get-tuple-element.18.refs_2_), channel_id=1, source_target_pairs={{0,4},{4,0},{8,12},{12,8},{16,20},{20,16},{24,28},{28,24},{32,36},... | collective-permute-start | bytes 3244040 | tf_op jit(solution)/shard_map/ppermute | solution.py:500
  13.9 28.1 %collective-permute-start.4 = (f32[2112,128]{1,0:T(8,128)S(1)}, f32[2112,128]{1,0:T(8,128)S(1)}, u32[]{:S(2)}, u32[]{:S(2)}) collective-permute-start(f32[2112,128]{1,0:T(8,128)S(1)} %get-tuple-element.19.refs_1_), channel_id=1, source_target_pairs={{0,0},{4,8},{8,4},{12,16},{16,12},{20,24},{24,20},{28,32},{32,28},... | collective-permute-start | bytes 3244040 | tf_op jit(solution)/shard_map/ppermute | solution.py:495
  38.1 38.9 %collective-permute-start.3 = (f32[2112,128]{1,0:T(8,128)S(1)}, f32[2112,128]{1,0:T(8,128)S(1)}, u32[]{:S(2)}, u32[]{:S(2)}) collective-permute-start(f32[2112,128]{1,0:T(8,128)S(1)} %collective-permute-done.2.refs_4_.refs_1_), channel_id=1, source_target_pairs={{4,8},{8,4},{12,16},{16,12},{20,24},{24,20},{28,32},{32,28},{36,40... | collective-permute-start | bytes 3244040 | tf_op jit(solution)/shard_map/ppermute | solution.py:495
  42.0 35.0 %collective-permute-start.5 = (f32[2112,128]{1,0:T(8,128)S(1)}, f32[2112,128]{1,0:T(8,128)S(1)}, u32[]{:S(2)}, u32[]{:S(2)}) collective-permute-start(f32[2112,128]{1,0:T(8,128)S(1)} %collective-permute-done.4.refs_0_), channel_id=1, source_target_pairs={{0,4},{4,0},{8,12},{12,8},{16,20},{20,16},{24,28},{28,24},{32,36},... | collective-permute-start | bytes 3244040 | tf_op jit(solution)/shard_map/ppermute | solution.py:500
  44.0 2.6 %collective-permute-start.6 = (f32[96,128]{1,0:T(8,128)S(1)}, f32[96,128]{1,0:T(8,128)S(1)}, u32[]{:S(2)}, u32[]{:S(2)}) collective-permute-start(f32[96,128]{1,0:T(8,128)S(1)} %shard_map.64), channel_id=1, source_target_pairs={{0,1},{1,0},{2,3},{3,2},{4,5},{5,4},{6,7},{7,6},{8,9},{9,8},{10,11... | collective-permute-start | bytes 147464 | tf_op jit(solution)/shard_map/ppermute | solution.py:522
  46.6 3.2 %collective-permute-start.7 = (f32[96,128]{1,0:T(8,128)S(1)}, f32[96,128]{1,0:T(8,128)S(1)}, u32[]{:S(2)}, u32[]{:S(2)}) collective-permute-start(f32[96,128]{1,0:T(8,128)S(1)} %add.10.refs_0_), channel_id=1, source_target_pairs={{0,2},{1,3},{2,0},{3,1},{4,6},{5,7},{6,4},{7,5},{8,10},{9,11},{10,... | collective-permute-start | bytes 147464 | tf_op jit(solution)/shard_map/ppermute | solution.py:522
  52.9 26.2 %collective-permute-start.8 = (f32[96,128]{1,0:T(8,128)S(1)}, f32[96,128]{1,0:T(8,128)S(1)}, u32[]{:S(2)}, u32[]{:S(2)}) collective-permute-start(f32[96,128]{1,0:T(8,128)S(1)} %get-tuple-element.20), channel_id=1, source_target_pairs={{0,0},{4,8},{8,4},{12,16},{16,12},{20,24},{24,20},{28,32},{32,28},... | collective-permute-start | bytes 147464 | tf_op jit(solution)/shard_map/ppermute | solution.py:495
  59.4 19.7 %collective-permute-start.9 = (f32[96,128]{1,0:T(8,128)S(1)}, f32[96,128]{1,0:T(8,128)S(1)}, u32[]{:S(2)}, u32[]{:S(2)}) collective-permute-start(f32[96,128]{1,0:T(8,128)S(1)} %get-tuple-element.21), channel_id=1, source_target_pairs={{0,4},{4,0},{8,12},{12,8},{16,20},{20,16},{24,28},{28,24},{32,36},... | collective-permute-start | bytes 147464 | tf_op jit(solution)/shard_map/ppermute | solution.py:500
  79.8 1.8 %collective-permute-start.10 = (f32[224,128]{1,0:T(8,128)S(1)}, f32[224,128]{1,0:T(8,128)S(1)}, u32[]{:S(2)}, u32[]{:S(2)}) collective-permute-start(f32[224,128]{1,0:T(8,128)S(1)} %shard_map.66), channel_id=1, source_target_pairs={{0,1},{1,0},{2,3},{3,2},{4,5},{5,4},{6,7},{7,6},{8,9},{9,8},{10,11... | collective-permute-start | bytes 344072 | tf_op jit(solution)/shard_map/ppermute | solution.py:522
  81.7 7.2 %collective-permute-start.13 = (f32[224,128]{1,0:T(8,128)S(1)}, f32[224,128]{1,0:T(8,128)S(1)}, u32[]{:S(2)}, u32[]{:S(2)}) collective-permute-start(f32[224,128]{1,0:T(8,128)S(1)} %add.11), channel_id=1, source_target_pairs={{0,4},{1,6},{2,5},{3,7},{4,0},{5,2},{6,1},{7,3},{8,12},{9,14},{10,... | collective-permute-start | bytes 344072 | tf_op jit(solution)/shard_map/ppermute | solution.py:510
  85.7 7.0 %collective-permute-start.11 = (f32[224,128]{1,0:T(8,128)S(1)}, f32[224,128]{1,0:T(8,128)S(1)}, u32[]{:S(2)}, u32[]{:S(2)}) collective-permute-start(f32[224,128]{1,0:T(8,128)S(1)} %add.11), channel_id=1, source_target_pairs={{0,0},{1,2},{2,1},{3,3},{4,8},{5,10},{6,9},{7,11},{8,4},{9,6},{10,... | collective-permute-start | bytes 344072 | tf_op jit(solution)/shard_map/ppermute | solution.py:510
  88.8 3.8 %collective-permute-start.14 = (f32[224,128]{1,0:T(8,128)S(1)}, f32[224,128]{1,0:T(8,128)S(1)}, u32[]{:S(2)}, u32[]{:S(2)}) collective-permute-start(f32[224,128]{1,0:T(8,128)S(1)} %collective-permute-done.13.refs_2_), channel_id=1, source_target_pairs={{0,1},{1,0},{2,3},{3,2},{4,5},{5,4},{6,7},{7,6},{8,9},{9,8},{10,11... | collective-permute-start | bytes 344072 | tf_op jit(solution)/shard_map/ppermute | solution.py:522
  92.7 1.3 %collective-permute-start.12 = (f32[224,128]{1,0:T(8,128)S(1)}, f32[224,128]{1,0:T(8,128)S(1)}, u32[]{:S(2)}, u32[]{:S(2)}) collective-permute-start(f32[224,128]{1,0:T(8,128)S(1)} %collective-permute-done.11.refs_0_), channel_id=1, source_target_pairs={{0,1},{1,0},{2,3},{3,2},{4,5},{5,4},{6,7},{7,6},{8,9},{9,8},{10,11... | collective-permute-start | bytes 344072 | tf_op jit(solution)/shard_map/ppermute | solution.py:522

commit v4 on v3

--- a/solution.py
+++ b/solution.py
@@ -10,8 +10,9 @@
 i32 = jnp.int32
 VMEM = pl.BlockSpec(memory_space=pltpu.VMEM)
 params = pltpu.CompilerParams(vmem_limit_bytes=24 * 1024 * 1024)
+CHUNKS = 8
+CUT = 5
 large_params = pltpu.CompilerParams(vmem_limit_bytes=52 * 1024 * 1024)
-PIECES = 1
 
 
 def split(value):
@@ -28,10 +29,6 @@
     return lax.dot_general(left, right, (((0,), (0,)), ((), ())), preferred_element_type=f32)
 
 
-def dot_fine(left, right):
-    return jnp.dot(left, right, precision=lax.Precision.HIGHEST, preferred_element_type=f32)
-
-
 def rotated(left, right):
     high, low = split(left)
     return dot(jnp.concatenate([high, low, high], 1), right)
@@ -47,8 +44,19 @@
     return rows // size, size
 
 
-def rows_at(index, size):
-    return pl.ds(pl.multiple_of(index * size, size), size)
+def part(refs, start, size):
+    for ref in refs:
+        if start < ref.shape[0]:
+            return ref[start : start + size, :]
+        start -= ref.shape[0]
+
+
+def put(refs, start, value):
+    for ref in refs:
+        if start < ref.shape[0]:
+            ref[start : start + value.shape[0], :] = value
+            return
+        start -= ref.shape[0]
 
 
 def call(body, out_shape, in_specs):
@@ -58,6 +66,7 @@
         in_specs=in_specs,
         out_specs=jax.tree.map(lambda _: VMEM, out_shape),
         compiler_params=params,
+        cost_estimate=pl.CostEstimate(flops=1, bytes_accessed=1, transcendentals=0),
     )
 
 
@@ -196,10 +205,6 @@
     )(samples, basis_cols, order)
 
 
-def diagonal_of(value, eye):
-    return jnp.sum(jnp.where(eye, value, 0.0), axis=0, keepdims=True)
-
-
 def lanes(value, index):
     return jnp.take_along_axis(value, index, axis=1, mode="promise_in_bounds")
 
@@ -210,48 +215,56 @@
     return row_id == col_id
 
 
-def turn_step(settled, carried, eye, index, sign, last):
-    width = settled.shape[0]
+def column_sums(value):
+    total = jnp.sum(value.reshape(-1, 8, value.shape[1]), axis=0)
+    for shift in (4, 2, 1):
+        total += pltpu.roll(total, shift, 0)
+    return total
+
+
+def scaled(value, factor):
+    return (value.reshape(-1, 8, value.shape[1]) * factor[None]).reshape(value.shape)
+
+
+def turn_step(settled, carried, eye, index, facing, sign, last):
     swapped = lanes(settled, index)
-    own = diagonal_of(settled, eye)
-    crossing = diagonal_of(swapped, eye)
-    both = lanes(
-        jnp.concatenate([jnp.broadcast_to(own, (8, width)), jnp.broadcast_to(crossing, (8, width))], 0),
-        index[:16],
-    )
-    across = sign * (own - both[0:1])
-    up = crossing + both[8:9]
+    own = column_sums(jnp.where(eye, settled, 0.0))
+    other = column_sums(jnp.where(facing, swapped, 0.0))
+    up = column_sums(jnp.where(eye, swapped, 0.0)) + column_sums(jnp.where(facing, settled, 0.0))
+    across = sign * (own - other)
     scale = jnp.maximum(jnp.abs(across), jnp.abs(up))
     found = scale > 0.0
     shrink = 1.0 / jnp.where(found, scale, 1.0)
     level = jnp.where(found, across * shrink, 1.0)
     slope = up * shrink
     inverse = lax.rsqrt(level * level + slope * slope)
-    square = 0.5 + 0.5 * jnp.abs(level) * inverse
-    against = lax.rsqrt(square)
-    major = square * against
+    major_square = 0.5 + 0.5 * jnp.abs(level) * inverse
+    against = lax.rsqrt(major_square)
+    major = major_square * against
     minor = 0.5 * jnp.abs(slope) * inverse * against
     ahead = level >= 0.0
     cosine = jnp.where(ahead, major, minor)
     sine = jnp.where(ahead, minor, major)
     sine = jnp.where(slope < 0.0, -sine, sine) * sign
-    carried = carried * cosine + lanes(carried, index) * sine
+    carried = scaled(carried, cosine) + scaled(lanes(carried, index), sine)
     if last == "turn":
         return None, carried
     if last == "sums":
-        return own * (cosine * cosine) + both[0:1] * (sine * sine) + up * (cosine * sine), carried
-    turned = (settled * cosine + swapped * sine).T
-    return turned * cosine + lanes(turned, index) * sine, carried
+        sums = own * (cosine * cosine) + other * (sine * sine) + up * (cosine * sine)
+        return sums[0:1], carried
+    turned = (scaled(settled, cosine) + scaled(swapped, sine)).T
+    return scaled(turned, cosine) + scaled(lanes(turned, index), sine), carried
 
 
 def solve(problems, partners, signs, last=None):
     width = problems[0][0].shape[0]
     eye = eye_of(width)
+    row_id = lax.broadcasted_iota(i32, (width, width), 0)
     for step in range(partners.shape[0]):
-        sign = signs[step : step + 1, :]
+        sign = jnp.broadcast_to(signs[step : step + 1, :], (8, width))
         index = jnp.broadcast_to(partners[step : step + 1, :], (width, width))
         ending = last if step == partners.shape[0] - 1 else None
-        problems = [turn_step(*problem, eye, index, sign, ending) for problem in problems]
+        problems = [turn_step(*problem, eye, index, row_id == index, sign, ending) for problem in problems]
     return problems
 
 
@@ -293,8 +306,8 @@
     )
 
 
-def rotate_body(factor_ref, projected_ref, turn_ref, *out_refs):
-    odd_refs, even_refs = out_refs[: len(out_refs) // 2], out_refs[len(out_refs) // 2 :]
+def rotate_body(odd_count, factor_ref, projected_ref, turn_ref, *out_refs):
+    odd_refs, even_refs = out_refs[:odd_count], out_refs[odd_count:]
     width = factor_ref.shape[1]
     half = width // 2
     packed = factor_ref.shape[0] // 2
@@ -310,26 +323,17 @@
         0,
     )
     weights = stacked(weights)
-    piece = packed // len(odd_refs)
-    count, size = chunks_of(piece, 512)
-    for number, (odd_ref, even_ref) in enumerate(zip(odd_refs, even_refs)):
-
-        def step(i, _):
-            start = pl.multiple_of(i * size, size)
-            lower = pl.ds(pl.multiple_of(number * piece + start, size), size)
-            upper = pl.ds(pl.multiple_of(packed + number * piece + start, size), size)
-            left = jnp.concatenate([factor_ref[lower, :], factor_ref[upper, :]], 1)
-            result = rotated(left, weights)
-            odd_ref[pl.ds(start, size), :] = result[:, :width]
-            even_ref[pl.ds(start, size), :] = result[:, width:]
-            return 0
-
-        lax.fori_loop(0, count, step, 0)
+
+    def spread(start, lower, upper):
+        result = rotated(jnp.concatenate([lower, upper], 1), weights)
+        put(odd_refs, start, result[:, :width])
+        put(even_refs, start, result[:, width:])
+
+    size = packed // CHUNKS
+    for start in range(0, packed, size):
+        spread(start, factor_ref[start : start + size, :], factor_ref[packed + start : packed + start + size, :])
     extra = projected_ref.shape[0] // 2
-    left = jnp.concatenate([projected_ref[:extra, :], projected_ref[extra:, :]], 1)
-    result = rotated(left, weights)
-    odd_refs[-1][piece : piece + extra, :] = result[:, :width]
-    even_refs[-1][piece : piece + extra, :] = result[:, width:]
+    spread(packed, projected_ref[:extra, :], projected_ref[extra:, :])
 
 
 def folded(whole):
@@ -347,23 +351,21 @@
     )
 
 
-def second_gram_body(piece, *refs):
+def second_gram_body(packed, count, *refs):
     refs, out_ref = refs[:-1], refs[-1]
-    odd_refs, even_refs = refs[: len(refs) // 2], refs[len(refs) // 2 :]
-    count, size = chunks_of(piece, 512)
-    width = 2 * odd_refs[0].shape[1]
+    odd_refs, even_refs = refs[:count], refs[count:]
+    size = packed // CHUNKS
+    width = 2 * refs[0].shape[1]
     total = jnp.zeros((width, 2 * width), f32)
-    for odd_ref, even_ref in zip(odd_refs, even_refs):
-
-        def step(i, total):
-            part = rows_at(i, size)
-            high, low = split(jnp.concatenate([odd_ref[part, :], even_ref[part, :]], 1))
-            return total + dot_rows(high, jnp.concatenate([high, low], 1))
-
-        total = lax.fori_loop(0, count, step, total)
+    for start in range(0, packed, size):
+        high, low = split(
+            jnp.concatenate([part(odd_refs, start, size), part(even_refs, start, size)], 1)
+        )
+        total += dot_rows(high, jnp.concatenate([high, low], 1))
     cross = folded(total[:, width:])
     gram = folded(total[:, :width]) + (cross + cross.T)
-    out_ref[...] = packed_gram(jnp.where(blk_index() % 2 == 1, swapped_rows(swapped_cols(gram)), gram))
+    gram = jnp.where(blk_index() % 2 == 1, swapped_rows(swapped_cols(gram)), gram)
+    out_ref[...] = packed_gram(gram)
 
 
 def second_solve_body(rounds, own_ref, other_ref, partner_ref, sign_ref, odd_ref, even_ref):
@@ -380,51 +382,42 @@
     even_ref[...] = jnp.where(take_top, bottom, top)
 
 
-def cross_body(piece, final, *refs):
-    refs, out_ref = refs[:-1], refs[-1]
-    number = len(refs) // 5
-    odd_far, odd_own, even_own, even_far, even_once = (
-        refs[i * number : (i + 1) * number] for i in range(5)
-    )
+def cross_body(packed, extra, final, odd_far, odd_own, even_own, even_far, even_once, *refs):
+    before_refs, out_ref = refs[:-1], refs[-1]
+    width = odd_own.shape[1]
+    half = width // 2
     position = blk_index()
     at_edge = jnp.logical_or(position == 0, position == final)
-    width = odd_own[0].shape[1]
-    half = width // 2
-    count, size = chunks_of(piece, 512)
-
-    def sides(index, part):
+
+    def sides(start, end):
+        odd_side = jnp.where(at_edge, even_once[start:end, :], odd_far[start:end, :])
         return (
-            jnp.concatenate(
-                [
-                    jnp.where(at_edge, even_once[index][part, :], odd_far[index][part, :]),
-                    odd_own[index][part, :],
-                ],
-                1,
-            ),
-            jnp.concatenate([even_own[index][part, :], even_far[index][part, :]], 1),
+            jnp.concatenate([odd_side, odd_own[start:end, :]], 1),
+            jnp.concatenate([even_own[start:end, :], even_far[start:end, :]], 1),
         )
 
+    size = packed // CHUNKS
+    rows = odd_own.shape[0] - extra
     total = jnp.zeros((2 * width, 2 * width), f32)
-    for index in range(number):
-
-        def step(i, total):
-            left, right = sides(index, rows_at(i, size))
-            left_high, left_low = split(left)
-            right_high, right_low = split(right)
-            return total + dot_rows(
-                jnp.concatenate([left_high, left_high, left_low], 0),
-                jnp.concatenate([right_high, right_low, right_high], 0),
-            )
-
-        total = lax.fori_loop(0, count, step, total)
-    out_ref[:width, :] = folded(total)
-    extra = odd_own[-1].shape[0] - piece
-    for side, value in enumerate(sides(-1, slice(piece, piece + extra))):
-        start = width + side * 2 * extra
-        out_ref[start : start + extra, :half] = value[:, :half]
-        out_ref[start : start + extra, half:] = value[:, width : width + half]
-        out_ref[start + extra : start + 2 * extra, :half] = value[:, half:width]
-        out_ref[start + extra : start + 2 * extra, half:] = value[:, width + half :]
+    for start in range(0, rows, size):
+        left, right = sides(start, start + size)
+        left_high, left_low = split(left)
+        right_high, right_low = split(right)
+        total += dot_rows(
+            jnp.concatenate([left_high, left_high, left_low], 0),
+            jnp.concatenate([right_high, right_low, right_high], 0),
+        )
+    total = folded(total)
+    for ref in before_refs:
+        total += ref[...]
+    out_ref[:width, :] = total
+    if extra:
+        for side, value in enumerate(sides(rows, rows + extra)):
+            start = width + side * 2 * extra
+            out_ref[start : start + extra, :half] = value[:, :half]
+            out_ref[start : start + extra, half:] = value[:, width : width + half]
+            out_ref[start + extra : start + 2 * extra, :half] = value[:, half:width]
+            out_ref[start + extra : start + 2 * extra, half:] = value[:, width + half :]
 
 
 def combine_body(final, cross_ref, odd_ref, even_ref, out_ref):
@@ -437,12 +430,14 @@
     odd_turn, even_turn = square(odd_ref[:half, :]), square(even_ref[:half, :])
     odd_turn = jnp.where(jnp.logical_xor(odd, at_edge), swapped_rows(odd_turn), odd_turn)
     even_turn = jnp.where(odd, swapped_rows(even_turn), even_turn)
-    cross = dot_fine(dot_fine(odd_turn.T, cross_ref[:width, :]), even_turn)
+    odd_stack, even_stack = stacked(odd_turn), stacked(even_turn)
+    high, low = split(rotated(cross_ref[:width, :], even_stack))
+    cross = dot_rows(odd_stack, jnp.concatenate([high, low, high], 0))
     share = 0.25
     odd_gram = square(odd_ref[half:, :]) * share
     even_gram = square(even_ref[half:, :]) * share
-    odd_samples = dot_fine(cross_ref[width : width + count, :], odd_turn)
-    even_samples = dot_fine(cross_ref[width + count :, :], even_turn)
+    odd_samples = rotated(cross_ref[width : width + count, :], odd_stack)
+    even_samples = rotated(cross_ref[width + count :, :], even_stack)
     first = jnp.where(odd, even_gram, odd_gram)
     second = jnp.where(odd, odd_gram, even_gram)
     cross = jnp.where(odd, cross.T, cross)
@@ -450,13 +445,15 @@
     out_ref[:count, half:] = jnp.where(odd, odd_samples, even_samples)
     out_ref[count : count + half, :half] = first
     out_ref[count : count + half, half:] = cross
-    out_ref[count + half :, :] = tall(second)
+    out_ref[count + half : count + half + half // 2, :] = tall(second)
+    out_ref[count + half + half // 2 :, :] = jnp.zeros((8, width), f32)
 
 
 def last_solve_body(
     rounds, final, odd_ref, odd_other_ref, even_ref, even_other_ref, partner_ref, sign_ref, sums_ref, squares_ref
 ):
-    wholes = [odd_ref[...] + odd_other_ref[...], even_ref[...] + even_other_ref[...]]
+    kept = odd_ref.shape[0]
+    wholes = [odd_ref[...] + odd_other_ref[...], even_ref[:kept, :] + even_other_ref[:kept, :]]
     width = wholes[0].shape[1]
     half = width // 2
     samples = wholes[0].shape[0] - width * 3 // 4
@@ -514,7 +511,7 @@
 def both_partners(value):
     count = lax.axis_size("blk")
     even = both_chips(value, even_partner)
-    odd = both_chips(value, lambda i: odd_partner(i, count))
+    odd = both_chips(value[:-8], lambda i: odd_partner(i, count))
     return odd + even
 
 
@@ -528,7 +525,6 @@
     sample_count = samples.shape[0]
     extra = sample_count // 2
     rounds, steps = pairing.shape[0], pairing.shape[1]
-    piece = packed // PIECES
     final = lax.axis_size("blk") - 1
 
     gram = first_gram(factor_cols)
@@ -538,34 +534,38 @@
     turn = call(lambda *refs: first_solve_body(rounds, *refs), shape(width, width), [VMEM] * 4)(
         paired, flipped(paired, 2), partner, sign
     )
-    pieces = [shape(piece + (extra if i == PIECES - 1 else 0), width) for i in range(PIECES)]
-    sent = call(rotate_body, tuple(pieces + pieces), [VMEM] * 3)(factor_cols, projected, turn)
-    to_odd, to_even = sent[:PIECES], sent[PIECES:]
-    odd_once, even_once, odd_twice, even_twice = [], [], [], []
-    for i in range(PIECES):
-        even_once.append(via_even(to_even[i]))
-        odd_once.append(via_odd(to_odd[i], True))
-    for i in range(PIECES):
-        odd_twice.append(via_odd(even_once[i], False))
-        even_twice.append(via_even(odd_once[i]))
-    gram = call(lambda *refs: second_gram_body(piece, *refs), shape(width * 3 // 4, width), [VMEM] * (2 * PIECES))(
-        *odd_once, *even_once
-    )
+    first, second = packed * CUT // CHUNKS, packed * (CHUNKS - CUT) // CHUNKS + extra
+    pieces = [shape(first, width), shape(second, width)]
+    count = len(pieces)
+    sent = call(
+        lambda *refs: rotate_body(count, *refs), tuple(pieces + pieces), [VMEM] * 3
+    )(factor_cols, projected, turn)
+    to_odd, to_even = sent[:count], sent[count:]
+    even_once = [via_even(value) for value in to_even]
+    odd_once = [via_odd(value, True) for value in to_odd]
+    odd_twice = [via_odd(value, False) for value in even_once]
+    even_twice = [via_even(value) for value in odd_once]
+    gram = call(
+        lambda *refs: second_gram_body(packed, count, *refs),
+        shape(width * 3 // 4, width),
+        [VMEM] * (2 * count),
+    )(*odd_once, *even_once)
     paired = gram + flipped(gram, 1)
     for_odd, for_even = call(
         lambda *refs: second_solve_body(rounds, *refs),
         (shape(width * 3 // 4, width), shape(width * 3 // 4, width)),
         [VMEM] * 4,
     )(paired, flipped(paired, 2), partner, sign)
+    groups = [list(group) for group in zip(odd_twice, to_odd, to_even, even_twice, even_once)]
+    groups[0][1], for_odd, for_even = lax.optimization_barrier((groups[0][1], for_odd, for_even))
+    cross = call(lambda *refs: cross_body(packed, 0, final, *refs), shape(width, width), [VMEM] * 5)(*groups[0])
     from_even = via_even(for_even)
     from_odd = via_odd(for_odd, True)
     cross = call(
-        lambda *refs: cross_body(piece, final, *refs),
-        shape(width + 2 * sample_count, width),
-        [VMEM] * (5 * PIECES),
-    )(*odd_twice, *to_odd, *to_even, *even_twice, *even_once)
+        lambda *refs: cross_body(packed, extra, final, *refs), shape(width + 2 * sample_count, width), [VMEM] * 6
+    )(*groups[1], cross)
     whole = call(
-        lambda *refs: combine_body(final, *refs), shape(width * 3 // 4 + sample_count, width), [VMEM] * 3
+        lambda *refs: combine_body(final, *refs), shape(width * 3 // 4 + sample_count + 8, width), [VMEM] * 3
     )(cross, from_odd, from_even)
     paired = whole + flipped(whole, 1)
     sums, squares = call(

time: 98 us -> 95.1 us (0.970)
  starting transfers between devices: 44.3 us -> 55.3 us
  waiting for transfers between devices: 31.4 us -> 21.1 us
  Pallas kernels: 21.2 us -> 17.5 us
    ppermute x3 -> x5, waiting for transfers between devices: 19.5 us -> 9.9 us  [via_even(): lax.ppermute(value, 'blk', [(i, even_partner(i)) for i in range(count)])]
    ppermute x3 -> x5, starting transfers between devices: 15.1 us -> 24.7 us  [via_odd(): lax.ppermute(value, 'blk', [pair for pair in pairs if closed or pair[0] !...]
    ppermute x7, starting transfers between devices: 5.07 us -> 7.22 us  [flipped(): lax.ppermute(value, 'rows', [(i, i ^ bit) for i in range(lax.axis_size('r...]
    pallas_call x3 -> x4, Pallas kernels: 5.73 us -> 3.86 us  [the longest x1 1.21 us: on_device(): call(lambda *refs: rotate_body(count, *refs), tuple(pieces + pieces), [VM...]
    ppermute x3 -> x5, starting transfers between devices: 18.3 us -> 18.3 us  [via_even(): lax.ppermute(value, 'blk', [(i, even_partner(i)) for i in range(count)])]
  transfers between devices with their start and end apart: 15 -> 19, of which waited for: 8 -> 9; matrix products, arithmetic and copies ran while one was open for 0% -> 0% of each run, Pallas kernels for 10% -> 8%
where the time goes in v4:
time: 95.1 us; the launch traced here: 94.8 us
  starting transfers between devices  55.3 us (58%)
  waiting for transfers between devices  21.1 us (22%)
  Pallas kernels  17.5 us (18%)
    ppermute x5, starting transfers between devices, via_odd(): lax.ppermute(value, 'blk', [pair for pair in pairs if closed or pair[0] !...  24.7 us
    ppermute x5, starting transfers between devices, via_even(): lax.ppermute(value, 'blk', [(i, even_partner(i)) for i in range(count)])  18.3 us
    ppermute x5, waiting for transfers between devices, via_even(): lax.ppermute(value, 'blk', [(i, even_partner(i)) for i in range(count)])  9.9 us
    ppermute x7, starting transfers between devices, flipped(): lax.ppermute(value, 'rows', [(i, i ^ bit) for i in range(lax.axis_size('r...  7.22 us
    ppermute x7, waiting for transfers between devices, flipped(): lax.ppermute(value, 'rows', [(i, i ^ bit) for i in range(lax.axis_size('r...  6.11 us
    ppermute x2, starting transfers between devices, both_chips(): mine = lax.ppermute(value, ('blk', 'rows'), pairs)  5.2 us
    ppermute x2, waiting for transfers between devices, both_chips(): mine = lax.ppermute(value, ('blk', 'rows'), pairs)  5.08 us
    pallas_call x1, Pallas kernels, on_device(): call(lambda *refs: last_solve_body(rounds, final, *refs), (shape(1, width...  3.28 us
  transfers between devices with their start and end apart: 19, of which 9 were waited for; matrix products, arithmetic and copies ran while one was open for 0% of the time, Pallas kernels for 8%

profile of v4, /device:TPU:33, one launch (start us, length us, event | category | flops | bytes accessed | tf_op | source)
XLA Modules:
  0.0 94.8 jit_solution(9623562110053258461)
XLA Ops:
  0.6 2.3 %shard_map.59 = f32[96,128]{1,0:T(8,128)S(1)} custom-call(f32[4096,128]{1,0:T(8,128)} %refs_0_.1), custom_call_target="tpu_custom_call" | custom-call | tf_op jit(solution)/shard_map/pallas_call | solution.py:135
  3.0 0.8 collective-permute-start
  3.7 0.9 collective-permute-done
  4.6 1.3 %collective-permute-start.1 = (f32[96,128]{1,0:T(8,128)S(1)}, f32[96,128]{1,0:T(8,128)S(1)}, u32[]{:S(2)}, u32[]{:S(2)}) collective-permute-start(f32[96,128]{1,0:T(8,128)S(1)} %add.9.refs_0_), channel_id=1, source_target_pairs={{0,2},{1,3},{2,0},{3,1},{4,6},{5,7},{6,4},{7,5},{8,10},{9,11},{10,... | collective-permute-start | bytes 147464 | tf_op jit(solution)/shard_map/ppermute | solution.py:519
  5.9 2.7 %shard_map.60 = (f32[128,128]{1,0:T(8,128)S(1)}, s32[24,128]{1,0:T(8,128)S(1)}, f32[24,128]{1,0:T(8,128)S(1)}) custom-call(f32[128,4096]{1,0:T(8,128)} %samples_hbm.1, f32[4096,128]{1,0:T(8,128)} %basis_hbm.1, s32[24,128]{1,0:T(8,128)S(1)} %bitcast.3), custom_call_target="tpu_custom_call" | custom-call | tf_op jit(solution)/shard_map/pallas_call | solution.py:190
  8.6 0.0 collective-permute-done.1.refs_1_
  8.6 2.3 %shard_map.61.refs_2_ = f32[128,128]{1,0:T(8,128)S(1)} custom-call(f32[96,128]{1,0:T(8,128)S(1)} %add.9.refs_0_, f32[96,128]{1,0:T(8,128)S(1)} %collective-permute-done.1.refs_1_, s32[24,128]{1,0:T(8,128)S(1)} %get-tuple-element.21.refs_2_.refs_4_, f32[24,128]{1,0:T(8,128)S(1)} %get-tuple-element.22.refs_3_.refs_5_), custom_call_target="tpu_custom_call" | custom-call | flops 1 | bytes 1 | tf_op jit(solution)/shard_map/pallas_call | solution.py:534
  10.9 1.2 %shard_map.62 = (f32[1280,128]{1,0:T(8,128)S(1)}, f32[832,128]{1,0:T(8,128)S(1)}, f32[1280,128]{1,0:T(8,128)S(1)}, f32[832,128]{1,0:T(8,128)S(1)}) custom-call(f32[4096,128]{1,0:T(8,128)S(1)} %copy-done, f32[128,128]{1,0:T(8,128)S(1)} %get-tuple-element.19.refs_1_, f32[128,128]{1,0:T(8,128)S(1)} %shard_map.61.refs_2_), custom_call_target="tpu_custom_call" | custom-call | flops 1 | bytes 1 | tf_op jit(solution)/shard_map/pallas_call | solution.py:540
  12.1 0.6 collective-permute-start.6
  12.7 4.7 %collective-permute-start.8 = (f32[1280,128]{1,0:T(8,128)S(1)}, f32[1280,128]{1,0:T(8,128)S(1)}, u32[]{:S(2)}, u32[]{:S(2)}) collective-permute-start(f32[1280,128]{1,0:T(8,128)S(1)} %get-tuple-element.29.refs_1_), channel_id=1, source_target_pairs={{0,0},{4,8},{8,4},{12,16},{16,12},{20,24},{24,20},{28,32},{32,28},... | collective-permute-start | bytes 1966088 | tf_op jit(solution)/shard_map/ppermute | solution.py:492
  17.4 0.1 collective-permute-start.2
  17.5 5.5 %collective-permute-start.4 = (f32[832,128]{1,0:T(8,128)S(1)}, f32[832,128]{1,0:T(8,128)S(1)}, u32[]{:S(2)}, u32[]{:S(2)}) collective-permute-start(f32[832,128]{1,0:T(8,128)S(1)} %get-tuple-element.24.refs_1_), channel_id=1, source_target_pairs={{0,0},{4,8},{8,4},{12,16},{16,12},{20,24},{24,20},{28,32},{32,28},... | collective-permute-start | bytes 1277960 | tf_op jit(solution)/shard_map/ppermute | solution.py:492
  22.9 4.8 %collective-permute-done.6.refs_2_.refs_4_ = f32[1280,128]{1,0:T(8,128)S(1)} collective-permute-done((f32[1280,128]{1,0:T(8,128)S(1)}, f32[1280,128]{1,0:T(8,128)S(1)}, u32[]{:S(2)}, u32[]{:S(2)}) %collective-permute-start.6) | collective-permute-done | bytes 655392 | tf_op jit(solution)/shard_map/ppermute | solution.py:497
  27.7 3.9 %collective-permute-start.7 = (f32[1280,128]{1,0:T(8,128)S(1)}, f32[1280,128]{1,0:T(8,128)S(1)}, u32[]{:S(2)}, u32[]{:S(2)}) collective-permute-start(f32[1280,128]{1,0:T(8,128)S(1)} %collective-permute-done.6.refs_2_.refs_4_), channel_id=1, source_target_pairs={{4,8},{8,4},{12,16},{16,12},{20,24},{24,20},{28,32},{32,28},{36,40... | collective-permute-start | bytes 1966088 | tf_op jit(solution)/shard_map/ppermute | solution.py:492
  31.7 0.0 collective-permute-done.8.refs_0_
  31.7 0.1 collective-permute-start.11
  31.8 5.1 %collective-permute-done.2.refs_3_.refs_4_ = f32[832,128]{1,0:T(8,128)S(1)} collective-permute-done((f32[832,128]{1,0:T(8,128)S(1)}, f32[832,128]{1,0:T(8,128)S(1)}, u32[]{:S(2)}, u32[]{:S(2)}) %collective-permute-start.2) | collective-permute-done | bytes 426016 | tf_op jit(solution)/shard_map/ppermute | solution.py:497
  36.9 3.9 %collective-permute-start.3 = (f32[832,128]{1,0:T(8,128)S(1)}, f32[832,128]{1,0:T(8,128)S(1)}, u32[]{:S(2)}, u32[]{:S(2)}) collective-permute-start(f32[832,128]{1,0:T(8,128)S(1)} %collective-permute-done.2.refs_3_.refs_4_), channel_id=1, source_target_pairs={{4,8},{8,4},{12,16},{16,12},{20,24},{24,20},{28,32},{32,28},{36,40... | collective-permute-start | bytes 1277960 | tf_op jit(solution)/shard_map/ppermute | solution.py:492
  40.8 0.0 collective-permute-done.4.refs_1_
  40.8 0.1 collective-permute-start.5
  40.9 1.1 %shard_map.63 = f32[96,128]{1,0:T(8,128)S(1)} custom-call(f32[1280,128]{1,0:T(8,128)S(1)} %collective-permute-done.8.refs_0_, f32[832,128]{1,0:T(8,128)S(1)} %collective-permute-done.4.refs_1_, f32[1280,128]{1,0:T(8,128)S(1)} %collective-permute-done.6.refs_2_.refs_4_, f32[832,128]{1,0:T(8,128)S(1)} %collective-permute-done.2.refs_3_.refs_4_), custom_call_target="tpu_custom_call" | custom-call | flops 1 | bytes 1 | tf_op jit(solution)/shard_map/pallas_call | solution.py:548
  42.0 2.7 %collective-permute-start.9 = (f32[96,128]{1,0:T(8,128)S(1)}, f32[96,128]{1,0:T(8,128)S(1)}, u32[]{:S(2)}, u32[]{:S(2)}) collective-permute-start(f32[96,128]{1,0:T(8,128)S(1)} %shard_map.63), channel_id=1, source_target_pairs={{0,1},{1,0},{2,3},{3,2},{4,5},{5,4},{6,7},{7,6},{8,9},{9,8},{10,11... | collective-permute-start | bytes 147464 | tf_op jit(solution)/shard_map/ppermute | solution.py:519
  44.7 0.9 collective-permute-done.9
  45.6 1.2 %collective-permute-start.10 = (f32[96,128]{1,0:T(8,128)S(1)}, f32[96,128]{1,0:T(8,128)S(1)}, u32[]{:S(2)}, u32[]{:S(2)}) collective-permute-start(f32[96,128]{1,0:T(8,128)S(1)} %add.10.refs_0_), channel_id=1, source_target_pairs={{0,2},{1,3},{2,0},{3,1},{4,6},{5,7},{6,4},{7,5},{8,10},{9,11},{10,... | collective-permute-start | bytes 147464 | tf_op jit(solution)/shard_map/ppermute | solution.py:519
  46.7 2.1 %collective-permute-done.10.refs_1_ = f32[96,128]{1,0:T(8,128)S(1)} collective-permute-done((f32[96,128]{1,0:T(8,128)S(1)}, f32[96,128]{1,0:T(8,128)S(1)}, u32[]{:S(2)}, u32[]{:S(2)}) %collective-permute-start.10) | collective-permute-done | bytes 49184 | tf_op jit(solution)/shard_map/ppermute | solution.py:519
  48.8 2.5 %shard_map.64 = (f32[96,128]{1,0:T(8,128)S(1)}, f32[96,128]{1,0:T(8,128)S(1)}) custom-call(f32[96,128]{1,0:T(8,128)S(1)} %add.10.refs_0_, f32[96,128]{1,0:T(8,128)S(1)} %collective-permute-done.10.refs_1_, s32[24,128]{1,0:T(8,128)S(1)} %get-tuple-element.21.refs_2_.refs_4_, f32[24,128]{1,0:T(8,128)S(1)} %get-tuple-element.22.refs_3_.refs_5_), custom_call_target="tpu_custom_call" | custom-call | flops 1 | bytes 1 | tf_op jit(solution)/shard_map/pallas_call | solution.py:554
  51.3 6.7 %collective-permute-start.12 = (f32[96,128]{1,0:T(8,128)S(1)}, f32[96,128]{1,0:T(8,128)S(1)}, u32[]{:S(2)}, u32[]{:S(2)}) collective-permute-start(f32[96,128]{1,0:T(8,128)S(1)} %get-tuple-element.30), channel_id=1, source_target_pairs={{0,0},{4,8},{8,4},{12,16},{16,12},{20,24},{24,20},{28,32},{32,28},... | collective-permute-start | bytes 147464 | tf_op jit(solution)/shard_map/ppermute | solution.py:492
  58.0 0.0 collective-permute-done.7.refs_0_
  58.0 17.4 %collective-permute-start.13 = (f32[96,128]{1,0:T(8,128)S(1)}, f32[96,128]{1,0:T(8,128)S(1)}, u32[]{:S(2)}, u32[]{:S(2)}) collective-permute-start(f32[96,128]{1,0:T(8,128)S(1)} %get-tuple-element.31), channel_id=1, source_target_pairs={{0,4},{4,0},{8,12},{12,8},{16,20},{20,16},{24,28},{28,24},{32,36},... | collective-permute-start | bytes 147464 | tf_op jit(solution)/shard_map/ppermute | solution.py:497
  75.4 0.0 collective-permute-done.11.refs_3_
  75.4 0.9 shard_map.65.refs_5_
  76.3 0.0 collective-permute-done.3.refs_0_
  76.3 0.0 collective-permute-done.5.refs_3_
  76.4 0.7 shard_map.66.refs_0_
  77.0 0.0 collective-permute-done.12.refs_1_
  77.1 0.0 collective-permute-done.13.refs_2_
  77.1 0.6 shard_map.67
  77.6 1.3 %collective-permute-start.14 = (f32[232,128]{1,0:T(8,128)S(1)}, f32[232,128]{1,0:T(8,128)S(1)}, u32[]{:S(2)}, u32[]{:S(2)}) collective-permute-start(f32[232,128]{1,0:T(8,128)S(1)} %shard_map.67), channel_id=1, source_target_pairs={{0,1},{1,0},{2,3},{3,2},{4,5},{5,4},{6,7},{7,6},{8,9},{9,8},{10,11... | collective-permute-start | bytes 356360 | tf_op jit(solution)/shard_map/ppermute | solution.py:519
  78.9 1.0 %collective-permute-done.14 = f32[232,128]{1,0:T(8,128)S(1)} collective-permute-done((f32[232,128]{1,0:T(8,128)S(1)}, f32[232,128]{1,0:T(8,128)S(1)}, u32[]{:S(2)}, u32[]{:S(2)}) %collective-permute-start.14) | collective-permute-done | bytes 118816 | tf_op jit(solution)/shard_map/ppermute | solution.py:519
  79.9 3.3 %collective-permute-start.17 = (f32[232,128]{1,0:T(8,128)S(1)}, f32[232,128]{1,0:T(8,128)S(1)}, u32[]{:S(2)}, u32[]{:S(2)}) collective-permute-start(f32[232,128]{1,0:T(8,128)S(1)} %add.11), channel_id=1, source_target_pairs={{0,4},{1,6},{2,5},{3,7},{4,0},{5,2},{6,1},{7,3},{8,12},{9,14},{10,... | collective-permute-start | bytes 356360 | tf_op jit(solution)/shard_map/ppermute | solution.py:507
  83.2 1.9 %collective-permute-start.15 = (f32[224,128]{1,0:T(8,128)S(1)}, f32[224,128]{1,0:T(8,128)S(1)}, u32[]{:S(2)}, u32[]{:S(2)}) collective-permute-start(f32[224,128]{1,0:T(8,128)S(1)} %slice.4), channel_id=1, source_target_pairs={{0,0},{1,2},{2,1},{3,3},{4,8},{5,10},{6,9},{7,11},{8,4},{9,6},{10,... | collective-permute-start | bytes 344072 | tf_op jit(solution)/shard_map/ppermute | solution.py:507
  85.1 1.3 %collective-permute-done.17.refs_2_ = f32[232,128]{1,0:T(8,128)S(1)} collective-permute-done((f32[232,128]{1,0:T(8,128)S(1)}, f32[232,128]{1,0:T(8,128)S(1)}, u32[]{:S(2)}, u32[]{:S(2)}) %collective-permute-start.17) | collective-permute-done | bytes 118816 | tf_op jit(solution)/shard_map/ppermute | solution.py:507
  86.4 0.0 collective-permute-start.18
  86.4 3.8 %collective-permute-done.15.refs_0_ = f32[224,128]{1,0:T(8,128)S(1)} collective-permute-done((f32[224,128]{1,0:T(8,128)S(1)}, f32[224,128]{1,0:T(8,128)S(1)}, u32[]{:S(2)}, u32[]{:S(2)}) %collective-permute-start.15) | collective-permute-done | bytes 114720 | tf_op jit(solution)/shard_map/ppermute | solution.py:507
  90.2 0.0 collective-permute-start.16
  90.2 1.3 %collective-permute-done.16.refs_1_ = f32[224,128]{1,0:T(8,128)S(1)} collective-permute-done((f32[224,128]{1,0:T(8,128)S(1)}, f32[224,128]{1,0:T(8,128)S(1)}, u32[]{:S(2)}, u32[]{:S(2)}) %collective-permute-start.16) | collective-permute-done | bytes 114720 | tf_op jit(solution)/shard_map/ppermute | solution.py:519
  91.5 0.0 collective-permute-done.18.refs_3_
  91.5 3.3 %shard_map.68 = (f32[1,128]{1,0:T(1,128)}, f32[1,128]{1,0:T(1,128)}) custom-call(f32[224,128]{1,0:T(8,128)S(1)} %collective-permute-done.15.refs_0_, f32[224,128]{1,0:T(8,128)S(1)} %collective-permute-done.16.refs_1_, f32[232,128]{1,0:T(8,128)S(1)} %collective-permute-done.17.refs_2_, f32[232,128]{1,0:T(8,128)S(1)} %collective-permute-done.18.refs_3_, ...), custom_call_target="tpu_custom_call" | custom-call | flops 1 | bytes 1 | tf_op jit(solution)/shard_map/pallas_call | solution.py:571
  (8 shorter events, 0.1 us)
Async XLA Ops:
  0.6 5.3 %copy-start.1 = (s32[3,8,128]{2,1,0:T(8,128)S(1)}, s32[3,8,128]{2,1,0:T(8,128)}, u32[]{:S(2)}) copy-start(s32[3,8,128]{2,1,0:T(8,128)} %param.7) | copy-start | bytes 36868
  3.0 1.6 %collective-permute-start = (f32[96,128]{1,0:T(8,128)S(1)}, f32[96,128]{1,0:T(8,128)S(1)}, u32[]{:S(2)}, u32[]{:S(2)}) collective-permute-start(f32[96,128]{1,0:T(8,128)S(1)} %shard_map.59), channel_id=1, source_target_pairs={{0,1},{1,0},{2,3},{3,2},{4,5},{5,4},{6,7},{7,6},{8,9},{9,8},{10,11... | collective-permute-start | bytes 147464 | tf_op jit(solution)/shard_map/ppermute | solution.py:519
  4.6 4.0 %collective-permute-start.1 = (f32[96,128]{1,0:T(8,128)S(1)}, f32[96,128]{1,0:T(8,128)S(1)}, u32[]{:S(2)}, u32[]{:S(2)}) collective-permute-start(f32[96,128]{1,0:T(8,128)S(1)} %add.9.refs_0_), channel_id=1, source_target_pairs={{0,2},{1,3},{2,0},{3,1},{4,6},{5,7},{6,4},{7,5},{8,10},{9,11},{10,... | collective-permute-start | bytes 147464 | tf_op jit(solution)/shard_map/ppermute | solution.py:519
  5.9 5.0 %copy-start = (f32[4096,128]{1,0:T(8,128)S(1)}, f32[4096,128]{1,0:T(8,128)}, u32[]{:S(2)}) copy-start(f32[4096,128]{1,0:T(8,128)} %refs_0_.1) | copy-start | bytes 6291460
  12.1 15.6 %collective-permute-start.6 = (f32[1280,128]{1,0:T(8,128)S(1)}, f32[1280,128]{1,0:T(8,128)S(1)}, u32[]{:S(2)}, u32[]{:S(2)}) collective-permute-start(f32[1280,128]{1,0:T(8,128)S(1)} %get-tuple-element.25.refs_2_), channel_id=1, source_target_pairs={{0,4},{4,0},{8,12},{12,8},{16,20},{20,16},{24,28},{28,24},{32,36},... | collective-permute-start | bytes 1966088 | tf_op jit(solution)/shard_map/ppermute | solution.py:497
  12.7 19.0 %collective-permute-start.8 = (f32[1280,128]{1,0:T(8,128)S(1)}, f32[1280,128]{1,0:T(8,128)S(1)}, u32[]{:S(2)}, u32[]{:S(2)}) collective-permute-start(f32[1280,128]{1,0:T(8,128)S(1)} %get-tuple-element.29.refs_1_), channel_id=1, source_target_pairs={{0,0},{4,8},{8,4},{12,16},{16,12},{20,24},{24,20},{28,32},{32,28},... | collective-permute-start | bytes 1966088 | tf_op jit(solution)/shard_map/ppermute | solution.py:492
  17.4 19.5 %collective-permute-start.2 = (f32[832,128]{1,0:T(8,128)S(1)}, f32[832,128]{1,0:T(8,128)S(1)}, u32[]{:S(2)}, u32[]{:S(2)}) collective-permute-start(f32[832,128]{1,0:T(8,128)S(1)} %get-tuple-element.23.refs_2_), channel_id=1, source_target_pairs={{0,4},{4,0},{8,12},{12,8},{16,20},{20,16},{24,28},{28,24},{32,36},... | collective-permute-start | bytes 1277960 | tf_op jit(solution)/shard_map/ppermute | solution.py:497
  17.5 23.3 %collective-permute-start.4 = (f32[832,128]{1,0:T(8,128)S(1)}, f32[832,128]{1,0:T(8,128)S(1)}, u32[]{:S(2)}, u32[]{:S(2)}) collective-permute-start(f32[832,128]{1,0:T(8,128)S(1)} %get-tuple-element.24.refs_1_), channel_id=1, source_target_pairs={{0,0},{4,8},{8,4},{12,16},{16,12},{20,24},{24,20},{28,32},{32,28},... | collective-permute-start | bytes 1277960 | tf_op jit(solution)/shard_map/ppermute | solution.py:492
  27.7 30.3 %collective-permute-start.7 = (f32[1280,128]{1,0:T(8,128)S(1)}, f32[1280,128]{1,0:T(8,128)S(1)}, u32[]{:S(2)}, u32[]{:S(2)}) collective-permute-start(f32[1280,128]{1,0:T(8,128)S(1)} %collective-permute-done.6.refs_2_.refs_4_), channel_id=1, source_target_pairs={{4,8},{8,4},{12,16},{16,12},{20,24},{24,20},{28,32},{32,28},{36,40... | collective-permute-start | bytes 1966088 | tf_op jit(solution)/shard_map/ppermute | solution.py:492
  31.7 43.7 %collective-permute-start.11 = (f32[1280,128]{1,0:T(8,128)S(1)}, f32[1280,128]{1,0:T(8,128)S(1)}, u32[]{:S(2)}, u32[]{:S(2)}) collective-permute-start(f32[1280,128]{1,0:T(8,128)S(1)} %collective-permute-done.8.refs_0_), channel_id=1, source_target_pairs={{0,4},{4,0},{8,12},{12,8},{16,20},{20,16},{24,28},{28,24},{32,36},... | collective-permute-start | bytes 1966088 | tf_op jit(solution)/shard_map/ppermute | solution.py:497
  36.9 39.5 %collective-permute-start.3 = (f32[832,128]{1,0:T(8,128)S(1)}, f32[832,128]{1,0:T(8,128)S(1)}, u32[]{:S(2)}, u32[]{:S(2)}) collective-permute-start(f32[832,128]{1,0:T(8,128)S(1)} %collective-permute-done.2.refs_3_.refs_4_), channel_id=1, source_target_pairs={{4,8},{8,4},{12,16},{16,12},{20,24},{24,20},{28,32},{32,28},{36,40... | collective-permute-start | bytes 1277960 | tf_op jit(solution)/shard_map/ppermute | solution.py:492
  40.8 35.5 %collective-permute-start.5 = (f32[832,128]{1,0:T(8,128)S(1)}, f32[832,128]{1,0:T(8,128)S(1)}, u32[]{:S(2)}, u32[]{:S(2)}) collective-permute-start(f32[832,128]{1,0:T(8,128)S(1)} %collective-permute-done.4.refs_1_), channel_id=1, source_target_pairs={{0,4},{4,0},{8,12},{12,8},{16,20},{20,16},{24,28},{28,24},{32,36},... | collective-permute-start | bytes 1277960 | tf_op jit(solution)/shard_map/ppermute | solution.py:497
  42.0 3.6 %collective-permute-start.9 = (f32[96,128]{1,0:T(8,128)S(1)}, f32[96,128]{1,0:T(8,128)S(1)}, u32[]{:S(2)}, u32[]{:S(2)}) collective-permute-start(f32[96,128]{1,0:T(8,128)S(1)} %shard_map.63), channel_id=1, source_target_pairs={{0,1},{1,0},{2,3},{3,2},{4,5},{5,4},{6,7},{7,6},{8,9},{9,8},{10,11... | collective-permute-start | bytes 147464 | tf_op jit(solution)/shard_map/ppermute | solution.py:519
  45.6 3.2 %collective-permute-start.10 = (f32[96,128]{1,0:T(8,128)S(1)}, f32[96,128]{1,0:T(8,128)S(1)}, u32[]{:S(2)}, u32[]{:S(2)}) collective-permute-start(f32[96,128]{1,0:T(8,128)S(1)} %add.10.refs_0_), channel_id=1, source_target_pairs={{0,2},{1,3},{2,0},{3,1},{4,6},{5,7},{6,4},{7,5},{8,10},{9,11},{10,... | collective-permute-start | bytes 147464 | tf_op jit(solution)/shard_map/ppermute | solution.py:519
  51.3 25.7 %collective-permute-start.12 = (f32[96,128]{1,0:T(8,128)S(1)}, f32[96,128]{1,0:T(8,128)S(1)}, u32[]{:S(2)}, u32[]{:S(2)}) collective-permute-start(f32[96,128]{1,0:T(8,128)S(1)} %get-tuple-element.30), channel_id=1, source_target_pairs={{0,0},{4,8},{8,4},{12,16},{16,12},{20,24},{24,20},{28,32},{32,28},... | collective-permute-start | bytes 147464 | tf_op jit(solution)/shard_map/ppermute | solution.py:492
  58.0 19.0 %collective-permute-start.13 = (f32[96,128]{1,0:T(8,128)S(1)}, f32[96,128]{1,0:T(8,128)S(1)}, u32[]{:S(2)}, u32[]{:S(2)}) collective-permute-start(f32[96,128]{1,0:T(8,128)S(1)} %get-tuple-element.31), channel_id=1, source_target_pairs={{0,4},{4,0},{8,12},{12,8},{16,20},{20,16},{24,28},{28,24},{32,36},... | collective-permute-start | bytes 147464 | tf_op jit(solution)/shard_map/ppermute | solution.py:497
  77.6 2.2 %collective-permute-start.14 = (f32[232,128]{1,0:T(8,128)S(1)}, f32[232,128]{1,0:T(8,128)S(1)}, u32[]{:S(2)}, u32[]{:S(2)}) collective-permute-start(f32[232,128]{1,0:T(8,128)S(1)} %shard_map.67), channel_id=1, source_target_pairs={{0,1},{1,0},{2,3},{3,2},{4,5},{5,4},{6,7},{7,6},{8,9},{9,8},{10,11... | collective-permute-start | bytes 356360 | tf_op jit(solution)/shard_map/ppermute | solution.py:519
  79.9 6.5 %collective-permute-start.17 = (f32[232,128]{1,0:T(8,128)S(1)}, f32[232,128]{1,0:T(8,128)S(1)}, u32[]{:S(2)}, u32[]{:S(2)}) collective-permute-start(f32[232,128]{1,0:T(8,128)S(1)} %add.11), channel_id=1, source_target_pairs={{0,4},{1,6},{2,5},{3,7},{4,0},{5,2},{6,1},{7,3},{8,12},{9,14},{10,... | collective-permute-start | bytes 356360 | tf_op jit(solution)/shard_map/ppermute | solution.py:507
  83.2 7.0 %collective-permute-start.15 = (f32[224,128]{1,0:T(8,128)S(1)}, f32[224,128]{1,0:T(8,128)S(1)}, u32[]{:S(2)}, u32[]{:S(2)}) collective-permute-start(f32[224,128]{1,0:T(8,128)S(1)} %slice.4), channel_id=1, source_target_pairs={{0,0},{1,2},{2,1},{3,3},{4,8},{5,10},{6,9},{7,11},{8,4},{9,6},{10,... | collective-permute-start | bytes 344072 | tf_op jit(solution)/shard_map/ppermute | solution.py:507
  86.4 5.1 %collective-permute-start.18 = (f32[232,128]{1,0:T(8,128)S(1)}, f32[232,128]{1,0:T(8,128)S(1)}, u32[]{:S(2)}, u32[]{:S(2)}) collective-permute-start(f32[232,128]{1,0:T(8,128)S(1)} %collective-permute-done.17.refs_2_), channel_id=1, source_target_pairs={{0,1},{1,0},{2,3},{3,2},{4,5},{5,4},{6,7},{7,6},{8,9},{9,8},{10,11... | collective-permute-start | bytes 356360 | tf_op jit(solution)/shard_map/ppermute | solution.py:519
  90.2 1.3 %collective-permute-start.16 = (f32[224,128]{1,0:T(8,128)S(1)}, f32[224,128]{1,0:T(8,128)S(1)}, u32[]{:S(2)}, u32[]{:S(2)}) collective-permute-start(f32[224,128]{1,0:T(8,128)S(1)} %collective-permute-done.15.refs_0_), channel_id=1, source_target_pairs={{0,1},{1,0},{2,3},{3,2},{4,5},{5,4},{6,7},{7,6},{8,9},{9,8},{10,11... | collective-permute-start | bytes 344072 | tf_op jit(solution)/shard_map/ppermute | solution.py:519

commit v5 on v4

--- a/solution.py
+++ b/solution.py
@@ -59,14 +59,14 @@
         start -= ref.shape[0]
 
 
-def call(body, out_shape, in_specs):
+def call(body, out_shape, in_specs, work=1):
     return pl.pallas_call(
         body,
         out_shape=out_shape,
         in_specs=in_specs,
         out_specs=jax.tree.map(lambda _: VMEM, out_shape),
         compiler_params=params,
-        cost_estimate=pl.CostEstimate(flops=1, bytes_accessed=1, transcendentals=0),
+        cost_estimate=pl.CostEstimate(flops=work, bytes_accessed=1, transcendentals=0),
     )
 
 
@@ -145,7 +145,7 @@
     )(factor_cols)
 
 
-def project_body(samples_hbm, basis_hbm, order_ref, out_ref, partner_ref, sign_ref, samples_ref, basis_ref, sems):
+def project_body(samples_hbm, basis_hbm, order_ref, mine_ref, theirs_ref, partner_ref, sign_ref, samples_ref, basis_ref, sems):
     width = basis_ref.shape[1]
     lefts, size = fetches(samples_hbm, samples_ref, sems, 0, 1)
     rights, size = fetches(basis_hbm, basis_ref, sems, len(lefts), 0)
@@ -173,7 +173,7 @@
     partner_ref[...] = jnp.where(first, found, found - width)
     sign_ref[...] = jnp.where(first, 1.0, -1.0).astype(f32)
 
-    total = jnp.zeros(out_ref.shape, f32)
+    total = jnp.zeros((samples_ref.shape[0], width), f32)
     for i, (left, right) in enumerate(zip(lefts, rights)):
         left.wait()
         right.wait()
@@ -181,7 +181,10 @@
         right_high, right_low = split(basis_ref[i * size : (i + 1) * size, :])
         both = dot(left_high, jnp.concatenate([right_high, right_low], 1))
         total += both[:, :width] + both[:, width:] + dot(left_low, right_high)
-    out_ref[...] = total
+    half = total.shape[0] // 2
+    first_core = lax.axis_index("rows") % 2 == 0
+    mine_ref[...] = jnp.where(first_core, total[:half], total[half:])
+    theirs_ref[...] = jnp.where(first_core, total[half:], total[:half])
 
 
 def project(samples, basis_cols, order):
@@ -190,12 +193,13 @@
     return pl.pallas_call(
         project_body,
         out_shape=(
-            shape(samples.shape[0], width),
+            shape(samples.shape[0] // 2, width),
+            shape(samples.shape[0] // 2, width),
             shape(lines, width, dtype=i32),
             shape(lines, width),
         ),
         in_specs=[pl.BlockSpec(memory_space=pl.ANY)] * 2 + [VMEM],
-        out_specs=(VMEM, VMEM, VMEM),
+        out_specs=(VMEM, VMEM, VMEM, VMEM),
         scratch_shapes=[
             pltpu.VMEM(samples.shape, f32),
             pltpu.VMEM((rows, width), f32),
@@ -441,8 +445,13 @@
     first = jnp.where(odd, even_gram, odd_gram)
     second = jnp.where(odd, odd_gram, even_gram)
     cross = jnp.where(odd, cross.T, cross)
-    out_ref[:count, :half] = jnp.where(odd, even_samples, odd_samples)
-    out_ref[:count, half:] = jnp.where(odd, odd_samples, even_samples)
+    samples = jnp.concatenate(
+        [jnp.where(odd, even_samples, odd_samples), jnp.where(odd, odd_samples, even_samples)], 1
+    )
+    first_core = lax.axis_index("rows") % 2 == 0
+    out_ref[:count, :] = jnp.where(first_core, samples, 0.0)
+    out_ref[count : 2 * count, :] = jnp.where(first_core, 0.0, samples)
+    count = 2 * count
     out_ref[count : count + half, :half] = first
     out_ref[count : count + half, half:] = cross
     out_ref[count + half : count + half + half // 2, :] = tall(second)
@@ -523,16 +532,18 @@
     width = factor_cols.shape[1]
     packed = factor_cols.shape[0] // 2
     sample_count = samples.shape[0]
-    extra = sample_count // 2
+    extra = sample_count // 4
     rounds, steps = pairing.shape[0], pairing.shape[1]
     final = lax.axis_size("blk") - 1
 
     gram = first_gram(factor_cols)
     paired = gram + flipped(gram, 1)
     pairing, paired = lax.optimization_barrier((pairing, paired))
-    projected, partner, sign = project(samples, basis_cols, pairing.reshape(rounds * steps, width))
-    turn = call(lambda *refs: first_solve_body(rounds, *refs), shape(width, width), [VMEM] * 4)(
-        paired, flipped(paired, 2), partner, sign
+    mine, theirs, partner, sign = project(samples, basis_cols, pairing.reshape(rounds * steps, width))
+    theirs, arrived = lax.optimization_barrier((theirs, flipped(paired, 2)))
+    projected = mine + flipped(theirs, 1)
+    turn = call(lambda *refs: first_solve_body(rounds, *refs), shape(width, width), [VMEM] * 4, 4 * 10**9)(
+        paired, arrived, partner, sign
     )
     first, second = packed * CUT // CHUNKS, packed * (CHUNKS - CUT) // CHUNKS + extra
     pieces = [shape(first, width), shape(second, width)]
@@ -562,7 +573,7 @@
     from_even = via_even(for_even)
     from_odd = via_odd(for_odd, True)
     cross = call(
-        lambda *refs: cross_body(packed, extra, final, *refs), shape(width + 2 * sample_count, width), [VMEM] * 6
+        lambda *refs: cross_body(packed, extra, final, *refs), shape(width + sample_count, width), [VMEM] * 6
     )(*groups[1], cross)
     whole = call(
         lambda *refs: combine_body(final, *refs), shape(width * 3 // 4 + sample_count + 8, width), [VMEM] * 3

time: 95.1 us -> 95.4 us (level)
    ppermute x5, starting transfers between devices: 18.3 us -> 20.2 us  [via_even(): lax.ppermute(value, 'blk', [(i, even_partner(i)) for i in range(count)])]
    ppermute x5, starting transfers between devices: 24.7 us -> 23.4 us  [via_odd(): lax.ppermute(value, 'blk', [pair for pair in pairs if closed or pair[0] !...]
    ppermute x7 -> x8, starting transfers between devices: 7.22 us -> 8.24 us  [flipped(): lax.ppermute(value, 'rows', [(i, i ^ bit) for i in range(lax.axis_size('r...]
    ppermute x7 -> x8, waiting for transfers between devices: 6.11 us -> 5.82 us  [flipped(): lax.ppermute(value, 'rows', [(i, i ^ bit) for i in range(lax.axis_size('r...]
  transfers between devices with their start and end apart: 19 -> 20, of which waited for: 9 -> 9; matrix products, arithmetic and copies ran while one was open for 0% -> 0% of each run, Pallas kernels for 8% -> 10%
where the time goes in v5:
time: 95.4 us; the launch traced here: 95.1 us
  starting transfers between devices  56.2 us (59%)
  waiting for transfers between devices  20.7 us (22%)
  Pallas kernels  17.3 us (18%)
    ppermute x5, starting transfers between devices, via_odd(): lax.ppermute(value, 'blk', [pair for pair in pairs if closed or pair[0] !...  23.4 us
    ppermute x5, starting transfers between devices, via_even(): lax.ppermute(value, 'blk', [(i, even_partner(i)) for i in range(count)])  20.2 us
    ppermute x5, waiting for transfers between devices, via_even(): lax.ppermute(value, 'blk', [(i, even_partner(i)) for i in range(count)])  10.4 us
    ppermute x8, starting transfers between devices, flipped(): lax.ppermute(value, 'rows', [(i, i ^ bit) for i in range(lax.axis_size('r...  8.24 us
    ppermute x8, waiting for transfers between devices, flipped(): lax.ppermute(value, 'rows', [(i, i ^ bit) for i in range(lax.axis_size('r...  5.82 us
    ppermute x2, waiting for transfers between devices, both_chips(): mine = lax.ppermute(value, ('blk', 'rows'), pairs)  4.43 us
    ppermute x2, starting transfers between devices, both_chips(): mine = lax.ppermute(value, ('blk', 'rows'), pairs)  4.42 us
    pallas_call x1, Pallas kernels, on_device(): call(lambda *refs: last_solve_body(rounds, final, *refs), (shape(1, width...  3.28 us
  transfers between devices with their start and end apart: 20, of which 9 were waited for; matrix products, arithmetic and copies ran while one was open for 0% of the time, Pallas kernels for 10%

profile of v5, /device:TPU:33, one launch (start us, length us, event | category | flops | bytes accessed | tf_op | source)
XLA Modules:
  0.0 95.1 jit_solution(5679151367582689832)
XLA Ops:
  0.6 2.3 %shard_map.59 = f32[96,128]{1,0:T(8,128)S(1)} custom-call(f32[4096,128]{1,0:T(8,128)} %refs_0_.1), custom_call_target="tpu_custom_call" | custom-call | tf_op jit(solution)/shard_map/pallas_call | solution.py:135
  3.0 0.8 collective-permute-start
  3.7 0.9 collective-permute-done
  4.6 1.3 %collective-permute-start.1 = (f32[96,128]{1,0:T(8,128)S(1)}, f32[96,128]{1,0:T(8,128)S(1)}, u32[]{:S(2)}, u32[]{:S(2)}) collective-permute-start(f32[96,128]{1,0:T(8,128)S(1)} %add.12.refs_0_), channel_id=1, source_target_pairs={{0,2},{1,3},{2,0},{3,1},{4,6},{5,7},{6,4},{7,5},{8,10},{9,11},{10,... | collective-permute-start | bytes 147464 | tf_op jit(solution)/shard_map/ppermute | solution.py:528
  5.9 2.6 %shard_map.60 = (f32[64,128]{1,0:T(8,128)S(1)}, f32[64,128]{1,0:T(8,128)S(1)}, s32[24,128]{1,0:T(8,128)S(1)}, f32[24,128]{1,0:T(8,128)S(1)}) custom-call(f32[128,4096]{1,0:T(8,128)} %samples_hbm.1, f32[4096,128]{1,0:T(8,128)} %basis_hbm.1, s32[24,128]{1,0:T(8,128)S(1)} %bitcast.3), custom_call_target="tpu_custom_call" | custom-call | tf_op jit(solution)/shard_map/pallas_call | solution.py:193
  8.5 0.0 collective-permute-done.1.refs_1_
  8.5 0.8 collective-permute-start.2
  9.3 2.3 %shard_map.61.refs_2_ = f32[128,128]{1,0:T(8,128)S(1)} custom-call(f32[96,128]{1,0:T(8,128)S(1)} %add.12.refs_0_, f32[96,128]{1,0:T(8,128)S(1)} %collective-permute-done.1.refs_1_, s32[24,128]{1,0:T(8,128)S(1)} %get-tuple-element.27.refs_2_.refs_4_, f32[24,128]{1,0:T(8,128)S(1)} %get-tuple-element.28.refs_3_.refs_5_), custom_call_target="tpu_custom_call" | custom-call | flops 4000000000 | bytes 1 | tf_op jit(solution)/shard_map/pallas_call | solution.py:545
  11.5 0.0 collective-permute-done.2
  11.6 1.2 %shard_map.62 = (f32[1280,128]{1,0:T(8,128)S(1)}, f32[800,128]{1,0:T(8,128)S(1)}, f32[1280,128]{1,0:T(8,128)S(1)}, f32[800,128]{1,0:T(8,128)S(1)}) custom-call(f32[4096,128]{1,0:T(8,128)S(1)} %copy-done, f32[64,128]{1,0:T(8,128)S(1)} %add.13.refs_1_, f32[128,128]{1,0:T(8,128)S(1)} %shard_map.61.refs_2_), custom_call_target="tpu_custom_call" | custom-call | flops 1 | bytes 1 | tf_op jit(solution)/shard_map/pallas_call | solution.py:551
  12.7 1.5 %collective-permute-start.7 = (f32[1280,128]{1,0:T(8,128)S(1)}, f32[1280,128]{1,0:T(8,128)S(1)}, u32[]{:S(2)}, u32[]{:S(2)}) collective-permute-start(f32[1280,128]{1,0:T(8,128)S(1)} %get-tuple-element.31.refs_2_), channel_id=1, source_target_pairs={{0,4},{4,0},{8,12},{12,8},{16,20},{20,16},{24,28},{28,24},{32,36},... | collective-permute-start | bytes 1966088 | tf_op jit(solution)/shard_map/ppermute | solution.py:506
  14.2 3.8 %collective-permute-start.9 = (f32[1280,128]{1,0:T(8,128)S(1)}, f32[1280,128]{1,0:T(8,128)S(1)}, u32[]{:S(2)}, u32[]{:S(2)}) collective-permute-start(f32[1280,128]{1,0:T(8,128)S(1)} %get-tuple-element.35.refs_1_), channel_id=1, source_target_pairs={{0,0},{4,8},{8,4},{12,16},{16,12},{20,24},{24,20},{28,32},{32,28},... | collective-permute-start | bytes 1966088 | tf_op jit(solution)/shard_map/ppermute | solution.py:501
  18.0 0.1 collective-permute-start.3
  18.1 5.5 %collective-permute-start.5 = (f32[800,128]{1,0:T(8,128)S(1)}, f32[800,128]{1,0:T(8,128)S(1)}, u32[]{:S(2)}, u32[]{:S(2)}) collective-permute-start(f32[800,128]{1,0:T(8,128)S(1)} %get-tuple-element.30.refs_1_), channel_id=1, source_target_pairs={{0,0},{4,8},{8,4},{12,16},{16,12},{20,24},{24,20},{28,32},{32,28},... | collective-permute-start | bytes 1228808 | tf_op jit(solution)/shard_map/ppermute | solution.py:501
  23.6 5.6 %collective-permute-done.7.refs_2_.refs_4_ = f32[1280,128]{1,0:T(8,128)S(1)} collective-permute-done((f32[1280,128]{1,0:T(8,128)S(1)}, f32[1280,128]{1,0:T(8,128)S(1)}, u32[]{:S(2)}, u32[]{:S(2)}) %collective-permute-start.7) | collective-permute-done | bytes 655392 | tf_op jit(solution)/shard_map/ppermute | solution.py:506
  29.2 3.8 %collective-permute-start.8 = (f32[1280,128]{1,0:T(8,128)S(1)}, f32[1280,128]{1,0:T(8,128)S(1)}, u32[]{:S(2)}, u32[]{:S(2)}) collective-permute-start(f32[1280,128]{1,0:T(8,128)S(1)} %collective-permute-done.7.refs_2_.refs_4_), channel_id=1, source_target_pairs={{4,8},{8,4},{12,16},{16,12},{20,24},{24,20},{28,32},{32,28},{36,40... | collective-permute-start | bytes 1966088 | tf_op jit(solution)/shard_map/ppermute | solution.py:501
  33.0 0.0 collective-permute-done.9.refs_0_
  33.0 0.1 collective-permute-start.12
  33.1 4.8 %collective-permute-done.3.refs_3_.refs_4_ = f32[800,128]{1,0:T(8,128)S(1)} collective-permute-done((f32[800,128]{1,0:T(8,128)S(1)}, f32[800,128]{1,0:T(8,128)S(1)}, u32[]{:S(2)}, u32[]{:S(2)}) %collective-permute-start.3) | collective-permute-done | bytes 409632 | tf_op jit(solution)/shard_map/ppermute | solution.py:506
  38.0 3.8 %collective-permute-start.4 = (f32[800,128]{1,0:T(8,128)S(1)}, f32[800,128]{1,0:T(8,128)S(1)}, u32[]{:S(2)}, u32[]{:S(2)}) collective-permute-start(f32[800,128]{1,0:T(8,128)S(1)} %collective-permute-done.3.refs_3_.refs_4_), channel_id=1, source_target_pairs={{4,8},{8,4},{12,16},{16,12},{20,24},{24,20},{28,32},{32,28},{36,40... | collective-permute-start | bytes 1228808 | tf_op jit(solution)/shard_map/ppermute | solution.py:501
  41.8 0.0 collective-permute-done.5.refs_1_
  41.8 0.1 collective-permute-start.6
  41.9 1.1 %shard_map.63 = f32[96,128]{1,0:T(8,128)S(1)} custom-call(f32[1280,128]{1,0:T(8,128)S(1)} %collective-permute-done.9.refs_0_, f32[800,128]{1,0:T(8,128)S(1)} %collective-permute-done.5.refs_1_, f32[1280,128]{1,0:T(8,128)S(1)} %collective-permute-done.7.refs_2_.refs_4_, f32[800,128]{1,0:T(8,128)S(1)} %collective-permute-done.3.refs_3_.refs_4_), custom_call_target="tpu_custom_call" | custom-call | flops 1 | bytes 1 | tf_op jit(solution)/shard_map/pallas_call | solution.py:559
  42.9 1.4 %collective-permute-start.10 = (f32[96,128]{1,0:T(8,128)S(1)}, f32[96,128]{1,0:T(8,128)S(1)}, u32[]{:S(2)}, u32[]{:S(2)}) collective-permute-start(f32[96,128]{1,0:T(8,128)S(1)} %shard_map.63), channel_id=1, source_target_pairs={{0,1},{1,0},{2,3},{3,2},{4,5},{5,4},{6,7},{7,6},{8,9},{9,8},{10,11... | collective-permute-start | bytes 147464 | tf_op jit(solution)/shard_map/ppermute | solution.py:528
  44.3 0.9 collective-permute-done.10
  45.2 1.3 %collective-permute-start.11 = (f32[96,128]{1,0:T(8,128)S(1)}, f32[96,128]{1,0:T(8,128)S(1)}, u32[]{:S(2)}, u32[]{:S(2)}) collective-permute-start(f32[96,128]{1,0:T(8,128)S(1)} %add.14.refs_0_), channel_id=1, source_target_pairs={{0,2},{1,3},{2,0},{3,1},{4,6},{5,7},{6,4},{7,5},{8,10},{9,11},{10,... | collective-permute-start | bytes 147464 | tf_op jit(solution)/shard_map/ppermute | solution.py:528
  46.5 2.1 %collective-permute-done.11.refs_1_ = f32[96,128]{1,0:T(8,128)S(1)} collective-permute-done((f32[96,128]{1,0:T(8,128)S(1)}, f32[96,128]{1,0:T(8,128)S(1)}, u32[]{:S(2)}, u32[]{:S(2)}) %collective-permute-start.11) | collective-permute-done | bytes 49184 | tf_op jit(solution)/shard_map/ppermute | solution.py:528
  48.6 2.5 %shard_map.64 = (f32[96,128]{1,0:T(8,128)S(1)}, f32[96,128]{1,0:T(8,128)S(1)}) custom-call(f32[96,128]{1,0:T(8,128)S(1)} %add.14.refs_0_, f32[96,128]{1,0:T(8,128)S(1)} %collective-permute-done.11.refs_1_, s32[24,128]{1,0:T(8,128)S(1)} %get-tuple-element.27.refs_2_.refs_4_, f32[24,128]{1,0:T(8,128)S(1)} %get-tuple-element.28.refs_3_.refs_5_), custom_call_target="tpu_custom_call" | custom-call | flops 1 | bytes 1 | tf_op jit(solution)/shard_map/pallas_call | solution.py:565
  51.1 6.6 %collective-permute-start.13 = (f32[96,128]{1,0:T(8,128)S(1)}, f32[96,128]{1,0:T(8,128)S(1)}, u32[]{:S(2)}, u32[]{:S(2)}) collective-permute-start(f32[96,128]{1,0:T(8,128)S(1)} %get-tuple-element.36), channel_id=1, source_target_pairs={{0,0},{4,8},{8,4},{12,16},{16,12},{20,24},{24,20},{28,32},{32,28},... | collective-permute-start | bytes 147464 | tf_op jit(solution)/shard_map/ppermute | solution.py:501
  57.7 0.0 collective-permute-done.8.refs_0_
  57.7 18.4 %collective-permute-start.14 = (f32[96,128]{1,0:T(8,128)S(1)}, f32[96,128]{1,0:T(8,128)S(1)}, u32[]{:S(2)}, u32[]{:S(2)}) collective-permute-start(f32[96,128]{1,0:T(8,128)S(1)} %get-tuple-element.37), channel_id=1, source_target_pairs={{0,4},{4,0},{8,12},{12,8},{16,20},{20,16},{24,28},{28,24},{32,36},... | collective-permute-start | bytes 147464 | tf_op jit(solution)/shard_map/ppermute | solution.py:506
  76.1 0.0 collective-permute-done.12.refs_3_
  76.1 0.9 shard_map.65.refs_5_
  77.0 0.0 collective-permute-done.4.refs_0_
  77.0 0.0 collective-permute-done.6.refs_3_
  77.0 0.7 shard_map.66.refs_0_
  77.7 0.0 collective-permute-done.13.refs_1_
  77.8 0.5 shard_map.67
  78.3 1.3 %collective-permute-start.15 = (f32[232,128]{1,0:T(8,128)S(1)}, f32[232,128]{1,0:T(8,128)S(1)}, u32[]{:S(2)}, u32[]{:S(2)}) collective-permute-start(f32[232,128]{1,0:T(8,128)S(1)} %shard_map.67), channel_id=1, source_target_pairs={{0,1},{1,0},{2,3},{3,2},{4,5},{5,4},{6,7},{7,6},{8,9},{9,8},{10,11... | collective-permute-start | bytes 356360 | tf_op jit(solution)/shard_map/ppermute | solution.py:528
  79.6 1.0 %collective-permute-done.15 = f32[232,128]{1,0:T(8,128)S(1)} collective-permute-done((f32[232,128]{1,0:T(8,128)S(1)}, f32[232,128]{1,0:T(8,128)S(1)}, u32[]{:S(2)}, u32[]{:S(2)}) %collective-permute-start.15) | collective-permute-done | bytes 118816 | tf_op jit(solution)/shard_map/ppermute | solution.py:528
  80.5 2.5 %collective-permute-start.18 = (f32[232,128]{1,0:T(8,128)S(1)}, f32[232,128]{1,0:T(8,128)S(1)}, u32[]{:S(2)}, u32[]{:S(2)}) collective-permute-start(f32[232,128]{1,0:T(8,128)S(1)} %add.15), channel_id=1, source_target_pairs={{0,4},{1,6},{2,5},{3,7},{4,0},{5,2},{6,1},{7,3},{8,12},{9,14},{10,... | collective-permute-start | bytes 356360 | tf_op jit(solution)/shard_map/ppermute | solution.py:516
  83.1 1.9 %collective-permute-start.16 = (f32[224,128]{1,0:T(8,128)S(1)}, f32[224,128]{1,0:T(8,128)S(1)}, u32[]{:S(2)}, u32[]{:S(2)}) collective-permute-start(f32[224,128]{1,0:T(8,128)S(1)} %slice.4), channel_id=1, source_target_pairs={{0,0},{1,2},{2,1},{3,3},{4,8},{5,10},{6,9},{7,11},{8,4},{9,6},{10,... | collective-permute-start | bytes 344072 | tf_op jit(solution)/shard_map/ppermute | solution.py:516
  85.0 1.3 %collective-permute-done.18.refs_2_ = f32[232,128]{1,0:T(8,128)S(1)} collective-permute-done((f32[232,128]{1,0:T(8,128)S(1)}, f32[232,128]{1,0:T(8,128)S(1)}, u32[]{:S(2)}, u32[]{:S(2)}) %collective-permute-start.18) | collective-permute-done | bytes 118816 | tf_op jit(solution)/shard_map/ppermute | solution.py:516
  86.3 0.7 collective-permute-start.19
  87.0 3.1 %collective-permute-done.16.refs_0_ = f32[224,128]{1,0:T(8,128)S(1)} collective-permute-done((f32[224,128]{1,0:T(8,128)S(1)}, f32[224,128]{1,0:T(8,128)S(1)}, u32[]{:S(2)}, u32[]{:S(2)}) %collective-permute-start.16) | collective-permute-done | bytes 114720 | tf_op jit(solution)/shard_map/ppermute | solution.py:516
  90.1 0.8 collective-permute-start.17
  90.9 1.0 %collective-permute-done.17.refs_1_ = f32[224,128]{1,0:T(8,128)S(1)} collective-permute-done((f32[224,128]{1,0:T(8,128)S(1)}, f32[224,128]{1,0:T(8,128)S(1)}, u32[]{:S(2)}, u32[]{:S(2)}) %collective-permute-start.17) | collective-permute-done | bytes 114720 | tf_op jit(solution)/shard_map/ppermute | solution.py:528
  91.8 3.3 %shard_map.68 = (f32[1,128]{1,0:T(1,128)}, f32[1,128]{1,0:T(1,128)}) custom-call(f32[224,128]{1,0:T(8,128)S(1)} %collective-permute-done.16.refs_0_, f32[224,128]{1,0:T(8,128)S(1)} %collective-permute-done.17.refs_1_, f32[232,128]{1,0:T(8,128)S(1)} %collective-permute-done.18.refs_2_, f32[232,128]{1,0:T(8,128)S(1)} %collective-permute-done.19.refs_3_, ...), custom_call_target="tpu_custom_call" | custom-call | flops 1 | bytes 1 | tf_op jit(solution)/shard_map/pallas_call | solution.py:582
  (11 shorter events, 0.1 us)
Async XLA Ops:
  0.6 5.3 %copy-start.1 = (s32[3,8,128]{2,1,0:T(8,128)S(1)}, s32[3,8,128]{2,1,0:T(8,128)}, u32[]{:S(2)}) copy-start(s32[3,8,128]{2,1,0:T(8,128)} %param.7) | copy-start | bytes 36868
  3.0 1.6 %collective-permute-start = (f32[96,128]{1,0:T(8,128)S(1)}, f32[96,128]{1,0:T(8,128)S(1)}, u32[]{:S(2)}, u32[]{:S(2)}) collective-permute-start(f32[96,128]{1,0:T(8,128)S(1)} %shard_map.59), channel_id=1, source_target_pairs={{0,1},{1,0},{2,3},{3,2},{4,5},{5,4},{6,7},{7,6},{8,9},{9,8},{10,11... | collective-permute-start | bytes 147464 | tf_op jit(solution)/shard_map/ppermute | solution.py:528
  4.6 3.9 %collective-permute-start.1 = (f32[96,128]{1,0:T(8,128)S(1)}, f32[96,128]{1,0:T(8,128)S(1)}, u32[]{:S(2)}, u32[]{:S(2)}) collective-permute-start(f32[96,128]{1,0:T(8,128)S(1)} %add.12.refs_0_), channel_id=1, source_target_pairs={{0,2},{1,3},{2,0},{3,1},{4,6},{5,7},{6,4},{7,5},{8,10},{9,11},{10,... | collective-permute-start | bytes 147464 | tf_op jit(solution)/shard_map/ppermute | solution.py:528
  8.5 3.1 %collective-permute-start.2 = (f32[64,128]{1,0:T(8,128)S(1)}, f32[64,128]{1,0:T(8,128)S(1)}, u32[]{:S(2)}, u32[]{:S(2)}) collective-permute-start(f32[64,128]{1,0:T(8,128)S(1)} %get-tuple-element.25), channel_id=1, source_target_pairs={{0,1},{1,0},{2,3},{3,2},{4,5},{5,4},{6,7},{7,6},{8,9},{9,8},{10,11... | collective-permute-start | bytes 98312 | tf_op jit(solution)/shard_map/ppermute | solution.py:528
  9.3 2.3 %copy-start = (f32[4096,128]{1,0:T(8,128)S(1)}, f32[4096,128]{1,0:T(8,128)}, u32[]{:S(2)}) copy-start(f32[4096,128]{1,0:T(8,128)} %refs_0_.1) | copy-start | bytes 6291460
  12.7 16.4 %collective-permute-start.7 = (f32[1280,128]{1,0:T(8,128)S(1)}, f32[1280,128]{1,0:T(8,128)S(1)}, u32[]{:S(2)}, u32[]{:S(2)}) collective-permute-start(f32[1280,128]{1,0:T(8,128)S(1)} %get-tuple-element.31.refs_2_), channel_id=1, source_target_pairs={{0,4},{4,0},{8,12},{12,8},{16,20},{20,16},{24,28},{28,24},{32,36},... | collective-permute-start | bytes 1966088 | tf_op jit(solution)/shard_map/ppermute | solution.py:506
  14.2 18.7 %collective-permute-start.9 = (f32[1280,128]{1,0:T(8,128)S(1)}, f32[1280,128]{1,0:T(8,128)S(1)}, u32[]{:S(2)}, u32[]{:S(2)}) collective-permute-start(f32[1280,128]{1,0:T(8,128)S(1)} %get-tuple-element.35.refs_1_), channel_id=1, source_target_pairs={{0,0},{4,8},{8,4},{12,16},{16,12},{20,24},{24,20},{28,32},{32,28},... | collective-permute-start | bytes 1966088 | tf_op jit(solution)/shard_map/ppermute | solution.py:501
  18.0 19.9 %collective-permute-start.3 = (f32[800,128]{1,0:T(8,128)S(1)}, f32[800,128]{1,0:T(8,128)S(1)}, u32[]{:S(2)}, u32[]{:S(2)}) collective-permute-start(f32[800,128]{1,0:T(8,128)S(1)} %get-tuple-element.29.refs_2_), channel_id=1, source_target_pairs={{0,4},{4,0},{8,12},{12,8},{16,20},{20,16},{24,28},{28,24},{32,36},... | collective-permute-start | bytes 1228808 | tf_op jit(solution)/shard_map/ppermute | solution.py:506
  18.1 23.7 %collective-permute-start.5 = (f32[800,128]{1,0:T(8,128)S(1)}, f32[800,128]{1,0:T(8,128)S(1)}, u32[]{:S(2)}, u32[]{:S(2)}) collective-permute-start(f32[800,128]{1,0:T(8,128)S(1)} %get-tuple-element.30.refs_1_), channel_id=1, source_target_pairs={{0,0},{4,8},{8,4},{12,16},{16,12},{20,24},{24,20},{28,32},{32,28},... | collective-permute-start | bytes 1228808 | tf_op jit(solution)/shard_map/ppermute | solution.py:501
  29.2 28.6 %collective-permute-start.8 = (f32[1280,128]{1,0:T(8,128)S(1)}, f32[1280,128]{1,0:T(8,128)S(1)}, u32[]{:S(2)}, u32[]{:S(2)}) collective-permute-start(f32[1280,128]{1,0:T(8,128)S(1)} %collective-permute-done.7.refs_2_.refs_4_), channel_id=1, source_target_pairs={{4,8},{8,4},{12,16},{16,12},{20,24},{24,20},{28,32},{32,28},{36,40... | collective-permute-start | bytes 1966088 | tf_op jit(solution)/shard_map/ppermute | solution.py:501
  33.0 43.1 %collective-permute-start.12 = (f32[1280,128]{1,0:T(8,128)S(1)}, f32[1280,128]{1,0:T(8,128)S(1)}, u32[]{:S(2)}, u32[]{:S(2)}) collective-permute-start(f32[1280,128]{1,0:T(8,128)S(1)} %collective-permute-done.9.refs_0_), channel_id=1, source_target_pairs={{0,4},{4,0},{8,12},{12,8},{16,20},{20,16},{24,28},{28,24},{32,36},... | collective-permute-start | bytes 1966088 | tf_op jit(solution)/shard_map/ppermute | solution.py:506
  38.0 39.1 %collective-permute-start.4 = (f32[800,128]{1,0:T(8,128)S(1)}, f32[800,128]{1,0:T(8,128)S(1)}, u32[]{:S(2)}, u32[]{:S(2)}) collective-permute-start(f32[800,128]{1,0:T(8,128)S(1)} %collective-permute-done.3.refs_3_.refs_4_), channel_id=1, source_target_pairs={{4,8},{8,4},{12,16},{16,12},{20,24},{24,20},{28,32},{32,28},{36,40... | collective-permute-start | bytes 1228808 | tf_op jit(solution)/shard_map/ppermute | solution.py:501
  41.8 35.3 %collective-permute-start.6 = (f32[800,128]{1,0:T(8,128)S(1)}, f32[800,128]{1,0:T(8,128)S(1)}, u32[]{:S(2)}, u32[]{:S(2)}) collective-permute-start(f32[800,128]{1,0:T(8,128)S(1)} %collective-permute-done.5.refs_1_), channel_id=1, source_target_pairs={{0,4},{4,0},{8,12},{12,8},{16,20},{20,16},{24,28},{28,24},{32,36},... | collective-permute-start | bytes 1228808 | tf_op jit(solution)/shard_map/ppermute | solution.py:506
  42.9 2.2 %collective-permute-start.10 = (f32[96,128]{1,0:T(8,128)S(1)}, f32[96,128]{1,0:T(8,128)S(1)}, u32[]{:S(2)}, u32[]{:S(2)}) collective-permute-start(f32[96,128]{1,0:T(8,128)S(1)} %shard_map.63), channel_id=1, source_target_pairs={{0,1},{1,0},{2,3},{3,2},{4,5},{5,4},{6,7},{7,6},{8,9},{9,8},{10,11... | collective-permute-start | bytes 147464 | tf_op jit(solution)/shard_map/ppermute | solution.py:528
  45.2 3.4 %collective-permute-start.11 = (f32[96,128]{1,0:T(8,128)S(1)}, f32[96,128]{1,0:T(8,128)S(1)}, u32[]{:S(2)}, u32[]{:S(2)}) collective-permute-start(f32[96,128]{1,0:T(8,128)S(1)} %add.14.refs_0_), channel_id=1, source_target_pairs={{0,2},{1,3},{2,0},{3,1},{4,6},{5,7},{6,4},{7,5},{8,10},{9,11},{10,... | collective-permute-start | bytes 147464 | tf_op jit(solution)/shard_map/ppermute | solution.py:528
  51.1 26.6 %collective-permute-start.13 = (f32[96,128]{1,0:T(8,128)S(1)}, f32[96,128]{1,0:T(8,128)S(1)}, u32[]{:S(2)}, u32[]{:S(2)}) collective-permute-start(f32[96,128]{1,0:T(8,128)S(1)} %get-tuple-element.36), channel_id=1, source_target_pairs={{0,0},{4,8},{8,4},{12,16},{16,12},{20,24},{24,20},{28,32},{32,28},... | collective-permute-start | bytes 147464 | tf_op jit(solution)/shard_map/ppermute | solution.py:501
  57.7 20.0 %collective-permute-start.14 = (f32[96,128]{1,0:T(8,128)S(1)}, f32[96,128]{1,0:T(8,128)S(1)}, u32[]{:S(2)}, u32[]{:S(2)}) collective-permute-start(f32[96,128]{1,0:T(8,128)S(1)} %get-tuple-element.37), channel_id=1, source_target_pairs={{0,4},{4,0},{8,12},{12,8},{16,20},{20,16},{24,28},{28,24},{32,36},... | collective-permute-start | bytes 147464 | tf_op jit(solution)/shard_map/ppermute | solution.py:506
  78.3 2.2 %collective-permute-start.15 = (f32[232,128]{1,0:T(8,128)S(1)}, f32[232,128]{1,0:T(8,128)S(1)}, u32[]{:S(2)}, u32[]{:S(2)}) collective-permute-start(f32[232,128]{1,0:T(8,128)S(1)} %shard_map.67), channel_id=1, source_target_pairs={{0,1},{1,0},{2,3},{3,2},{4,5},{5,4},{6,7},{7,6},{8,9},{9,8},{10,11... | collective-permute-start | bytes 356360 | tf_op jit(solution)/shard_map/ppermute | solution.py:528
  80.5 5.8 %collective-permute-start.18 = (f32[232,128]{1,0:T(8,128)S(1)}, f32[232,128]{1,0:T(8,128)S(1)}, u32[]{:S(2)}, u32[]{:S(2)}) collective-permute-start(f32[232,128]{1,0:T(8,128)S(1)} %add.15), channel_id=1, source_target_pairs={{0,4},{1,6},{2,5},{3,7},{4,0},{5,2},{6,1},{7,3},{8,12},{9,14},{10,... | collective-permute-start | bytes 356360 | tf_op jit(solution)/shard_map/ppermute | solution.py:516
  83.1 7.0 %collective-permute-start.16 = (f32[224,128]{1,0:T(8,128)S(1)}, f32[224,128]{1,0:T(8,128)S(1)}, u32[]{:S(2)}, u32[]{:S(2)}) collective-permute-start(f32[224,128]{1,0:T(8,128)S(1)} %slice.4), channel_id=1, source_target_pairs={{0,0},{1,2},{2,1},{3,3},{4,8},{5,10},{6,9},{7,11},{8,4},{9,6},{10,... | collective-permute-start | bytes 344072 | tf_op jit(solution)/shard_map/ppermute | solution.py:516
  86.3 5.5 %collective-permute-start.19 = (f32[232,128]{1,0:T(8,128)S(1)}, f32[232,128]{1,0:T(8,128)S(1)}, u32[]{:S(2)}, u32[]{:S(2)}) collective-permute-start(f32[232,128]{1,0:T(8,128)S(1)} %collective-permute-done.18.refs_2_), channel_id=1, source_target_pairs={{0,1},{1,0},{2,3},{3,2},{4,5},{5,4},{6,7},{7,6},{8,9},{9,8},{10,11... | collective-permute-start | bytes 356360 | tf_op jit(solution)/shard_map/ppermute | solution.py:528
  90.1 1.8 %collective-permute-start.17 = (f32[224,128]{1,0:T(8,128)S(1)}, f32[224,128]{1,0:T(8,128)S(1)}, u32[]{:S(2)}, u32[]{:S(2)}) collective-permute-start(f32[224,128]{1,0:T(8,128)S(1)} %collective-permute-done.16.refs_0_), channel_id=1, source_target_pairs={{0,1},{1,0},{2,3},{3,2},{4,5},{5,4},{6,7},{7,6},{8,9},{9,8},{10,11... | collective-permute-start | bytes 344072 | tf_op jit(solution)/shard_map/ppermute | solution.py:528

commit v6 on v4

--- a/solution.py
+++ b/solution.py
@@ -246,7 +246,10 @@
     cosine = jnp.where(ahead, major, minor)
     sine = jnp.where(ahead, minor, major)
     sine = jnp.where(slope < 0.0, -sine, sine) * sign
-    carried = scaled(carried, cosine) + scaled(lanes(carried, index), sine)
+    if carried is None:
+        carried = scaled(jnp.where(eye, 1.0, 0.0), cosine) + scaled(jnp.where(facing, 1.0, 0.0), sine)
+    else:
+        carried = scaled(carried, cosine) + scaled(lanes(carried, index), sine)
     if last == "turn":
         return None, carried
     if last == "sums":
@@ -299,7 +302,7 @@
 def first_solve_body(rounds, own_ref, other_ref, partner_ref, sign_ref, turn_ref):
     gram = unpacked_gram(own_ref[...] + other_ref[...])
     ((_, turn_ref[...]),) = solve(
-        [(gram, identity_of(gram.shape[0]))],
+        [(gram, None)],
         round_of(partner_ref, 0, rounds),
         round_of(sign_ref, 0, rounds),
         "turn",
@@ -373,7 +376,7 @@
     width = gram.shape[0]
     half = width // 2
     ((settled, turn),) = solve(
-        [(gram, identity_of(width))], round_of(partner_ref, 1, rounds), round_of(sign_ref, 1, rounds)
+        [(gram, None)], round_of(partner_ref, 1, rounds), round_of(sign_ref, 1, rounds)
     )
     top = jnp.concatenate([tall(turn[:, :half]), tall(settled[:half, :half])], 0)
     bottom = jnp.concatenate([tall(turn[:, half:]), tall(settled[half:, half:])], 0)

time: 95.1 us -> 95.1 us (level)
  no operation moved by 1% of the time
where the time goes in v6:
time: 95.1 us; the launch traced here: 94.8 us
  starting transfers between devices  55.3 us (58%)
  waiting for transfers between devices  21.1 us (22%)
  Pallas kernels  17.4 us (18%)
    ppermute x5, starting transfers between devices, via_odd(): lax.ppermute(value, 'blk', [pair for pair in pairs if closed or pair[0] !...  24.6 us
    ppermute x5, starting transfers between devices, via_even(): lax.ppermute(value, 'blk', [(i, even_partner(i)) for i in range(count)])  18.3 us
    ppermute x5, waiting for transfers between devices, via_even(): lax.ppermute(value, 'blk', [(i, even_partner(i)) for i in range(count)])  9.91 us
    ppermute x7, starting transfers between devices, flipped(): lax.ppermute(value, 'rows', [(i, i ^ bit) for i in range(lax.axis_size('r...  7.23 us
    ppermute x7, waiting for transfers between devices, flipped(): lax.ppermute(value, 'rows', [(i, i ^ bit) for i in range(lax.axis_size('r...  6.13 us
    ppermute x2, starting transfers between devices, both_chips(): mine = lax.ppermute(value, ('blk', 'rows'), pairs)  5.19 us
    ppermute x2, waiting for transfers between devices, both_chips(): mine = lax.ppermute(value, ('blk', 'rows'), pairs)  5.08 us
    pallas_call x1, Pallas kernels, on_device(): call(lambda *refs: last_solve_body(rounds, final, *refs), (shape(1, width...  3.28 us
  transfers between devices with their start and end apart: 19, of which 9 were waited for; matrix products, arithmetic and copies ran while one was open for 0% of the time, Pallas kernels for 8%

profile of v6, /device:TPU:33, one launch (start us, length us, event | category | flops | bytes accessed | tf_op | source)
XLA Modules:
  0.0 94.8 jit_solution(13452895991014468591)
XLA Ops:
  0.6 2.3 %shard_map.59 = f32[96,128]{1,0:T(8,128)S(1)} custom-call(f32[4096,128]{1,0:T(8,128)} %refs_0_.1), custom_call_target="tpu_custom_call" | custom-call | tf_op jit(solution)/shard_map/pallas_call | solution.py:135
  3.0 0.8 collective-permute-start
  3.7 0.9 collective-permute-done
  4.6 1.3 %collective-permute-start.1 = (f32[96,128]{1,0:T(8,128)S(1)}, f32[96,128]{1,0:T(8,128)S(1)}, u32[]{:S(2)}, u32[]{:S(2)}) collective-permute-start(f32[96,128]{1,0:T(8,128)S(1)} %add.9.refs_0_), channel_id=1, source_target_pairs={{0,2},{1,3},{2,0},{3,1},{4,6},{5,7},{6,4},{7,5},{8,10},{9,11},{10,... | collective-permute-start | bytes 147464 | tf_op jit(solution)/shard_map/ppermute | solution.py:522
  5.9 2.7 %shard_map.60 = (f32[128,128]{1,0:T(8,128)S(1)}, s32[24,128]{1,0:T(8,128)S(1)}, f32[24,128]{1,0:T(8,128)S(1)}) custom-call(f32[128,4096]{1,0:T(8,128)} %samples_hbm.1, f32[4096,128]{1,0:T(8,128)} %basis_hbm.1, s32[24,128]{1,0:T(8,128)S(1)} %bitcast.3), custom_call_target="tpu_custom_call" | custom-call | tf_op jit(solution)/shard_map/pallas_call | solution.py:190
  8.6 0.0 collective-permute-done.1.refs_1_
  8.6 2.3 %shard_map.61.refs_2_ = f32[128,128]{1,0:T(8,128)S(1)} custom-call(f32[96,128]{1,0:T(8,128)S(1)} %add.9.refs_0_, f32[96,128]{1,0:T(8,128)S(1)} %collective-permute-done.1.refs_1_, s32[24,128]{1,0:T(8,128)S(1)} %get-tuple-element.21.refs_2_.refs_4_, f32[24,128]{1,0:T(8,128)S(1)} %get-tuple-element.22.refs_3_.refs_5_), custom_call_target="tpu_custom_call" | custom-call | flops 1 | bytes 1 | tf_op jit(solution)/shard_map/pallas_call | solution.py:537
  10.9 1.2 %shard_map.62 = (f32[1280,128]{1,0:T(8,128)S(1)}, f32[832,128]{1,0:T(8,128)S(1)}, f32[1280,128]{1,0:T(8,128)S(1)}, f32[832,128]{1,0:T(8,128)S(1)}) custom-call(f32[4096,128]{1,0:T(8,128)S(1)} %copy-done, f32[128,128]{1,0:T(8,128)S(1)} %get-tuple-element.19.refs_1_, f32[128,128]{1,0:T(8,128)S(1)} %shard_map.61.refs_2_), custom_call_target="tpu_custom_call" | custom-call | flops 1 | bytes 1 | tf_op jit(solution)/shard_map/pallas_call | solution.py:543
  12.1 0.6 collective-permute-start.6
  12.7 4.7 %collective-permute-start.8 = (f32[1280,128]{1,0:T(8,128)S(1)}, f32[1280,128]{1,0:T(8,128)S(1)}, u32[]{:S(2)}, u32[]{:S(2)}) collective-permute-start(f32[1280,128]{1,0:T(8,128)S(1)} %get-tuple-element.29.refs_1_), channel_id=1, source_target_pairs={{0,0},{4,8},{8,4},{12,16},{16,12},{20,24},{24,20},{28,32},{32,28},... | collective-permute-start | bytes 1966088 | tf_op jit(solution)/shard_map/ppermute | solution.py:495
  17.4 0.1 collective-permute-start.2
  17.5 5.5 %collective-permute-start.4 = (f32[832,128]{1,0:T(8,128)S(1)}, f32[832,128]{1,0:T(8,128)S(1)}, u32[]{:S(2)}, u32[]{:S(2)}) collective-permute-start(f32[832,128]{1,0:T(8,128)S(1)} %get-tuple-element.24.refs_1_), channel_id=1, source_target_pairs={{0,0},{4,8},{8,4},{12,16},{16,12},{20,24},{24,20},{28,32},{32,28},... | collective-permute-start | bytes 1277960 | tf_op jit(solution)/shard_map/ppermute | solution.py:495
  22.9 4.8 %collective-permute-done.6.refs_2_.refs_4_ = f32[1280,128]{1,0:T(8,128)S(1)} collective-permute-done((f32[1280,128]{1,0:T(8,128)S(1)}, f32[1280,128]{1,0:T(8,128)S(1)}, u32[]{:S(2)}, u32[]{:S(2)}) %collective-permute-start.6) | collective-permute-done | bytes 655392 | tf_op jit(solution)/shard_map/ppermute | solution.py:500
  27.7 3.9 %collective-permute-start.7 = (f32[1280,128]{1,0:T(8,128)S(1)}, f32[1280,128]{1,0:T(8,128)S(1)}, u32[]{:S(2)}, u32[]{:S(2)}) collective-permute-start(f32[1280,128]{1,0:T(8,128)S(1)} %collective-permute-done.6.refs_2_.refs_4_), channel_id=1, source_target_pairs={{4,8},{8,4},{12,16},{16,12},{20,24},{24,20},{28,32},{32,28},{36,40... | collective-permute-start | bytes 1966088 | tf_op jit(solution)/shard_map/ppermute | solution.py:495
  31.7 0.0 collective-permute-done.8.refs_0_
  31.7 0.1 collective-permute-start.11
  31.8 5.1 %collective-permute-done.2.refs_3_.refs_4_ = f32[832,128]{1,0:T(8,128)S(1)} collective-permute-done((f32[832,128]{1,0:T(8,128)S(1)}, f32[832,128]{1,0:T(8,128)S(1)}, u32[]{:S(2)}, u32[]{:S(2)}) %collective-permute-start.2) | collective-permute-done | bytes 426016 | tf_op jit(solution)/shard_map/ppermute | solution.py:500
  36.9 3.9 %collective-permute-start.3 = (f32[832,128]{1,0:T(8,128)S(1)}, f32[832,128]{1,0:T(8,128)S(1)}, u32[]{:S(2)}, u32[]{:S(2)}) collective-permute-start(f32[832,128]{1,0:T(8,128)S(1)} %collective-permute-done.2.refs_3_.refs_4_), channel_id=1, source_target_pairs={{4,8},{8,4},{12,16},{16,12},{20,24},{24,20},{28,32},{32,28},{36,40... | collective-permute-start | bytes 1277960 | tf_op jit(solution)/shard_map/ppermute | solution.py:495
  40.8 0.0 collective-permute-done.4.refs_1_
  40.8 0.1 collective-permute-start.5
  40.9 1.1 %shard_map.63 = f32[96,128]{1,0:T(8,128)S(1)} custom-call(f32[1280,128]{1,0:T(8,128)S(1)} %collective-permute-done.8.refs_0_, f32[832,128]{1,0:T(8,128)S(1)} %collective-permute-done.4.refs_1_, f32[1280,128]{1,0:T(8,128)S(1)} %collective-permute-done.6.refs_2_.refs_4_, f32[832,128]{1,0:T(8,128)S(1)} %collective-permute-done.2.refs_3_.refs_4_), custom_call_target="tpu_custom_call" | custom-call | flops 1 | bytes 1 | tf_op jit(solution)/shard_map/pallas_call | solution.py:551
  42.0 2.7 %collective-permute-start.9 = (f32[96,128]{1,0:T(8,128)S(1)}, f32[96,128]{1,0:T(8,128)S(1)}, u32[]{:S(2)}, u32[]{:S(2)}) collective-permute-start(f32[96,128]{1,0:T(8,128)S(1)} %shard_map.63), channel_id=1, source_target_pairs={{0,1},{1,0},{2,3},{3,2},{4,5},{5,4},{6,7},{7,6},{8,9},{9,8},{10,11... | collective-permute-start | bytes 147464 | tf_op jit(solution)/shard_map/ppermute | solution.py:522
  44.7 0.9 collective-permute-done.9
  45.6 1.2 %collective-permute-start.10 = (f32[96,128]{1,0:T(8,128)S(1)}, f32[96,128]{1,0:T(8,128)S(1)}, u32[]{:S(2)}, u32[]{:S(2)}) collective-permute-start(f32[96,128]{1,0:T(8,128)S(1)} %add.10.refs_0_), channel_id=1, source_target_pairs={{0,2},{1,3},{2,0},{3,1},{4,6},{5,7},{6,4},{7,5},{8,10},{9,11},{10,... | collective-permute-start | bytes 147464 | tf_op jit(solution)/shard_map/ppermute | solution.py:522
  46.7 2.1 %collective-permute-done.10.refs_1_ = f32[96,128]{1,0:T(8,128)S(1)} collective-permute-done((f32[96,128]{1,0:T(8,128)S(1)}, f32[96,128]{1,0:T(8,128)S(1)}, u32[]{:S(2)}, u32[]{:S(2)}) %collective-permute-start.10) | collective-permute-done | bytes 49184 | tf_op jit(solution)/shard_map/ppermute | solution.py:522
  48.8 2.5 %shard_map.64 = (f32[96,128]{1,0:T(8,128)S(1)}, f32[96,128]{1,0:T(8,128)S(1)}) custom-call(f32[96,128]{1,0:T(8,128)S(1)} %add.10.refs_0_, f32[96,128]{1,0:T(8,128)S(1)} %collective-permute-done.10.refs_1_, s32[24,128]{1,0:T(8,128)S(1)} %get-tuple-element.21.refs_2_.refs_4_, f32[24,128]{1,0:T(8,128)S(1)} %get-tuple-element.22.refs_3_.refs_5_), custom_call_target="tpu_custom_call" | custom-call | flops 1 | bytes 1 | tf_op jit(solution)/shard_map/pallas_call | solution.py:557
  51.3 6.7 %collective-permute-start.12 = (f32[96,128]{1,0:T(8,128)S(1)}, f32[96,128]{1,0:T(8,128)S(1)}, u32[]{:S(2)}, u32[]{:S(2)}) collective-permute-start(f32[96,128]{1,0:T(8,128)S(1)} %get-tuple-element.30), channel_id=1, source_target_pairs={{0,0},{4,8},{8,4},{12,16},{16,12},{20,24},{24,20},{28,32},{32,28},... | collective-permute-start | bytes 147464 | tf_op jit(solution)/shard_map/ppermute | solution.py:495
  58.0 0.0 collective-permute-done.7.refs_0_
  58.0 17.4 %collective-permute-start.13 = (f32[96,128]{1,0:T(8,128)S(1)}, f32[96,128]{1,0:T(8,128)S(1)}, u32[]{:S(2)}, u32[]{:S(2)}) collective-permute-start(f32[96,128]{1,0:T(8,128)S(1)} %get-tuple-element.31), channel_id=1, source_target_pairs={{0,4},{4,0},{8,12},{12,8},{16,20},{20,16},{24,28},{28,24},{32,36},... | collective-permute-start | bytes 147464 | tf_op jit(solution)/shard_map/ppermute | solution.py:500
  75.4 0.0 collective-permute-done.11.refs_3_
  75.4 0.9 shard_map.65.refs_5_
  76.3 0.0 collective-permute-done.3.refs_0_
  76.3 0.0 collective-permute-done.5.refs_3_
  76.3 0.7 shard_map.66.refs_0_
  77.0 0.0 collective-permute-done.12.refs_1_
  77.0 0.0 collective-permute-done.13.refs_2_
  77.1 0.6 shard_map.67
  77.6 1.3 %collective-permute-start.14 = (f32[232,128]{1,0:T(8,128)S(1)}, f32[232,128]{1,0:T(8,128)S(1)}, u32[]{:S(2)}, u32[]{:S(2)}) collective-permute-start(f32[232,128]{1,0:T(8,128)S(1)} %shard_map.67), channel_id=1, source_target_pairs={{0,1},{1,0},{2,3},{3,2},{4,5},{5,4},{6,7},{7,6},{8,9},{9,8},{10,11... | collective-permute-start | bytes 356360 | tf_op jit(solution)/shard_map/ppermute | solution.py:522
  78.9 1.0 %collective-permute-done.14 = f32[232,128]{1,0:T(8,128)S(1)} collective-permute-done((f32[232,128]{1,0:T(8,128)S(1)}, f32[232,128]{1,0:T(8,128)S(1)}, u32[]{:S(2)}, u32[]{:S(2)}) %collective-permute-start.14) | collective-permute-done | bytes 118816 | tf_op jit(solution)/shard_map/ppermute | solution.py:522
  79.9 3.3 %collective-permute-start.17 = (f32[232,128]{1,0:T(8,128)S(1)}, f32[232,128]{1,0:T(8,128)S(1)}, u32[]{:S(2)}, u32[]{:S(2)}) collective-permute-start(f32[232,128]{1,0:T(8,128)S(1)} %add.11), channel_id=1, source_target_pairs={{0,4},{1,6},{2,5},{3,7},{4,0},{5,2},{6,1},{7,3},{8,12},{9,14},{10,... | collective-permute-start | bytes 356360 | tf_op jit(solution)/shard_map/ppermute | solution.py:510
  83.2 1.9 %collective-permute-start.15 = (f32[224,128]{1,0:T(8,128)S(1)}, f32[224,128]{1,0:T(8,128)S(1)}, u32[]{:S(2)}, u32[]{:S(2)}) collective-permute-start(f32[224,128]{1,0:T(8,128)S(1)} %slice.4), channel_id=1, source_target_pairs={{0,0},{1,2},{2,1},{3,3},{4,8},{5,10},{6,9},{7,11},{8,4},{9,6},{10,... | collective-permute-start | bytes 344072 | tf_op jit(solution)/shard_map/ppermute | solution.py:510
  85.1 1.3 %collective-permute-done.17.refs_2_ = f32[232,128]{1,0:T(8,128)S(1)} collective-permute-done((f32[232,128]{1,0:T(8,128)S(1)}, f32[232,128]{1,0:T(8,128)S(1)}, u32[]{:S(2)}, u32[]{:S(2)}) %collective-permute-start.17) | collective-permute-done | bytes 118816 | tf_op jit(solution)/shard_map/ppermute | solution.py:510
  86.4 0.0 collective-permute-start.18
  86.4 3.8 %collective-permute-done.15.refs_0_ = f32[224,128]{1,0:T(8,128)S(1)} collective-permute-done((f32[224,128]{1,0:T(8,128)S(1)}, f32[224,128]{1,0:T(8,128)S(1)}, u32[]{:S(2)}, u32[]{:S(2)}) %collective-permute-start.15) | collective-permute-done | bytes 114720 | tf_op jit(solution)/shard_map/ppermute | solution.py:510
  90.2 0.0 collective-permute-start.16
  90.2 1.3 %collective-permute-done.16.refs_1_ = f32[224,128]{1,0:T(8,128)S(1)} collective-permute-done((f32[224,128]{1,0:T(8,128)S(1)}, f32[224,128]{1,0:T(8,128)S(1)}, u32[]{:S(2)}, u32[]{:S(2)}) %collective-permute-start.16) | collective-permute-done | bytes 114720 | tf_op jit(solution)/shard_map/ppermute | solution.py:522
  91.5 0.0 collective-permute-done.18.refs_3_
  91.5 3.3 %shard_map.68 = (f32[1,128]{1,0:T(1,128)}, f32[1,128]{1,0:T(1,128)}) custom-call(f32[224,128]{1,0:T(8,128)S(1)} %collective-permute-done.15.refs_0_, f32[224,128]{1,0:T(8,128)S(1)} %collective-permute-done.16.refs_1_, f32[232,128]{1,0:T(8,128)S(1)} %collective-permute-done.17.refs_2_, f32[232,128]{1,0:T(8,128)S(1)} %collective-permute-done.18.refs_3_, ...), custom_call_target="tpu_custom_call" | custom-call | flops 1 | bytes 1 | tf_op jit(solution)/shard_map/pallas_call | solution.py:574
  (8 shorter events, 0.1 us)
Async XLA Ops:
  0.6 5.3 %copy-start.1 = (s32[3,8,128]{2,1,0:T(8,128)S(1)}, s32[3,8,128]{2,1,0:T(8,128)}, u32[]{:S(2)}) copy-start(s32[3,8,128]{2,1,0:T(8,128)} %param.7) | copy-start | bytes 36868
  3.0 1.6 %collective-permute-start = (f32[96,128]{1,0:T(8,128)S(1)}, f32[96,128]{1,0:T(8,128)S(1)}, u32[]{:S(2)}, u32[]{:S(2)}) collective-permute-start(f32[96,128]{1,0:T(8,128)S(1)} %shard_map.59), channel_id=1, source_target_pairs={{0,1},{1,0},{2,3},{3,2},{4,5},{5,4},{6,7},{7,6},{8,9},{9,8},{10,11... | collective-permute-start | bytes 147464 | tf_op jit(solution)/shard_map/ppermute | solution.py:522
  4.6 4.0 %collective-permute-start.1 = (f32[96,128]{1,0:T(8,128)S(1)}, f32[96,128]{1,0:T(8,128)S(1)}, u32[]{:S(2)}, u32[]{:S(2)}) collective-permute-start(f32[96,128]{1,0:T(8,128)S(1)} %add.9.refs_0_), channel_id=1, source_target_pairs={{0,2},{1,3},{2,0},{3,1},{4,6},{5,7},{6,4},{7,5},{8,10},{9,11},{10,... | collective-permute-start | bytes 147464 | tf_op jit(solution)/shard_map/ppermute | solution.py:522
  5.9 5.0 %copy-start = (f32[4096,128]{1,0:T(8,128)S(1)}, f32[4096,128]{1,0:T(8,128)}, u32[]{:S(2)}) copy-start(f32[4096,128]{1,0:T(8,128)} %refs_0_.1) | copy-start | bytes 6291460
  12.1 15.6 %collective-permute-start.6 = (f32[1280,128]{1,0:T(8,128)S(1)}, f32[1280,128]{1,0:T(8,128)S(1)}, u32[]{:S(2)}, u32[]{:S(2)}) collective-permute-start(f32[1280,128]{1,0:T(8,128)S(1)} %get-tuple-element.25.refs_2_), channel_id=1, source_target_pairs={{0,4},{4,0},{8,12},{12,8},{16,20},{20,16},{24,28},{28,24},{32,36},... | collective-permute-start | bytes 1966088 | tf_op jit(solution)/shard_map/ppermute | solution.py:500
  12.7 19.0 %collective-permute-start.8 = (f32[1280,128]{1,0:T(8,128)S(1)}, f32[1280,128]{1,0:T(8,128)S(1)}, u32[]{:S(2)}, u32[]{:S(2)}) collective-permute-start(f32[1280,128]{1,0:T(8,128)S(1)} %get-tuple-element.29.refs_1_), channel_id=1, source_target_pairs={{0,0},{4,8},{8,4},{12,16},{16,12},{20,24},{24,20},{28,32},{32,28},... | collective-permute-start | bytes 1966088 | tf_op jit(solution)/shard_map/ppermute | solution.py:495
  17.4 19.5 %collective-permute-start.2 = (f32[832,128]{1,0:T(8,128)S(1)}, f32[832,128]{1,0:T(8,128)S(1)}, u32[]{:S(2)}, u32[]{:S(2)}) collective-permute-start(f32[832,128]{1,0:T(8,128)S(1)} %get-tuple-element.23.refs_2_), channel_id=1, source_target_pairs={{0,4},{4,0},{8,12},{12,8},{16,20},{20,16},{24,28},{28,24},{32,36},... | collective-permute-start | bytes 1277960 | tf_op jit(solution)/shard_map/ppermute | solution.py:500
  17.5 23.3 %collective-permute-start.4 = (f32[832,128]{1,0:T(8,128)S(1)}, f32[832,128]{1,0:T(8,128)S(1)}, u32[]{:S(2)}, u32[]{:S(2)}) collective-permute-start(f32[832,128]{1,0:T(8,128)S(1)} %get-tuple-element.24.refs_1_), channel_id=1, source_target_pairs={{0,0},{4,8},{8,4},{12,16},{16,12},{20,24},{24,20},{28,32},{32,28},... | collective-permute-start | bytes 1277960 | tf_op jit(solution)/shard_map/ppermute | solution.py:495
  27.7 30.3 %collective-permute-start.7 = (f32[1280,128]{1,0:T(8,128)S(1)}, f32[1280,128]{1,0:T(8,128)S(1)}, u32[]{:S(2)}, u32[]{:S(2)}) collective-permute-start(f32[1280,128]{1,0:T(8,128)S(1)} %collective-permute-done.6.refs_2_.refs_4_), channel_id=1, source_target_pairs={{4,8},{8,4},{12,16},{16,12},{20,24},{24,20},{28,32},{32,28},{36,40... | collective-permute-start | bytes 1966088 | tf_op jit(solution)/shard_map/ppermute | solution.py:495
  31.7 43.8 %collective-permute-start.11 = (f32[1280,128]{1,0:T(8,128)S(1)}, f32[1280,128]{1,0:T(8,128)S(1)}, u32[]{:S(2)}, u32[]{:S(2)}) collective-permute-start(f32[1280,128]{1,0:T(8,128)S(1)} %collective-permute-done.8.refs_0_), channel_id=1, source_target_pairs={{0,4},{4,0},{8,12},{12,8},{16,20},{20,16},{24,28},{28,24},{32,36},... | collective-permute-start | bytes 1966088 | tf_op jit(solution)/shard_map/ppermute | solution.py:500
  36.9 39.5 %collective-permute-start.3 = (f32[832,128]{1,0:T(8,128)S(1)}, f32[832,128]{1,0:T(8,128)S(1)}, u32[]{:S(2)}, u32[]{:S(2)}) collective-permute-start(f32[832,128]{1,0:T(8,128)S(1)} %collective-permute-done.2.refs_3_.refs_4_), channel_id=1, source_target_pairs={{4,8},{8,4},{12,16},{16,12},{20,24},{24,20},{28,32},{32,28},{36,40... | collective-permute-start | bytes 1277960 | tf_op jit(solution)/shard_map/ppermute | solution.py:495
  40.8 35.5 %collective-permute-start.5 = (f32[832,128]{1,0:T(8,128)S(1)}, f32[832,128]{1,0:T(8,128)S(1)}, u32[]{:S(2)}, u32[]{:S(2)}) collective-permute-start(f32[832,128]{1,0:T(8,128)S(1)} %collective-permute-done.4.refs_1_), channel_id=1, source_target_pairs={{0,4},{4,0},{8,12},{12,8},{16,20},{20,16},{24,28},{28,24},{32,36},... | collective-permute-start | bytes 1277960 | tf_op jit(solution)/shard_map/ppermute | solution.py:500
  42.0 3.6 %collective-permute-start.9 = (f32[96,128]{1,0:T(8,128)S(1)}, f32[96,128]{1,0:T(8,128)S(1)}, u32[]{:S(2)}, u32[]{:S(2)}) collective-permute-start(f32[96,128]{1,0:T(8,128)S(1)} %shard_map.63), channel_id=1, source_target_pairs={{0,1},{1,0},{2,3},{3,2},{4,5},{5,4},{6,7},{7,6},{8,9},{9,8},{10,11... | collective-permute-start | bytes 147464 | tf_op jit(solution)/shard_map/ppermute | solution.py:522
  45.6 3.2 %collective-permute-start.10 = (f32[96,128]{1,0:T(8,128)S(1)}, f32[96,128]{1,0:T(8,128)S(1)}, u32[]{:S(2)}, u32[]{:S(2)}) collective-permute-start(f32[96,128]{1,0:T(8,128)S(1)} %add.10.refs_0_), channel_id=1, source_target_pairs={{0,2},{1,3},{2,0},{3,1},{4,6},{5,7},{6,4},{7,5},{8,10},{9,11},{10,... | collective-permute-start | bytes 147464 | tf_op jit(solution)/shard_map/ppermute | solution.py:522
  51.3 25.7 %collective-permute-start.12 = (f32[96,128]{1,0:T(8,128)S(1)}, f32[96,128]{1,0:T(8,128)S(1)}, u32[]{:S(2)}, u32[]{:S(2)}) collective-permute-start(f32[96,128]{1,0:T(8,128)S(1)} %get-tuple-element.30), channel_id=1, source_target_pairs={{0,0},{4,8},{8,4},{12,16},{16,12},{20,24},{24,20},{28,32},{32,28},... | collective-permute-start | bytes 147464 | tf_op jit(solution)/shard_map/ppermute | solution.py:495
  58.0 19.0 %collective-permute-start.13 = (f32[96,128]{1,0:T(8,128)S(1)}, f32[96,128]{1,0:T(8,128)S(1)}, u32[]{:S(2)}, u32[]{:S(2)}) collective-permute-start(f32[96,128]{1,0:T(8,128)S(1)} %get-tuple-element.31), channel_id=1, source_target_pairs={{0,4},{4,0},{8,12},{12,8},{16,20},{20,16},{24,28},{28,24},{32,36},... | collective-permute-start | bytes 147464 | tf_op jit(solution)/shard_map/ppermute | solution.py:500
  77.6 2.3 %collective-permute-start.14 = (f32[232,128]{1,0:T(8,128)S(1)}, f32[232,128]{1,0:T(8,128)S(1)}, u32[]{:S(2)}, u32[]{:S(2)}) collective-permute-start(f32[232,128]{1,0:T(8,128)S(1)} %shard_map.67), channel_id=1, source_target_pairs={{0,1},{1,0},{2,3},{3,2},{4,5},{5,4},{6,7},{7,6},{8,9},{9,8},{10,11... | collective-permute-start | bytes 356360 | tf_op jit(solution)/shard_map/ppermute | solution.py:522
  79.9 6.5 %collective-permute-start.17 = (f32[232,128]{1,0:T(8,128)S(1)}, f32[232,128]{1,0:T(8,128)S(1)}, u32[]{:S(2)}, u32[]{:S(2)}) collective-permute-start(f32[232,128]{1,0:T(8,128)S(1)} %add.11), channel_id=1, source_target_pairs={{0,4},{1,6},{2,5},{3,7},{4,0},{5,2},{6,1},{7,3},{8,12},{9,14},{10,... | collective-permute-start | bytes 356360 | tf_op jit(solution)/shard_map/ppermute | solution.py:510
  83.2 7.0 %collective-permute-start.15 = (f32[224,128]{1,0:T(8,128)S(1)}, f32[224,128]{1,0:T(8,128)S(1)}, u32[]{:S(2)}, u32[]{:S(2)}) collective-permute-start(f32[224,128]{1,0:T(8,128)S(1)} %slice.4), channel_id=1, source_target_pairs={{0,0},{1,2},{2,1},{3,3},{4,8},{5,10},{6,9},{7,11},{8,4},{9,6},{10,... | collective-permute-start | bytes 344072 | tf_op jit(solution)/shard_map/ppermute | solution.py:510
  86.4 5.1 %collective-permute-start.18 = (f32[232,128]{1,0:T(8,128)S(1)}, f32[232,128]{1,0:T(8,128)S(1)}, u32[]{:S(2)}, u32[]{:S(2)}) collective-permute-start(f32[232,128]{1,0:T(8,128)S(1)} %collective-permute-done.17.refs_2_), channel_id=1, source_target_pairs={{0,1},{1,0},{2,3},{3,2},{4,5},{5,4},{6,7},{7,6},{8,9},{9,8},{10,11... | collective-permute-start | bytes 356360 | tf_op jit(solution)/shard_map/ppermute | solution.py:522
  90.2 1.3 %collective-permute-start.16 = (f32[224,128]{1,0:T(8,128)S(1)}, f32[224,128]{1,0:T(8,128)S(1)}, u32[]{:S(2)}, u32[]{:S(2)}) collective-permute-start(f32[224,128]{1,0:T(8,128)S(1)} %collective-permute-done.15.refs_0_), channel_id=1, source_target_pairs={{0,1},{1,0},{2,3},{3,2},{4,5},{5,4},{6,7},{7,6},{8,9},{9,8},{10,11... | collective-permute-start | bytes 344072 | tf_op jit(solution)/shard_map/ppermute | solution.py:522
